TPU v7x, 256 devices: a whole 4x4x8 slice. The times are simulated.
256 devices in a mesh: segment: 4 (over y), row: 64 (over x, z, core).
Axes of the slice: x: 4, y: 4, z: 8, core: 2. Of those that a mesh axis runs over, the one named last changes fastest.
Arguments:
- latents: bfloat16 [4, 128, 128, 256], P(None, 'row'), may hold values from -6 to 6
- noise: bfloat16 [4, 4, 128, 128, 256], P('segment', None, 'row'), may hold values from -6 to 6
- timesteps: int32 [4, 4, 2], replicated, may hold values from 1 to 1000
- text: bfloat16 [4, 77, 4096], P('segment', None, 'row'), may hold values from -48 to 48
- text_weight: bfloat16 [4096, 256], P('row'), may hold values from -0.09375 to 0.09375
- time_weight: bfloat16 [256, 256], replicated, may hold values from -0.375 to 0.375
- film_weight: bfloat16 [4, 256, 512], P('segment'), may hold values from -0.375 to 0.375
- conv_weight: bfloat16 [4, 3, 3, 256, 256], P('segment'), may hold values from -0.125 to 0.125
- norm_gain: float32 [4, 256], P('segment'), may hold values from 0.5 to 1.5
Outputs:
- denoised: bfloat16 [4, 128, 128, 256], P('segment', 'row')
All inputs are finite; a program needn't handle non-finite values.
Results may differ from a plain program's by a relative error of at most 0.012.
Values may be sent and summed in bfloat16 or wider, within the bound.
No kernel may reach another device: no remote copies, remote signals or barrier semaphores. Data moves between devices by JAX's collectives and lax.ppermute only.
A program may use at most 64 MiB of HBM per device.

v0:
```python
import jax
import jax.numpy as jnp
from jax import lax
from jax.sharding import PartitionSpec as P

STEPS = 2


def padded_2(shard, sides, width):
    for axis, dim in sides:
        count, length = (lax.axis_size(axis), shard.shape[dim])
        up = [(i, (i + 1) % count) for i in range(count - 1)]
        down = [(j, i) for i, j in up]
        last = lax.slice_in_dim(shard, length - width, length, axis=dim)
        first = lax.slice_in_dim(shard, 0, width, axis=dim)
        before = lax.ppermute(last, axis, up)
        after = lax.ppermute(first, axis, down)
        shard = jnp.concatenate([before, shard, after], axis=dim)
    return shard


def from_behind(value, axis, steps):
    count = lax.axis_size(axis)
    first, last = (max(0, -steps), min(count, count - steps))
    return lax.ppermute(value, axis, [(source, source + steps) for source in range(first, last)])


def sinusoid(times, channels):
    half = channels // 2
    freqs = jnp.exp(-jnp.log(10000.0) * jnp.arange(half, dtype=jnp.float32) / half)
    angles = times.astype(jnp.float32)[..., None] * freqs
    return jnp.concatenate([jnp.cos(angles), jnp.sin(angles)], axis=-1).astype(jnp.bfloat16)


def conditioning(pooled, times, time_weight, film_matrix):
    channels = time_weight.shape[0]
    embed = sinusoid(times, channels)
    flat = embed.reshape(-1, channels)
    time_part = jax.nn.silu(jnp.dot(flat, time_weight, preferred_element_type=jnp.float32))
    time_part = time_part.reshape(times.shape + (channels,))
    cond = (pooled[:, None, :] + time_part).astype(jnp.bfloat16)
    film = jnp.dot(cond.reshape(-1, channels), film_matrix, preferred_element_type=jnp.float32)
    return film.reshape(times.shape + (2 * channels,))


def normalize(x, gain):
    values = x.astype(jnp.float32)
    scale_inv = lax.rsqrt(jnp.mean(values * values, axis=-1, keepdims=True) + 1e-06)
    return (values * scale_inv * gain).astype(jnp.bfloat16)


def convolve(padded, kernel):
    full = jnp.pad(padded, ((0, 0), (1, 1), (0, 0)))
    rows = padded.shape[0] - 2
    width = padded.shape[1]
    channels = padded.shape[2]
    total = None
    for dy in range(3):
        for dx in range(3):
            piece = full[dy : dy + rows, dx : dx + width, :].reshape(-1, channels)
            term = jnp.dot(piece, kernel[dy, dx], preferred_element_type=jnp.float32)
            total = term if total is None else total + term
    return total.reshape(rows, width, channels)


def advance(x, padded, kernel, film, extra):
    channels = x.shape[-1]
    conv = convolve(padded, kernel)
    branch = jax.nn.silu(conv * (1.0 + film[:channels]) + film[channels:])
    return (x.astype(jnp.float32) + branch + extra).astype(jnp.bfloat16)


def run_section(x, film, noise_now, sigma, gain, kernel):
    for step in range(STEPS):
        normed = normalize(x, gain)
        padded = padded_2(normed, (("row", 0),), 1)
        extra = 0.0
        if step == STEPS - 1:
            extra = sigma * noise_now.astype(jnp.float32)
        x = advance(x, padded, kernel, film[step], extra)
    return x


def body(
    latents, noise, timesteps, text, text_weight, time_weight, film_weight, conv_weight, norm_gain
):
    segments = lax.axis_size("segment")
    segment = lax.axis_index("segment")
    count = latents.shape[0]
    text_mean = jnp.mean(text.astype(jnp.float32), axis=1).astype(jnp.bfloat16)
    partial_pool = jnp.dot(text_mean, text_weight, preferred_element_type=jnp.float32)
    summed = lax.psum(partial_pool, "row")
    pooled = lax.all_gather(summed, "segment", axis=0, tiled=True)
    my_times = lax.dynamic_index_in_dim(timesteps, segment, 1, keepdims=False)
    film_all = conditioning(pooled, my_times, time_weight, film_weight[0])
    sigma_all = my_times[:, STEPS - 1].astype(jnp.float32) / 1000.0
    gain = norm_gain[0]
    kernel = conv_weight[0]
    my_noise = noise[0]

    def tick(moment, carry):
        buffer, collected = carry
        micro = moment - segment
        picked = jnp.clip(micro, 0, count - 1)
        entering = lax.dynamic_index_in_dim(
            latents, jnp.clip(moment, 0, count - 1), 0, keepdims=False
        )
        current_x = jnp.where(segment == 0, entering, buffer)
        film = lax.dynamic_index_in_dim(film_all, picked, 0, keepdims=False)
        noise_now = lax.dynamic_index_in_dim(my_noise, picked, 0, keepdims=False)
        sigma = lax.dynamic_index_in_dim(sigma_all, picked, 0, keepdims=False)
        result = run_section(current_x, film, noise_now, sigma, gain, kernel)
        keeping = (micro >= 0) & (micro < count) & (segment == segments - 1)
        previous = lax.dynamic_index_in_dim(collected, picked, 0, keepdims=False)
        collected = lax.dynamic_update_index_in_dim(
            collected, jnp.where(keeping, result, previous), picked, 0
        )
        buffer = from_behind(result, "segment", 1)
        return (buffer, collected)

    start_buffer = jnp.zeros(latents.shape[1:], jnp.bfloat16)
    start_collected = jnp.zeros(latents.shape, jnp.bfloat16)
    final_buffer, collected = lax.fori_loop(
        0, count + segments - 1, tick, (start_buffer, start_collected)
    )
    finished = lax.psum_scatter(collected, "segment", scatter_dimension=0, tiled=True).astype(
        jnp.float32
    )
    return finished.astype(jnp.bfloat16)


def solution(mesh):
    in_specs = (
        P(None, "row", None, None),
        P("segment", None, "row", None, None),
        P(),
        P("segment", None, "row"),
        P("row", None),
        P(),
        P("segment", None, None),
        P("segment", None, None, None, None),
        P("segment", None),
    )
    out_specs = P("segment", "row", None, None)
    return jax.shard_map(body, mesh=mesh, in_specs=in_specs, out_specs=out_specs, check_vma=False)
```

profile of v0, /device:TPU:1, one launch (start us, length us, event | category | flops | bytes accessed | tf_op | source)
XLA Modules:
  0.0 390.3 jit_solution(8271290338843873010)
XLA Ops:
  9.3 128.0 %psum.7 = f32[1,256]{1,0:T(1,128)S(1)} all-reduce(f32[1,256]{1,0:T(1,128)S(1)} %fusion.65), channel_id=1, replica_groups=mesh['segment'=4,'row'=64] {'row'}, use_global_device_ids=true, to_apply=%region_1.0 | all-reduce | flops 256 | bytes 2048 | tf_op jit(solution)/shard_map/psum | solution.py:92
  137.3 7.9 %all-gather = f32[4,1,256]{2,1,0:T(1,128)S(1)} all-gather(f32[1,1,256]{2,1,0:T(1,128)S(1)} %bitcast.278), channel_id=1, replica_groups=mesh['segment'=4,'row'=64] {'segment'}, dimensions={0}, use_global_device_ids=true | all-gather | bytes 5120 | tf_op jit(solution)/shard_map/all_gather | solution.py:93
  146.8 203.7 %while.17 = (s32[]{:T(128)}, bf16[2,128,256]{2,1,0:T(8,128)(2,1)S(1)}, bf16[4,2,128,256]{3,2,1,0:T(8,128)(2,1)S(1)}, pred[]{:T(512)}, bf16[4,2,128,256]{3,2,1,0:...) while((s32[]{:T(128)}, ...), condition=%wide.region_5.6_spmd, body=%wide.region_2.5_spmd.sunk | while | flops 610911232 | bytes 23624192 | solution.py:123
  148.0 8.9 %collective-permute-start = (bf16[1,128,256]{2,1,0:T(8,128)(2,1)S(1)}, bf16[1,128,256]{2,1,0:T(8,128)(2,1)S(1)}, u32[]{:S(2)}, u32[]{:S(2)}) collective-permute-start(bf16[1,128,256]{2,1,0:T(8,128)(2,1)S(1)} %get-tuple-element.460), channel_id=1, source_target_pairs={{1,0},{2,1},{3,2},{4,3},{5,4},{6,5},{7,6},{8,7},{9,8},{10,9},{11,1... | collective-permute-start | bytes 196616 | tf_op jit(solution)/shard_map/while/body/eval_jaxpr/ppermute | solution.py:17
  157.0 1.9 collective-permute-start.1
  162.5 2.0 collective-permute-start.2
  164.5 4.2 %collective-permute-start.3 = (bf16[1,128,256]{2,1,0:T(8,128)(2,1)S(1)}, bf16[1,128,256]{2,1,0:T(8,128)(2,1)S(1)}, u32[]{:S(2)}, u32[]{:S(2)}) collective-permute-start(bf16[1,128,256]{2,1,0:T(8,128)(2,1)S(1)} %get-tuple-element.474), channel_id=1, source_target_pairs={{0,1},{1,2},{2,3},{3,4},{4,5},{5,6},{6,7},{7,8},{8,9},{9,10},{10,1... | collective-permute-start | bytes 196616 | tf_op jit(solution)/shard_map/while/body/eval_jaxpr/ppermute | solution.py:16
  172.0 1.7 bitcast_dynamic-update-slice_fusion.2
  175.0 1.9 collective-permute-done.4
  178.1 1.9 collective-permute-start
  180.0 5.0 %collective-permute-start.1 = (bf16[1,128,256]{2,1,0:T(8,128)(2,1)S(1)}, bf16[1,128,256]{2,1,0:T(8,128)(2,1)S(1)}, u32[]{:S(2)}, u32[]{:S(2)}) collective-permute-start(bf16[1,128,256]{2,1,0:T(8,128)(2,1)S(1)} %get-tuple-element.461), channel_id=1, source_target_pairs={{0,1},{1,2},{2,3},{3,4},{4,5},{5,6},{6,7},{7,8},{8,9},{9,10},{10,1... | collective-permute-start | bytes 196616 | tf_op jit(solution)/shard_map/while/body/eval_jaxpr/ppermute | solution.py:16
  188.6 1.9 collective-permute-start.2
  190.5 4.3 %collective-permute-start.3 = (bf16[1,128,256]{2,1,0:T(8,128)(2,1)S(1)}, bf16[1,128,256]{2,1,0:T(8,128)(2,1)S(1)}, u32[]{:S(2)}, u32[]{:S(2)}) collective-permute-start(bf16[1,128,256]{2,1,0:T(8,128)(2,1)S(1)} %get-tuple-element.474), channel_id=1, source_target_pairs={{0,1},{1,2},{2,3},{3,4},{4,5},{5,6},{6,7},{7,8},{8,9},{9,10},{10,1... | collective-permute-start | bytes 196616 | tf_op jit(solution)/shard_map/while/body/eval_jaxpr/ppermute | solution.py:16
  198.0 1.7 bitcast_dynamic-update-slice_fusion.2
  199.7 4.1 %collective-permute-start.4 = (bf16[2,128,256]{2,1,0:T(8,128)(2,1)S(1)}, bf16[2,128,256]{2,1,0:T(8,128)(2,1)S(1)}, u32[]{:S(2)}, u32[]{:S(2)}) collective-permute-start(bf16[2,128,256]{2,1,0:T(8,128)(2,1)S(1)} %get-tuple-element.484), channel_id=1, source_target_pairs={{0,64},{64,128},{128,192},{1,65},{65,129},{129,193},{2,66},{66,130... | collective-permute-start | bytes 393224 | tf_op jit(solution)/shard_map/while/body/eval_jaxpr/ppermute | solution.py:25
  203.8 1.9 collective-permute-done.4
  206.9 1.9 collective-permute-start
  208.8 5.1 %collective-permute-start.1 = (bf16[1,128,256]{2,1,0:T(8,128)(2,1)S(1)}, bf16[1,128,256]{2,1,0:T(8,128)(2,1)S(1)}, u32[]{:S(2)}, u32[]{:S(2)}) collective-permute-start(bf16[1,128,256]{2,1,0:T(8,128)(2,1)S(1)} %get-tuple-element.461), channel_id=1, source_target_pairs={{0,1},{1,2},{2,3},{3,4},{4,5},{5,6},{6,7},{7,8},{8,9},{9,10},{10,1... | collective-permute-start | bytes 196616 | tf_op jit(solution)/shard_map/while/body/eval_jaxpr/ppermute | solution.py:16
  217.5 1.9 collective-permute-start.2
  219.5 4.3 %collective-permute-start.3 = (bf16[1,128,256]{2,1,0:T(8,128)(2,1)S(1)}, bf16[1,128,256]{2,1,0:T(8,128)(2,1)S(1)}, u32[]{:S(2)}, u32[]{:S(2)}) collective-permute-start(bf16[1,128,256]{2,1,0:T(8,128)(2,1)S(1)} %get-tuple-element.474), channel_id=1, source_target_pairs={{0,1},{1,2},{2,3},{3,4},{4,5},{5,6},{6,7},{7,8},{8,9},{9,10},{10,1... | collective-permute-start | bytes 196616 | tf_op jit(solution)/shard_map/while/body/eval_jaxpr/ppermute | solution.py:16
  227.0 1.7 bitcast_dynamic-update-slice_fusion.2
  228.7 4.1 %collective-permute-start.4 = (bf16[2,128,256]{2,1,0:T(8,128)(2,1)S(1)}, bf16[2,128,256]{2,1,0:T(8,128)(2,1)S(1)}, u32[]{:S(2)}, u32[]{:S(2)}) collective-permute-start(bf16[2,128,256]{2,1,0:T(8,128)(2,1)S(1)} %get-tuple-element.484), channel_id=1, source_target_pairs={{0,64},{64,128},{128,192},{1,65},{65,129},{129,193},{2,66},{66,130... | collective-permute-start | bytes 393224 | tf_op jit(solution)/shard_map/while/body/eval_jaxpr/ppermute | solution.py:25
  232.8 1.9 collective-permute-done.4
  235.8 1.9 collective-permute-start
  237.8 5.1 %collective-permute-start.1 = (bf16[1,128,256]{2,1,0:T(8,128)(2,1)S(1)}, bf16[1,128,256]{2,1,0:T(8,128)(2,1)S(1)}, u32[]{:S(2)}, u32[]{:S(2)}) collective-permute-start(bf16[1,128,256]{2,1,0:T(8,128)(2,1)S(1)} %get-tuple-element.461), channel_id=1, source_target_pairs={{0,1},{1,2},{2,3},{3,4},{4,5},{5,6},{6,7},{7,8},{8,9},{9,10},{10,1... | collective-permute-start | bytes 196616 | tf_op jit(solution)/shard_map/while/body/eval_jaxpr/ppermute | solution.py:16
  246.5 1.9 collective-permute-start.2
  248.4 4.3 %collective-permute-start.3 = (bf16[1,128,256]{2,1,0:T(8,128)(2,1)S(1)}, bf16[1,128,256]{2,1,0:T(8,128)(2,1)S(1)}, u32[]{:S(2)}, u32[]{:S(2)}) collective-permute-start(bf16[1,128,256]{2,1,0:T(8,128)(2,1)S(1)} %get-tuple-element.474), channel_id=1, source_target_pairs={{0,1},{1,2},{2,3},{3,4},{4,5},{5,6},{6,7},{7,8},{8,9},{9,10},{10,1... | collective-permute-start | bytes 196616 | tf_op jit(solution)/shard_map/while/body/eval_jaxpr/ppermute | solution.py:16
  257.6 4.1 %collective-permute-start.4 = (bf16[2,128,256]{2,1,0:T(8,128)(2,1)S(1)}, bf16[2,128,256]{2,1,0:T(8,128)(2,1)S(1)}, u32[]{:S(2)}, u32[]{:S(2)}) collective-permute-start(bf16[2,128,256]{2,1,0:T(8,128)(2,1)S(1)} %get-tuple-element.484), channel_id=1, source_target_pairs={{0,64},{64,128},{128,192},{1,65},{65,129},{129,193},{2,66},{66,130... | collective-permute-start | bytes 393224 | tf_op jit(solution)/shard_map/while/body/eval_jaxpr/ppermute | solution.py:25
  261.7 1.9 collective-permute-done.4
  264.8 1.9 collective-permute-start
  266.7 5.1 %collective-permute-start.1 = (bf16[1,128,256]{2,1,0:T(8,128)(2,1)S(1)}, bf16[1,128,256]{2,1,0:T(8,128)(2,1)S(1)}, u32[]{:S(2)}, u32[]{:S(2)}) collective-permute-start(bf16[1,128,256]{2,1,0:T(8,128)(2,1)S(1)} %get-tuple-element.461), channel_id=1, source_target_pairs={{0,1},{1,2},{2,3},{3,4},{4,5},{5,6},{6,7},{7,8},{8,9},{9,10},{10,1... | collective-permute-start | bytes 196616 | tf_op jit(solution)/shard_map/while/body/eval_jaxpr/ppermute | solution.py:16
  275.5 1.9 collective-permute-start.2
  277.4 4.3 %collective-permute-start.3 = (bf16[1,128,256]{2,1,0:T(8,128)(2,1)S(1)}, bf16[1,128,256]{2,1,0:T(8,128)(2,1)S(1)}, u32[]{:S(2)}, u32[]{:S(2)}) collective-permute-start(bf16[1,128,256]{2,1,0:T(8,128)(2,1)S(1)} %get-tuple-element.474), channel_id=1, source_target_pairs={{0,1},{1,2},{2,3},{3,4},{4,5},{5,6},{6,7},{7,8},{8,9},{9,10},{10,1... | collective-permute-start | bytes 196616 | tf_op jit(solution)/shard_map/while/body/eval_jaxpr/ppermute | solution.py:16
  286.6 4.1 %collective-permute-start.4 = (bf16[2,128,256]{2,1,0:T(8,128)(2,1)S(1)}, bf16[2,128,256]{2,1,0:T(8,128)(2,1)S(1)}, u32[]{:S(2)}, u32[]{:S(2)}) collective-permute-start(bf16[2,128,256]{2,1,0:T(8,128)(2,1)S(1)} %get-tuple-element.484), channel_id=1, source_target_pairs={{0,64},{64,128},{128,192},{1,65},{65,129},{129,193},{2,66},{66,130... | collective-permute-start | bytes 393224 | tf_op jit(solution)/shard_map/while/body/eval_jaxpr/ppermute | solution.py:25
  290.7 1.9 collective-permute-done.4
  293.8 1.9 collective-permute-start
  295.7 5.1 %collective-permute-start.1 = (bf16[1,128,256]{2,1,0:T(8,128)(2,1)S(1)}, bf16[1,128,256]{2,1,0:T(8,128)(2,1)S(1)}, u32[]{:S(2)}, u32[]{:S(2)}) collective-permute-start(bf16[1,128,256]{2,1,0:T(8,128)(2,1)S(1)} %get-tuple-element.461), channel_id=1, source_target_pairs={{0,1},{1,2},{2,3},{3,4},{4,5},{5,6},{6,7},{7,8},{8,9},{9,10},{10,1... | collective-permute-start | bytes 196616 | tf_op jit(solution)/shard_map/while/body/eval_jaxpr/ppermute | solution.py:16
  304.4 1.9 collective-permute-start.2
  306.4 4.3 %collective-permute-start.3 = (bf16[1,128,256]{2,1,0:T(8,128)(2,1)S(1)}, bf16[1,128,256]{2,1,0:T(8,128)(2,1)S(1)}, u32[]{:S(2)}, u32[]{:S(2)}) collective-permute-start(bf16[1,128,256]{2,1,0:T(8,128)(2,1)S(1)} %get-tuple-element.474), channel_id=1, source_target_pairs={{0,1},{1,2},{2,3},{3,4},{4,5},{5,6},{6,7},{7,8},{8,9},{9,10},{10,1... | collective-permute-start | bytes 196616 | tf_op jit(solution)/shard_map/while/body/eval_jaxpr/ppermute | solution.py:16
  315.6 4.1 %collective-permute-start.4 = (bf16[2,128,256]{2,1,0:T(8,128)(2,1)S(1)}, bf16[2,128,256]{2,1,0:T(8,128)(2,1)S(1)}, u32[]{:S(2)}, u32[]{:S(2)}) collective-permute-start(bf16[2,128,256]{2,1,0:T(8,128)(2,1)S(1)} %get-tuple-element.484), channel_id=1, source_target_pairs={{0,64},{64,128},{128,192},{1,65},{65,129},{129,193},{2,66},{66,130... | collective-permute-start | bytes 393224 | tf_op jit(solution)/shard_map/while/body/eval_jaxpr/ppermute | solution.py:25
  319.7 1.9 collective-permute-done.4
  322.8 1.9 collective-permute-start
  324.7 5.1 %collective-permute-start.1 = (bf16[1,128,256]{2,1,0:T(8,128)(2,1)S(1)}, bf16[1,128,256]{2,1,0:T(8,128)(2,1)S(1)}, u32[]{:S(2)}, u32[]{:S(2)}) collective-permute-start(bf16[1,128,256]{2,1,0:T(8,128)(2,1)S(1)} %get-tuple-element.461), channel_id=1, source_target_pairs={{0,1},{1,2},{2,3},{3,4},{4,5},{5,6},{6,7},{7,8},{8,9},{9,10},{10,1... | collective-permute-start | bytes 196616 | tf_op jit(solution)/shard_map/while/body/eval_jaxpr/ppermute | solution.py:16
  333.4 1.9 collective-permute-start.2
  335.3 4.3 %collective-permute-start.3 = (bf16[1,128,256]{2,1,0:T(8,128)(2,1)S(1)}, bf16[1,128,256]{2,1,0:T(8,128)(2,1)S(1)}, u32[]{:S(2)}, u32[]{:S(2)}) collective-permute-start(bf16[1,128,256]{2,1,0:T(8,128)(2,1)S(1)} %get-tuple-element.474), channel_id=1, source_target_pairs={{0,1},{1,2},{2,3},{3,4},{4,5},{5,6},{6,7},{7,8},{8,9},{9,10},{10,1... | collective-permute-start | bytes 196616 | tf_op jit(solution)/shard_map/while/body/eval_jaxpr/ppermute | solution.py:16
  344.5 4.1 %collective-permute-start.4 = (bf16[2,128,256]{2,1,0:T(8,128)(2,1)S(1)}, bf16[2,128,256]{2,1,0:T(8,128)(2,1)S(1)}, u32[]{:S(2)}, u32[]{:S(2)}) collective-permute-start(bf16[2,128,256]{2,1,0:T(8,128)(2,1)S(1)} %get-tuple-element.484), channel_id=1, source_target_pairs={{0,64},{64,128},{128,192},{1,65},{65,129},{129,193},{2,66},{66,130... | collective-permute-start | bytes 393224 | tf_op jit(solution)/shard_map/while/body/eval_jaxpr/ppermute | solution.py:25
  348.6 1.9 collective-permute-done.4
  351.4 32.1 %reduce-scatter.2.cloned.1.call-done = bf16[1,2,128,256]{3,2,1,0:T(8,128)(2,1)} async-done(((bf16[4,2,128,256]{3,2,1,0:T(8,128)(2,1)}), bf16[1,2,128,256]{3,2,1,0:T(8,128)(2,1)}) %reduce-scatter.2.cloned.1.call-update) | async-done | bytes 131088 | tf_op jit(solution)/shard_map/reduce_scatter | solution.py:126
  (304 shorter events, 67.5 us)
Async XLA Ops:
  6.5 140.1 %copy-start = (bf16[1,256,512]{2,1,0:T(8,128)(2,1)S(1)}, bf16[1,256,512]{2,1,0:T(8,128)(2,1)}, u32[]{:S(2)}) copy-start(bf16[1,256,512]{2,1,0:T(8,128)(2,1)} %param.17) | copy-start | bytes 786436
  6.5 140.3 %copy-start.1 = (bf16[1,3,3,256,256]{4,3,2,1,0:T(8,128)(2,1)S(1)}, bf16[1,3,3,256,256]{4,3,2,1,0:T(8,128)(2,1)}, u32[]{:S(2)}) copy-start(bf16[1,3,3,256,256]{4,3,2,1,0:T(8,128)(2,1)} %param.18) | copy-start | bytes 3538948
  6.5 140.3 %copy-start.3 = (f32[1,256]{1,0:T(1,128)S(1)}, f32[1,256]{1,0:T(1,128)}, u32[]{:S(2)}) copy-start(f32[1,256]{1,0:T(1,128)} %param.19) | copy-start | bytes 3076
  6.5 376.9 %reduce-scatter.2.cloned.1.call-start = ((), (), s32[]{:S(2)}) async-start(), calls=%async_computation.1 | async-start | bytes 655360 | tf_op jit(solution)/shard_map/reduce_scatter | solution.py:126
  148.0 11.6 %collective-permute-start = (bf16[1,128,256]{2,1,0:T(8,128)(2,1)S(1)}, bf16[1,128,256]{2,1,0:T(8,128)(2,1)S(1)}, u32[]{:S(2)}, u32[]{:S(2)}) collective-permute-start(bf16[1,128,256]{2,1,0:T(8,128)(2,1)S(1)} %get-tuple-element.460), channel_id=1, source_target_pairs={{1,0},{2,1},{3,2},{4,3},{5,4},{6,5},{7,6},{8,7},{9,8},{10,9},{11,1... | collective-permute-start | bytes 196616 | tf_op jit(solution)/shard_map/while/body/eval_jaxpr/ppermute | solution.py:17
  157.0 3.2 collective-permute-start.1
  162.5 6.2 %collective-permute-start.2 = (bf16[1,128,256]{2,1,0:T(8,128)(2,1)S(1)}, bf16[1,128,256]{2,1,0:T(8,128)(2,1)S(1)}, u32[]{:S(2)}, u32[]{:S(2)}) collective-permute-start(bf16[1,128,256]{2,1,0:T(8,128)(2,1)S(1)} %get-tuple-element.473), channel_id=1, source_target_pairs={{1,0},{2,1},{3,2},{4,3},{5,4},{6,5},{7,6},{8,7},{9,8},{10,9},{11,1... | collective-permute-start | bytes 196616 | tf_op jit(solution)/shard_map/while/body/eval_jaxpr/ppermute | solution.py:17
  164.5 5.5 %collective-permute-start.3 = (bf16[1,128,256]{2,1,0:T(8,128)(2,1)S(1)}, bf16[1,128,256]{2,1,0:T(8,128)(2,1)S(1)}, u32[]{:S(2)}, u32[]{:S(2)}) collective-permute-start(bf16[1,128,256]{2,1,0:T(8,128)(2,1)S(1)} %get-tuple-element.474), channel_id=1, source_target_pairs={{0,1},{1,2},{2,3},{3,4},{4,5},{5,6},{6,7},{7,8},{8,9},{9,10},{10,1... | collective-permute-start | bytes 196616 | tf_op jit(solution)/shard_map/while/body/eval_jaxpr/ppermute | solution.py:16
  173.7 3.2 collective-permute-start.4
  178.1 7.6 %collective-permute-start = (bf16[1,128,256]{2,1,0:T(8,128)(2,1)S(1)}, bf16[1,128,256]{2,1,0:T(8,128)(2,1)S(1)}, u32[]{:S(2)}, u32[]{:S(2)}) collective-permute-start(bf16[1,128,256]{2,1,0:T(8,128)(2,1)S(1)} %get-tuple-element.460), channel_id=1, source_target_pairs={{1,0},{2,1},{3,2},{4,3},{5,4},{6,5},{7,6},{8,7},{9,8},{10,9},{11,1... | collective-permute-start | bytes 196616 | tf_op jit(solution)/shard_map/while/body/eval_jaxpr/ppermute | solution.py:17
  180.0 6.3 %collective-permute-start.1 = (bf16[1,128,256]{2,1,0:T(8,128)(2,1)S(1)}, bf16[1,128,256]{2,1,0:T(8,128)(2,1)S(1)}, u32[]{:S(2)}, u32[]{:S(2)}) collective-permute-start(bf16[1,128,256]{2,1,0:T(8,128)(2,1)S(1)} %get-tuple-element.461), channel_id=1, source_target_pairs={{0,1},{1,2},{2,3},{3,4},{4,5},{5,6},{6,7},{7,8},{8,9},{9,10},{10,1... | collective-permute-start | bytes 196616 | tf_op jit(solution)/shard_map/while/body/eval_jaxpr/ppermute | solution.py:16
  188.6 6.2 %collective-permute-start.2 = (bf16[1,128,256]{2,1,0:T(8,128)(2,1)S(1)}, bf16[1,128,256]{2,1,0:T(8,128)(2,1)S(1)}, u32[]{:S(2)}, u32[]{:S(2)}) collective-permute-start(bf16[1,128,256]{2,1,0:T(8,128)(2,1)S(1)} %get-tuple-element.473), channel_id=1, source_target_pairs={{1,0},{2,1},{3,2},{4,3},{5,4},{6,5},{7,6},{8,7},{9,8},{10,9},{11,1... | collective-permute-start | bytes 196616 | tf_op jit(solution)/shard_map/while/body/eval_jaxpr/ppermute | solution.py:17
  190.5 5.6 %collective-permute-start.3 = (bf16[1,128,256]{2,1,0:T(8,128)(2,1)S(1)}, bf16[1,128,256]{2,1,0:T(8,128)(2,1)S(1)}, u32[]{:S(2)}, u32[]{:S(2)}) collective-permute-start(bf16[1,128,256]{2,1,0:T(8,128)(2,1)S(1)} %get-tuple-element.474), channel_id=1, source_target_pairs={{0,1},{1,2},{2,3},{3,4},{4,5},{5,6},{6,7},{7,8},{8,9},{9,10},{10,1... | collective-permute-start | bytes 196616 | tf_op jit(solution)/shard_map/while/body/eval_jaxpr/ppermute | solution.py:16
  199.7 6.0 %collective-permute-start.4 = (bf16[2,128,256]{2,1,0:T(8,128)(2,1)S(1)}, bf16[2,128,256]{2,1,0:T(8,128)(2,1)S(1)}, u32[]{:S(2)}, u32[]{:S(2)}) collective-permute-start(bf16[2,128,256]{2,1,0:T(8,128)(2,1)S(1)} %get-tuple-element.484), channel_id=1, source_target_pairs={{0,64},{64,128},{128,192},{1,65},{65,129},{129,193},{2,66},{66,130... | collective-permute-start | bytes 393224 | tf_op jit(solution)/shard_map/while/body/eval_jaxpr/ppermute | solution.py:25
  206.9 7.8 %collective-permute-start = (bf16[1,128,256]{2,1,0:T(8,128)(2,1)S(1)}, bf16[1,128,256]{2,1,0:T(8,128)(2,1)S(1)}, u32[]{:S(2)}, u32[]{:S(2)}) collective-permute-start(bf16[1,128,256]{2,1,0:T(8,128)(2,1)S(1)} %get-tuple-element.460), channel_id=1, source_target_pairs={{1,0},{2,1},{3,2},{4,3},{5,4},{6,5},{7,6},{8,7},{9,8},{10,9},{11,1... | collective-permute-start | bytes 196616 | tf_op jit(solution)/shard_map/while/body/eval_jaxpr/ppermute | solution.py:17
  208.8 6.4 %collective-permute-start.1 = (bf16[1,128,256]{2,1,0:T(8,128)(2,1)S(1)}, bf16[1,128,256]{2,1,0:T(8,128)(2,1)S(1)}, u32[]{:S(2)}, u32[]{:S(2)}) collective-permute-start(bf16[1,128,256]{2,1,0:T(8,128)(2,1)S(1)} %get-tuple-element.461), channel_id=1, source_target_pairs={{0,1},{1,2},{2,3},{3,4},{4,5},{5,6},{6,7},{7,8},{8,9},{9,10},{10,1... | collective-permute-start | bytes 196616 | tf_op jit(solution)/shard_map/while/body/eval_jaxpr/ppermute | solution.py:16
  217.5 6.2 %collective-permute-start.2 = (bf16[1,128,256]{2,1,0:T(8,128)(2,1)S(1)}, bf16[1,128,256]{2,1,0:T(8,128)(2,1)S(1)}, u32[]{:S(2)}, u32[]{:S(2)}) collective-permute-start(bf16[1,128,256]{2,1,0:T(8,128)(2,1)S(1)} %get-tuple-element.473), channel_id=1, source_target_pairs={{1,0},{2,1},{3,2},{4,3},{5,4},{6,5},{7,6},{8,7},{9,8},{10,9},{11,1... | collective-permute-start | bytes 196616 | tf_op jit(solution)/shard_map/while/body/eval_jaxpr/ppermute | solution.py:17
  219.5 5.6 %collective-permute-start.3 = (bf16[1,128,256]{2,1,0:T(8,128)(2,1)S(1)}, bf16[1,128,256]{2,1,0:T(8,128)(2,1)S(1)}, u32[]{:S(2)}, u32[]{:S(2)}) collective-permute-start(bf16[1,128,256]{2,1,0:T(8,128)(2,1)S(1)} %get-tuple-element.474), channel_id=1, source_target_pairs={{0,1},{1,2},{2,3},{3,4},{4,5},{5,6},{6,7},{7,8},{8,9},{9,10},{10,1... | collective-permute-start | bytes 196616 | tf_op jit(solution)/shard_map/while/body/eval_jaxpr/ppermute | solution.py:16
  228.7 6.0 %collective-permute-start.4 = (bf16[2,128,256]{2,1,0:T(8,128)(2,1)S(1)}, bf16[2,128,256]{2,1,0:T(8,128)(2,1)S(1)}, u32[]{:S(2)}, u32[]{:S(2)}) collective-permute-start(bf16[2,128,256]{2,1,0:T(8,128)(2,1)S(1)} %get-tuple-element.484), channel_id=1, source_target_pairs={{0,64},{64,128},{128,192},{1,65},{65,129},{129,193},{2,66},{66,130... | collective-permute-start | bytes 393224 | tf_op jit(solution)/shard_map/while/body/eval_jaxpr/ppermute | solution.py:25
  235.8 7.8 %collective-permute-start = (bf16[1,128,256]{2,1,0:T(8,128)(2,1)S(1)}, bf16[1,128,256]{2,1,0:T(8,128)(2,1)S(1)}, u32[]{:S(2)}, u32[]{:S(2)}) collective-permute-start(bf16[1,128,256]{2,1,0:T(8,128)(2,1)S(1)} %get-tuple-element.460), channel_id=1, source_target_pairs={{1,0},{2,1},{3,2},{4,3},{5,4},{6,5},{7,6},{8,7},{9,8},{10,9},{11,1... | collective-permute-start | bytes 196616 | tf_op jit(solution)/shard_map/while/body/eval_jaxpr/ppermute | solution.py:17
  237.8 6.4 %collective-permute-start.1 = (bf16[1,128,256]{2,1,0:T(8,128)(2,1)S(1)}, bf16[1,128,256]{2,1,0:T(8,128)(2,1)S(1)}, u32[]{:S(2)}, u32[]{:S(2)}) collective-permute-start(bf16[1,128,256]{2,1,0:T(8,128)(2,1)S(1)} %get-tuple-element.461), channel_id=1, source_target_pairs={{0,1},{1,2},{2,3},{3,4},{4,5},{5,6},{6,7},{7,8},{8,9},{9,10},{10,1... | collective-permute-start | bytes 196616 | tf_op jit(solution)/shard_map/while/body/eval_jaxpr/ppermute | solution.py:16
  246.5 6.2 %collective-permute-start.2 = (bf16[1,128,256]{2,1,0:T(8,128)(2,1)S(1)}, bf16[1,128,256]{2,1,0:T(8,128)(2,1)S(1)}, u32[]{:S(2)}, u32[]{:S(2)}) collective-permute-start(bf16[1,128,256]{2,1,0:T(8,128)(2,1)S(1)} %get-tuple-element.473), channel_id=1, source_target_pairs={{1,0},{2,1},{3,2},{4,3},{5,4},{6,5},{7,6},{8,7},{9,8},{10,9},{11,1... | collective-permute-start | bytes 196616 | tf_op jit(solution)/shard_map/while/body/eval_jaxpr/ppermute | solution.py:17
  248.4 5.6 %collective-permute-start.3 = (bf16[1,128,256]{2,1,0:T(8,128)(2,1)S(1)}, bf16[1,128,256]{2,1,0:T(8,128)(2,1)S(1)}, u32[]{:S(2)}, u32[]{:S(2)}) collective-permute-start(bf16[1,128,256]{2,1,0:T(8,128)(2,1)S(1)} %get-tuple-element.474), channel_id=1, source_target_pairs={{0,1},{1,2},{2,3},{3,4},{4,5},{5,6},{6,7},{7,8},{8,9},{9,10},{10,1... | collective-permute-start | bytes 196616 | tf_op jit(solution)/shard_map/while/body/eval_jaxpr/ppermute | solution.py:16
  257.6 6.0 %collective-permute-start.4 = (bf16[2,128,256]{2,1,0:T(8,128)(2,1)S(1)}, bf16[2,128,256]{2,1,0:T(8,128)(2,1)S(1)}, u32[]{:S(2)}, u32[]{:S(2)}) collective-permute-start(bf16[2,128,256]{2,1,0:T(8,128)(2,1)S(1)} %get-tuple-element.484), channel_id=1, source_target_pairs={{0,64},{64,128},{128,192},{1,65},{65,129},{129,193},{2,66},{66,130... | collective-permute-start | bytes 393224 | tf_op jit(solution)/shard_map/while/body/eval_jaxpr/ppermute | solution.py:25
  264.8 7.8 %collective-permute-start = (bf16[1,128,256]{2,1,0:T(8,128)(2,1)S(1)}, bf16[1,128,256]{2,1,0:T(8,128)(2,1)S(1)}, u32[]{:S(2)}, u32[]{:S(2)}) collective-permute-start(bf16[1,128,256]{2,1,0:T(8,128)(2,1)S(1)} %get-tuple-element.460), channel_id=1, source_target_pairs={{1,0},{2,1},{3,2},{4,3},{5,4},{6,5},{7,6},{8,7},{9,8},{10,9},{11,1... | collective-permute-start | bytes 196616 | tf_op jit(solution)/shard_map/while/body/eval_jaxpr/ppermute | solution.py:17
  266.7 6.4 %collective-permute-start.1 = (bf16[1,128,256]{2,1,0:T(8,128)(2,1)S(1)}, bf16[1,128,256]{2,1,0:T(8,128)(2,1)S(1)}, u32[]{:S(2)}, u32[]{:S(2)}) collective-permute-start(bf16[1,128,256]{2,1,0:T(8,128)(2,1)S(1)} %get-tuple-element.461), channel_id=1, source_target_pairs={{0,1},{1,2},{2,3},{3,4},{4,5},{5,6},{6,7},{7,8},{8,9},{9,10},{10,1... | collective-permute-start | bytes 196616 | tf_op jit(solution)/shard_map/while/body/eval_jaxpr/ppermute | solution.py:16
  275.5 6.2 %collective-permute-start.2 = (bf16[1,128,256]{2,1,0:T(8,128)(2,1)S(1)}, bf16[1,128,256]{2,1,0:T(8,128)(2,1)S(1)}, u32[]{:S(2)}, u32[]{:S(2)}) collective-permute-start(bf16[1,128,256]{2,1,0:T(8,128)(2,1)S(1)} %get-tuple-element.473), channel_id=1, source_target_pairs={{1,0},{2,1},{3,2},{4,3},{5,4},{6,5},{7,6},{8,7},{9,8},{10,9},{11,1... | collective-permute-start | bytes 196616 | tf_op jit(solution)/shard_map/while/body/eval_jaxpr/ppermute | solution.py:17
  277.4 5.6 %collective-permute-start.3 = (bf16[1,128,256]{2,1,0:T(8,128)(2,1)S(1)}, bf16[1,128,256]{2,1,0:T(8,128)(2,1)S(1)}, u32[]{:S(2)}, u32[]{:S(2)}) collective-permute-start(bf16[1,128,256]{2,1,0:T(8,128)(2,1)S(1)} %get-tuple-element.474), channel_id=1, source_target_pairs={{0,1},{1,2},{2,3},{3,4},{4,5},{5,6},{6,7},{7,8},{8,9},{9,10},{10,1... | collective-permute-start | bytes 196616 | tf_op jit(solution)/shard_map/while/body/eval_jaxpr/ppermute | solution.py:16
  286.6 6.0 %collective-permute-start.4 = (bf16[2,128,256]{2,1,0:T(8,128)(2,1)S(1)}, bf16[2,128,256]{2,1,0:T(8,128)(2,1)S(1)}, u32[]{:S(2)}, u32[]{:S(2)}) collective-permute-start(bf16[2,128,256]{2,1,0:T(8,128)(2,1)S(1)} %get-tuple-element.484), channel_id=1, source_target_pairs={{0,64},{64,128},{128,192},{1,65},{65,129},{129,193},{2,66},{66,130... | collective-permute-start | bytes 393224 | tf_op jit(solution)/shard_map/while/body/eval_jaxpr/ppermute | solution.py:25
  293.8 7.8 %collective-permute-start = (bf16[1,128,256]{2,1,0:T(8,128)(2,1)S(1)}, bf16[1,128,256]{2,1,0:T(8,128)(2,1)S(1)}, u32[]{:S(2)}, u32[]{:S(2)}) collective-permute-start(bf16[1,128,256]{2,1,0:T(8,128)(2,1)S(1)} %get-tuple-element.460), channel_id=1, source_target_pairs={{1,0},{2,1},{3,2},{4,3},{5,4},{6,5},{7,6},{8,7},{9,8},{10,9},{11,1... | collective-permute-start | bytes 196616 | tf_op jit(solution)/shard_map/while/body/eval_jaxpr/ppermute | solution.py:17
  295.7 6.4 %collective-permute-start.1 = (bf16[1,128,256]{2,1,0:T(8,128)(2,1)S(1)}, bf16[1,128,256]{2,1,0:T(8,128)(2,1)S(1)}, u32[]{:S(2)}, u32[]{:S(2)}) collective-permute-start(bf16[1,128,256]{2,1,0:T(8,128)(2,1)S(1)} %get-tuple-element.461), channel_id=1, source_target_pairs={{0,1},{1,2},{2,3},{3,4},{4,5},{5,6},{6,7},{7,8},{8,9},{9,10},{10,1... | collective-permute-start | bytes 196616 | tf_op jit(solution)/shard_map/while/body/eval_jaxpr/ppermute | solution.py:16
  304.4 6.2 %collective-permute-start.2 = (bf16[1,128,256]{2,1,0:T(8,128)(2,1)S(1)}, bf16[1,128,256]{2,1,0:T(8,128)(2,1)S(1)}, u32[]{:S(2)}, u32[]{:S(2)}) collective-permute-start(bf16[1,128,256]{2,1,0:T(8,128)(2,1)S(1)} %get-tuple-element.473), channel_id=1, source_target_pairs={{1,0},{2,1},{3,2},{4,3},{5,4},{6,5},{7,6},{8,7},{9,8},{10,9},{11,1... | collective-permute-start | bytes 196616 | tf_op jit(solution)/shard_map/while/body/eval_jaxpr/ppermute | solution.py:17
  306.4 5.6 %collective-permute-start.3 = (bf16[1,128,256]{2,1,0:T(8,128)(2,1)S(1)}, bf16[1,128,256]{2,1,0:T(8,128)(2,1)S(1)}, u32[]{:S(2)}, u32[]{:S(2)}) collective-permute-start(bf16[1,128,256]{2,1,0:T(8,128)(2,1)S(1)} %get-tuple-element.474), channel_id=1, source_target_pairs={{0,1},{1,2},{2,3},{3,4},{4,5},{5,6},{6,7},{7,8},{8,9},{9,10},{10,1... | collective-permute-start | bytes 196616 | tf_op jit(solution)/shard_map/while/body/eval_jaxpr/ppermute | solution.py:16
  315.6 6.0 %collective-permute-start.4 = (bf16[2,128,256]{2,1,0:T(8,128)(2,1)S(1)}, bf16[2,128,256]{2,1,0:T(8,128)(2,1)S(1)}, u32[]{:S(2)}, u32[]{:S(2)}) collective-permute-start(bf16[2,128,256]{2,1,0:T(8,128)(2,1)S(1)} %get-tuple-element.484), channel_id=1, source_target_pairs={{0,64},{64,128},{128,192},{1,65},{65,129},{129,193},{2,66},{66,130... | collective-permute-start | bytes 393224 | tf_op jit(solution)/shard_map/while/body/eval_jaxpr/ppermute | solution.py:25
  322.8 7.8 %collective-permute-start = (bf16[1,128,256]{2,1,0:T(8,128)(2,1)S(1)}, bf16[1,128,256]{2,1,0:T(8,128)(2,1)S(1)}, u32[]{:S(2)}, u32[]{:S(2)}) collective-permute-start(bf16[1,128,256]{2,1,0:T(8,128)(2,1)S(1)} %get-tuple-element.460), channel_id=1, source_target_pairs={{1,0},{2,1},{3,2},{4,3},{5,4},{6,5},{7,6},{8,7},{9,8},{10,9},{11,1... | collective-permute-start | bytes 196616 | tf_op jit(solution)/shard_map/while/body/eval_jaxpr/ppermute | solution.py:17
  324.7 6.4 %collective-permute-start.1 = (bf16[1,128,256]{2,1,0:T(8,128)(2,1)S(1)}, bf16[1,128,256]{2,1,0:T(8,128)(2,1)S(1)}, u32[]{:S(2)}, u32[]{:S(2)}) collective-permute-start(bf16[1,128,256]{2,1,0:T(8,128)(2,1)S(1)} %get-tuple-element.461), channel_id=1, source_target_pairs={{0,1},{1,2},{2,3},{3,4},{4,5},{5,6},{6,7},{7,8},{8,9},{9,10},{10,1... | collective-permute-start | bytes 196616 | tf_op jit(solution)/shard_map/while/body/eval_jaxpr/ppermute | solution.py:16
  333.4 6.2 %collective-permute-start.2 = (bf16[1,128,256]{2,1,0:T(8,128)(2,1)S(1)}, bf16[1,128,256]{2,1,0:T(8,128)(2,1)S(1)}, u32[]{:S(2)}, u32[]{:S(2)}) collective-permute-start(bf16[1,128,256]{2,1,0:T(8,128)(2,1)S(1)} %get-tuple-element.473), channel_id=1, source_target_pairs={{1,0},{2,1},{3,2},{4,3},{5,4},{6,5},{7,6},{8,7},{9,8},{10,9},{11,1... | collective-permute-start | bytes 196616 | tf_op jit(solution)/shard_map/while/body/eval_jaxpr/ppermute | solution.py:17
  335.3 5.6 %collective-permute-start.3 = (bf16[1,128,256]{2,1,0:T(8,128)(2,1)S(1)}, bf16[1,128,256]{2,1,0:T(8,128)(2,1)S(1)}, u32[]{:S(2)}, u32[]{:S(2)}) collective-permute-start(bf16[1,128,256]{2,1,0:T(8,128)(2,1)S(1)} %get-tuple-element.474), channel_id=1, source_target_pairs={{0,1},{1,2},{2,3},{3,4},{4,5},{5,6},{6,7},{7,8},{8,9},{9,10},{10,1... | collective-permute-start | bytes 196616 | tf_op jit(solution)/shard_map/while/body/eval_jaxpr/ppermute | solution.py:16
  344.5 6.0 %collective-permute-start.4 = (bf16[2,128,256]{2,1,0:T(8,128)(2,1)S(1)}, bf16[2,128,256]{2,1,0:T(8,128)(2,1)S(1)}, u32[]{:S(2)}, u32[]{:S(2)}) collective-permute-start(bf16[2,128,256]{2,1,0:T(8,128)(2,1)S(1)} %get-tuple-element.484), channel_id=1, source_target_pairs={{0,64},{64,128},{128,192},{1,65},{65,129},{129,193},{2,66},{66,130... | collective-permute-start | bytes 393224 | tf_op jit(solution)/shard_map/while/body/eval_jaxpr/ppermute | solution.py:25
  350.5 0.8 copy-start.2
Sparse Core Ops, SparseCore 0:
  351.5 31.9 reduce-scatter.1
where the time goes:
time: 393 us; the launch traced here: 390 us
  blocking collectives  136 us (35%)
  starting transfers between devices  122 us (31%)
  waiting for transfers between devices  58.7 us (15%)
  other arithmetic  25.8 us (7%)
  matrix products  25.5 us (6%)
  between operations  13.5 us (3%)
  local copies, waits for them, and re-layouts  6.84 us (2%)
    psum x1, blocking collectives, body(): summed = lax.psum(partial_pool, 'row')  128 us
    ppermute x14, starting transfers between devices, padded_2(): before = lax.ppermute(last, axis, up)  62.3 us
    ppermute x14, starting transfers between devices, padded_2(): after = lax.ppermute(first, axis, down)  34 us
    reduce_scatter x1, waiting for transfers between devices, body(): lax.psum_scatter(collected, 'segment', scatter_dimension=0, tiled=True)  32.1 us
    ppermute x7, starting transfers between devices, from_behind(): lax.ppermute(value, axis, [(source, source + steps) for source in range(f...  25.8 us
    dot_general x126, matrix products, convolve(): term = jnp.dot(piece, kernel[dy, dx], preferred_element_type=jnp.float32)  23.4 us
    ppermute x7, waiting for transfers between devices, from_behind(): lax.ppermute(value, axis, [(source, source + steps) for source in range(f...  13.4 us
    ppermute x14, waiting for transfers between devices, padded_2(): before = lax.ppermute(last, axis, up)  13.1 us
  transfers between devices with their start and end apart: 36, of which 22 were waited for; matrix products, arithmetic and copies ran while one was open for 1% of the time, Pallas kernels for 0%

commit v1 on v0

v1 whole, which is shorter than its diff:
```python
import functools

import jax
import jax.numpy as jnp
from jax import lax
from jax.experimental import pallas as pl
from jax.experimental.pallas import tpu as pltpu
from jax.sharding import PartitionSpec as P

STEPS = 2
GAIN_ROWS = 16


def sinusoid(times, channels):
    half = channels // 2
    freqs = jnp.exp(-jnp.log(10000.0) * jnp.arange(half, dtype=jnp.float32) / half)
    angles = times.astype(jnp.float32)[..., None] * freqs
    return jnp.concatenate([jnp.cos(angles), jnp.sin(angles)], axis=-1).astype(jnp.bfloat16)


def pool_kernel(text_ref, weight_ref, out_ref):
    tokens = text_ref.shape[1]
    total = jnp.sum(text_ref[0].astype(jnp.float32), axis=0, keepdims=True)
    mean = (total / tokens).astype(jnp.bfloat16)
    part = jnp.dot(mean, weight_ref[...], preferred_element_type=jnp.float32)
    out_ref[...] = jnp.broadcast_to(part[None], out_ref.shape)


def section_kernel(
    section,
    height,
    ints_ref,
    sigma_ref,
    x_ref,
    across_ref,
    beyond_ref,
    parts_ref,
    tpart_ref,
    conv_ref,
    film_ref,
    pay_ref,
    got1_ref,
    got2_ref,
    got3_ref,
    swap1_ref,
    swap2_ref,
    swap3_ref,
    noise_ref,
    noise1_ref,
    noise2_ref,
    noise3_ref,
    out_ref,
    conv_buf,
    film_buf,
    gain_buf,
    noise_buf,
    xs,
    lhs,
    mid,
    sems,
):
    behind = ints_ref[0]
    core = ints_ref[1]
    first = ints_ref[2]
    micro = ints_ref[3]
    rows, cols, channels = xs.shape
    taps = conv_buf.shape[0]
    half = taps // 2

    def copies(j):
        if j == 0:
            pairs = [
                (conv_ref, conv_buf),
                (film_ref.at[:, :channels], film_buf.at[0]),
                (film_ref.at[:, channels:], film_buf.at[1]),
                (pay_ref.at[pl.ds(half + channels, GAIN_ROWS)], gain_buf),
                (noise_ref.at[micro], noise_buf),
            ]
        else:
            got = (got1_ref, got2_ref, got3_ref)[j - 1]
            swap = (swap1_ref, swap2_ref, swap3_ref)[j - 1]
            noise = (noise1_ref, noise2_ref, noise3_ref)[j - 1]
            here = pl.ds(pl.multiple_of(core * half, half), half)
            there = pl.ds(pl.multiple_of((1 - core) * half, half), half)
            pairs = [
                (got.at[pl.ds(0, half)], conv_buf.at[here]),
                (swap.at[pl.ds(0, half)], conv_buf.at[there]),
                (got.at[pl.ds(half, channels)], film_buf.at[core]),
                (swap.at[pl.ds(half, channels)], film_buf.at[1 - core]),
                (got.at[pl.ds(half + channels, GAIN_ROWS)], gain_buf),
                (noise, noise_buf),
            ]
        return [pltpu.make_async_copy(a, b, sems.at[i]) for i, (a, b) in enumerate(pairs)]

    for j in range(4):

        @pl.when(behind == j)
        def _(j=j):
            for copy in copies(j):
                copy.start()

    xs[2:4] = x_ref[...]
    xs[pl.ds(4 * (1 - core), 2)] = across_ref[...]
    xs[pl.ds(4 * core, 2)] = beyond_ref[...]

    for j in range(4):

        @pl.when(behind == j)
        def _(j=j):
            for copy in copies(j):
                copy.wait()

    gains = gain_buf[...].astype(jnp.float32)
    gain = gains[0:1] + gains[1:2] + gains[2:3]
    pooled = jnp.sum(parts_ref[...], axis=0)
    cond = (pooled + tpart_ref[...]).astype(jnp.bfloat16)
    scales = 1.0 + jnp.dot(cond, film_buf[0], preferred_element_type=jnp.float32)
    shifts = jnp.dot(cond, film_buf[1], preferred_element_type=jnp.float32)
    place = lax.broadcasted_iota(jnp.int32, (cols, channels), 0)

    for step in range(STEPS):
        source = xs if step == 0 else mid
        count = rows - 2 * step
        for i in range(count):
            values = source[i].astype(jnp.float32)
            inv = lax.rsqrt(jnp.mean(values * values, axis=-1, keepdims=True) + 1e-06)
            normed = values * inv * gain
            if step > 0:
                image_row = first + i + step
                inside = (image_row >= 0) & (image_row < height)
                normed = jnp.where(inside, normed, 0.0)
            at = pl.ds(i * cols, cols)
            left = jnp.where(place == 0, 0.0, pltpu.roll(normed, 1, 0))
            right = jnp.where(place == cols - 1, 0.0, pltpu.roll(normed, cols - 1, 0))
            lhs[at, 0:channels] = left.astype(jnp.bfloat16)
            lhs[at, channels : 2 * channels] = normed.astype(jnp.bfloat16)
            lhs[at, 2 * channels :] = right.astype(jnp.bfloat16)
        scale = scales[step : step + 1]
        shift = shifts[step : step + 1]
        for i in range(0, count - 2, 2):
            total = None
            for dy in range(3):
                term = jnp.dot(
                    lhs[pl.ds((i + dy) * cols, 2 * cols), :],
                    conv_buf[pl.ds(dy * 3 * channels, 3 * channels), :],
                    preferred_element_type=jnp.float32,
                )
                total = term if total is None else total + term
            moved = total * scale + shift
            branch = moved * (0.5 + 0.5 * jnp.tanh(0.5 * moved))
            before = source[i + 1 : i + 3].astype(jnp.float32).reshape(2 * cols, channels)
            after = before + branch
            if step == STEPS - 1:
                fresh = noise_buf[i : i + 2].astype(jnp.float32).reshape(2 * cols, channels)
                after = after + sigma_ref[section] * fresh
            after = after.astype(jnp.bfloat16).reshape(2, cols, channels)
            if step == STEPS - 1:
                out_ref[i : i + 2] = after
            else:
                mid[i : i + 2] = after


def body(
    latents, noise, timesteps, text, text_weight, time_weight, film_weight, conv_weight, norm_gain
):
    sections = lax.axis_size("segment")
    count = lax.axis_size("row")
    segment = lax.axis_index("segment")
    row = lax.axis_index("row")
    core = row % 2
    own, cols, channels = latents.shape[1:]
    height = own * count
    taps = 9 * channels
    half = taps // 2

    vmem = pl.BlockSpec(memory_space=pltpu.VMEM)
    smem = pl.BlockSpec(memory_space=pltpu.SMEM)
    hbm = pl.BlockSpec(memory_space=pl.ANY)

    conv = conv_weight.reshape(taps, channels)
    film = film_weight[0]
    top = norm_gain.astype(jnp.bfloat16)
    rest = norm_gain - top.astype(jnp.float32)
    middle = rest.astype(jnp.bfloat16)
    low = (rest - middle.astype(jnp.float32)).astype(jnp.bfloat16)
    gains = jnp.concatenate([top, middle, low, jnp.zeros((GAIN_ROWS - 3, channels), jnp.bfloat16)])
    payload = jnp.concatenate(
        [
            lax.dynamic_slice_in_dim(conv, core * half, half, 0),
            lax.dynamic_slice_in_dim(film, core * channels, channels, 1),
            gains,
        ]
    )
    swap_cores = [(i, i ^ 1) for i in range(count)]
    swap_chips = [(i, i + 1) for i in range(1, count - 1, 2)]
    swap_chips = swap_chips + [(b, a) for a, b in swap_chips]

    def turned(value, k):
        return lax.ppermute(value, "segment", [(i, (i + k) % sections) for i in range(sections)])

    got = {k: turned(payload, k) for k in (1, 3, 2)}

    parts = pl.pallas_call(
        pool_kernel,
        out_shape=jax.ShapeDtypeStruct((count, 1, channels), jnp.float32),
        in_specs=[vmem, vmem],
        out_specs=vmem,
    )(text, text_weight)
    parts = lax.all_to_all(parts, "row", split_axis=0, concat_axis=0, tiled=True)

    my_times = lax.dynamic_index_in_dim(timesteps, segment, 0, keepdims=False)
    embed = sinusoid(my_times, channels).reshape(-1, channels)
    tpart = jax.nn.silu(jnp.dot(embed, time_weight, preferred_element_type=jnp.float32))
    tpart = tpart.reshape(sections, STEPS, channels)
    sigma = my_times[:, STEPS - 1].astype(jnp.float32) / 1000.0

    fresh = {}
    for k in (1, 3, 2):
        mine = lax.dynamic_index_in_dim(noise[0], (segment + k) % sections, 0, keepdims=False)
        fresh[k] = turned(mine, k)
    swapped = {k: lax.ppermute(got[k], "row", swap_cores) for k in (1, 3, 2)}

    x = lax.dynamic_index_in_dim(latents, segment, 0, keepdims=False)
    for section in range(sections):
        across = lax.ppermute(x, "row", swap_cores)
        beyond = lax.ppermute(x, "row", swap_chips)
        ints = jnp.stack(
            [(segment - section) % sections, core, row * own - 2, segment]
        ).astype(jnp.int32)
        x = pl.pallas_call(
            functools.partial(section_kernel, section, height),
            out_shape=jax.ShapeDtypeStruct((own, cols, channels), jnp.bfloat16),
            in_specs=[smem, smem] + [vmem] * 5 + [hbm] * 13,
            out_specs=vmem,
            scratch_shapes=[
                pltpu.VMEM((taps, channels), jnp.bfloat16),
                pltpu.VMEM((2, channels, channels), jnp.bfloat16),
                pltpu.VMEM((GAIN_ROWS, channels), jnp.bfloat16),
                pltpu.VMEM((own, cols, channels), jnp.bfloat16),
                pltpu.VMEM((own + 4, cols, channels), jnp.bfloat16),
                pltpu.VMEM(((own + 4) * cols, 3 * channels), jnp.bfloat16),
                pltpu.VMEM((own + 2, cols, channels), jnp.bfloat16),
                pltpu.SemaphoreType.DMA((6,)),
            ],
            compiler_params=pltpu.CompilerParams(vmem_limit_bytes=32 * 1024 * 1024),
        )(
            ints,
            sigma,
            x,
            across,
            beyond,
            parts,
            tpart[section],
            conv,
            film,
            payload,
            got[1],
            got[2],
            got[3],
            swapped[1],
            swapped[2],
            swapped[3],
            noise[0],
            fresh[1],
            fresh[2],
            fresh[3],
        )
    return x[None]


def solution(mesh):
    in_specs = (
        P(None, "row", None, None),
        P("segment", None, "row", None, None),
        P(),
        P("segment", None, "row"),
        P("row", None),
        P(),
        P("segment", None, None),
        P("segment", None, None, None, None),
        P("segment", None),
    )
    out_specs = P("segment", "row", None, None)
    return jax.shard_map(body, mesh=mesh, in_specs=in_specs, out_specs=out_specs, check_vma=False)
```

time: 393 us -> 109 us (0.28)
  the two profiles are of different devices: /device:TPU:1 before, /device:TPU:6 now
where the time goes in v1:
time: 109 us; the launch traced here: 108 us
  starting transfers between devices  41.5 us (38%)
  waiting for transfers between devices  29.4 us (27%)
  Pallas kernels  21.1 us (19%)
  local copies, waits for them, and re-layouts  10.8 us (10%)
  other arithmetic  3.63 us (3%)
  matrix products  1.66 us (2%)
    ppermute x4, starting transfers between devices, body(): beyond = lax.ppermute(x, 'row', swap_chips)  24.6 us
    ppermute x6, waiting for transfers between devices, turned(): lax.ppermute(value, 'segment', [(i, (i + k) % sections) for i in range(se...  21.1 us
    pallas_call x4, Pallas kernels, body(): pl.pallas_call(functools.partial(section_kernel, section, height), out_sh...  19.5 us
    all_to_all x1, starting transfers between devices, body(): lax.all_to_all(parts, 'row', split_axis=0, concat_axis=0, tiled=True)  8.56 us
    ppermute x4, waiting for transfers between devices, body(): beyond = lax.ppermute(x, 'row', swap_chips)  8.26 us
    ppermute x6, starting transfers between devices, turned(): lax.ppermute(value, 'segment', [(i, (i + k) % sections) for i in range(se...  7.42 us
    unnamed x27, local copies, waits for them, and re-layouts  5.84 us
  transfers between devices with their start and end apart: 18, of which 8 were waited for; matrix products, arithmetic and copies ran while one was open for 7% of the time, Pallas kernels for 1%

profile of v1, /device:TPU:6, one launch (start us, length us, event | category | flops | bytes accessed | tf_op | source)
XLA Modules:
  0.0 108.5 jit_solution(10897535171074102994)
XLA Ops:
  0.0 0.8 subtract_convert_fusion
  0.8 0.9 dynamic-slice_bitcast_fusion.3
  1.7 1.1 %constant_dynamic-slice_fusion = bf16[1152,256]{1,0:T(8,128)(2,1)S(1)} fusion(bf16[2304,256]{1,0:T(8,128)(2,1)} %bitcast.26, s32[]{:T(128)S(6)} %select_n.62), kind=kLoop, calls=%fused_computation.14 | loop fusion | bytes 1179652 | tf_op jit(solution)/shard_map/dynamic_slice | solution.py:189
  2.8 0.6 concatenate.9.pay_ref
  3.4 3.1 %collective-permute-start.4 = (bf16[1424,256]{1,0:T(8,128)(2,1)S(1)}, bf16[1424,256]{1,0:T(8,128)(2,1)}, u32[]{:S(2)}, u32[]{:S(2)}) collective-permute-start(bf16[1424,256]{1,0:T(8,128)(2,1)S(1)} %concatenate.9.pay_ref), channel_id=1, source_target_pairs={{0,192},{64,0},{128,64},{192,128},{1,193},{65,1},{129,65},{193,129... | collective-permute-start | bytes 2187272 | tf_op jit(solution)/shard_map/ppermute | solution.py:199
  6.5 0.6 collective-permute-start.3
  7.2 1.0 collective-permute-start.2
  8.2 6.6 %collective-permute-start.1 = (bf16[2,128,256]{2,1,0:T(8,128)(2,1)S(1)}, bf16[2,128,256]{2,1,0:T(8,128)(2,1)S(1)}, u32[]{:S(2)}, u32[]{:S(2)}) collective-permute-start(bf16[2,128,256]{2,1,0:T(8,128)(2,1)S(1)} %dynamic-slice_bitcast_fusion.4.x_ref), channel_id=1, source_target_pairs={{1,2},{3,4},{5,6},{7,8},{9,10},{11,12},{13,14},{15,16},{17,18},{19... | collective-permute-start | bytes 393224 | tf_op jit(solution)/shard_map/ppermute | solution.py:226
  14.8 0.1 collective-permute-start
  14.9 0.7 copy.12.text_ref
  15.6 1.6 %shard_map.91 = f32[64,1,256]{2,1,0:T(1,128)} custom-call(bf16[1,77,64]{2,1,0:T(8,128)(2,1)} %copy.12.text_ref, bf16[64,256]{1,0:T(8,128)(2,1)} %weight_ref.1), custom_call_target="tpu_custom_call" | custom-call | tf_op jit(solution)/shard_map/pallas_call | solution.py:203
  17.2 8.6 %all-to-all-start = ((f32[64,1,256]{2,1,0:T(1,128)}), f32[64,1,256]{2,1,0:T(1,128)S(1)}, u32[]{:S(2)}, u32[]{:S(2)}) async-start(f32[64,1,256]{2,1,0:T(1,128)} %shard_map.91), calls=%async_computation | async-start | bytes 131072 | tf_op jit(solution)/shard_map/all_to_all | solution.py:209
  25.7 1.2 %fusion.8 = (f32[1,4,2]{1,2,0:T(2,128)S(1)}, s32[4,2]{0,1:T(2,128)}) fusion(s32[4,4,2]{1,2,0:T(2,128)} %param.11, s32[]{:T(128)S(6)} %select_n.58), kind=kLoop, calls=%fused_computation.18 | loop fusion | flops 8 | bytes 100 | tf_op jit(solution)/shard_map/convert_element_type | solution.py:17
  27.2 0.1 fusion
  27.3 10.4 %collective-permute-done.4.got3_ref = bf16[1424,256]{1,0:T(8,128)(2,1)} collective-permute-done((bf16[1424,256]{1,0:T(8,128)(2,1)S(1)}, bf16[1424,256]{1,0:T(8,128)(2,1)}, u32[]{:S(2)}, u32[]{:S(2)}) %collective-permute-start.4) | collective-permute-done | bytes 729120 | tf_op jit(solution)/shard_map/ppermute | solution.py:199
  37.7 0.5 collective-permute-start.6
  38.2 3.3 %collective-permute-done.2.got1_ref = bf16[1424,256]{1,0:T(8,128)(2,1)} collective-permute-done((bf16[1424,256]{1,0:T(8,128)(2,1)S(1)}, bf16[1424,256]{1,0:T(8,128)(2,1)}, u32[]{:S(2)}, u32[]{:S(2)}) %collective-permute-start.2) | collective-permute-done | bytes 729120 | tf_op jit(solution)/shard_map/ppermute | solution.py:199
  41.5 1.7 %divide_multiply_fusion = f32[8,256]{1,0:T(8,128)} fusion(bf16[256,256]{1,0:T(8,128)(2,1)} %param.14, bf16[8,128]{1,0:T(8,128)(2,1)S(1)} %get-tuple-element.18, bf16[8,128]{1,0:T(8,128)(2,1)S(1)} %get-tuple-element.17), kind=kOutput, calls=%fused_computation.5 | convolution fusion | flops 1064960 | bytes 143360 | tf_op jit(solution)/shard_map/dot_general | solution.py:213
  43.2 0.7 dynamic-slice_bitcast_fusion
  44.0 0.6 copy-done.6
  44.6 0.6 collective-permute-start.10
  45.2 1.4 %fusion.12 = (f32[2,256]{1,0:T(2,128)S(1)}, f32[2,256]{1,0:T(2,128)}, f32[2,256]{1,0:T(2,128)}, f32[2,256]{1,0:T(2,128)}) fusion(f32[8,256]{1,0:T(8,128)} %divide_multiply_fusion), kind=kLoop, calls=%fused_computation.28 | loop fusion | bytes 16384 | tf_op jit(solution)/shard_map/slice | solution.py:253
  46.7 1.5 %collective-permute-start.8 = (bf16[2,128,256]{2,1,0:T(8,128)(2,1)}, bf16[2,128,256]{2,1,0:T(8,128)(2,1)S(1)}, u32[]{:S(2)}, u32[]{:S(2)}) collective-permute-start(bf16[2,128,256]{2,1,0:T(8,128)(2,1)} %get-tuple-element.6), channel_id=1, source_target_pairs={{0,64},{64,128},{128,192},{192,0},{1,65},{65,129},{129,193},{193,1... | collective-permute-start | bytes 393224 | tf_op jit(solution)/shard_map/ppermute | solution.py:199
  48.2 2.3 %collective-permute-done.10.noise3_ref = bf16[2,128,256]{2,1,0:T(8,128)(2,1)S(1)} collective-permute-done((bf16[2,128,256]{2,1,0:T(8,128)(2,1)S(1)}, bf16[2,128,256]{2,1,0:T(8,128)(2,1)S(1)}, u32[]{:S(2)}, u32[]{:S(2)}) %collective-permute-start.10) | collective-permute-done | bytes 131104 | tf_op jit(solution)/shard_map/ppermute | solution.py:199
  50.5 0.6 collective-permute-start.9
  51.1 0.7 multiply_bitcast_fusion.sigma_ref
  51.8 0.6 add_add_fusion.3.ints_ref
  52.4 1.4 %collective-permute-done.8.noise1_ref = bf16[2,128,256]{2,1,0:T(8,128)(2,1)S(1)} collective-permute-done((bf16[2,128,256]{2,1,0:T(8,128)(2,1)}, bf16[2,128,256]{2,1,0:T(8,128)(2,1)S(1)}, u32[]{:S(2)}, u32[]{:S(2)}) %collective-permute-start.8) | collective-permute-done | bytes 131104 | tf_op jit(solution)/shard_map/ppermute | solution.py:199
  53.8 3.7 %collective-permute-done.9.noise2_ref = bf16[2,128,256]{2,1,0:T(8,128)(2,1)} collective-permute-done((bf16[2,128,256]{2,1,0:T(8,128)(2,1)}, bf16[2,128,256]{2,1,0:T(8,128)(2,1)}, u32[]{:S(2)}, u32[]{:S(2)}) %collective-permute-start.9) | collective-permute-done | bytes 131104 | tf_op jit(solution)/shard_map/ppermute | solution.py:199
  57.5 0.9 copy-done.5
  58.4 0.9 copy-done.7
  59.3 0.7 copy-done.10
  60.0 0.6 copy-done.11
  60.6 4.2 %shard_map.92.x_ref = bf16[2,128,256]{2,1,0:T(8,128)(2,1)} custom-call(s32[4]{0:T(128)S(1)} %copy-done.11, f32[4]{0:T(128)S(1)} %multiply_bitcast_fusion.sigma_ref, bf16[2,128,256]{2,1,0:T(8,128)(2,1)S(1)} %copy-done.5, bf16[2,128,256]{2,1,0:T(8,128)(2,1)} %collective-permute-done.across_ref, bf16[2,128,256]{2,1,0:T(8,128)(2,1)S(1)} %copy-done.7, ...), custom_call_target="tpu_custom_call" | custom-call | tf_op jit(solution)/shard_map/pallas_call | solution.py:230
  64.8 6.5 %collective-permute-start.12 = (bf16[2,128,256]{2,1,0:T(8,128)(2,1)}, bf16[2,128,256]{2,1,0:T(8,128)(2,1)}, u32[]{:S(2)}, u32[]{:S(2)}) collective-permute-start(bf16[2,128,256]{2,1,0:T(8,128)(2,1)} %shard_map.92.x_ref), channel_id=1, source_target_pairs={{1,2},{3,4},{5,6},{7,8},{9,10},{11,12},{13,14},{15,16},{17,18},{19... | collective-permute-start | bytes 393224 | tf_op jit(solution)/shard_map/ppermute | solution.py:226
  71.2 0.1 collective-permute-start.11
  71.4 2.8 %collective-permute-done.12.beyond_ref = bf16[2,128,256]{2,1,0:T(8,128)(2,1)} collective-permute-done((bf16[2,128,256]{2,1,0:T(8,128)(2,1)}, bf16[2,128,256]{2,1,0:T(8,128)(2,1)}, u32[]{:S(2)}, u32[]{:S(2)}) %collective-permute-start.12) | collective-permute-done | bytes 131104 | tf_op jit(solution)/shard_map/ppermute | solution.py:226
  74.2 0.7 copy-done.9
  74.9 5.1 %shard_map.93.x_ref = bf16[2,128,256]{2,1,0:T(8,128)(2,1)} custom-call(s32[4]{0:T(128)S(1)} %add_add_fusion.2.ints_ref, f32[4]{0:T(128)S(1)} %multiply_bitcast_fusion.sigma_ref, bf16[2,128,256]{2,1,0:T(8,128)(2,1)} %shard_map.92.x_ref, bf16[2,128,256]{2,1,0:T(8,128)(2,1)} %collective-permute-done.11.across_ref, ...), custom_call_target="tpu_custom_call" | custom-call | tf_op jit(solution)/shard_map/pallas_call | solution.py:230
  80.0 5.8 %collective-permute-start.14 = (bf16[2,128,256]{2,1,0:T(8,128)(2,1)}, bf16[2,128,256]{2,1,0:T(8,128)(2,1)}, u32[]{:S(2)}, u32[]{:S(2)}) collective-permute-start(bf16[2,128,256]{2,1,0:T(8,128)(2,1)} %shard_map.93.x_ref), channel_id=1, source_target_pairs={{1,2},{3,4},{5,6},{7,8},{9,10},{11,12},{13,14},{15,16},{17,18},{19... | collective-permute-start | bytes 393224 | tf_op jit(solution)/shard_map/ppermute | solution.py:226
  85.7 0.1 collective-permute-start.13
  85.9 2.8 %collective-permute-done.14.beyond_ref = bf16[2,128,256]{2,1,0:T(8,128)(2,1)} collective-permute-done((bf16[2,128,256]{2,1,0:T(8,128)(2,1)}, bf16[2,128,256]{2,1,0:T(8,128)(2,1)}, u32[]{:S(2)}, u32[]{:S(2)}) %collective-permute-start.14) | collective-permute-done | bytes 131104 | tf_op jit(solution)/shard_map/ppermute | solution.py:226
  88.7 0.7 copy-done.8
  89.4 5.1 %shard_map.94.x_ref = bf16[2,128,256]{2,1,0:T(8,128)(2,1)} custom-call(s32[4]{0:T(128)S(1)} %add_add_fusion.1.ints_ref, f32[4]{0:T(128)S(1)} %multiply_bitcast_fusion.sigma_ref, bf16[2,128,256]{2,1,0:T(8,128)(2,1)} %shard_map.93.x_ref, bf16[2,128,256]{2,1,0:T(8,128)(2,1)} %collective-permute-done.13.across_ref, ...), custom_call_target="tpu_custom_call" | custom-call | tf_op jit(solution)/shard_map/pallas_call | solution.py:230
  94.5 5.8 %collective-permute-start.16 = (bf16[2,128,256]{2,1,0:T(8,128)(2,1)}, bf16[2,128,256]{2,1,0:T(8,128)(2,1)}, u32[]{:S(2)}, u32[]{:S(2)}) collective-permute-start(bf16[2,128,256]{2,1,0:T(8,128)(2,1)} %shard_map.94.x_ref), channel_id=1, source_target_pairs={{1,2},{3,4},{5,6},{7,8},{9,10},{11,12},{13,14},{15,16},{17,18},{19... | collective-permute-start | bytes 393224 | tf_op jit(solution)/shard_map/ppermute | solution.py:226
  100.3 0.1 collective-permute-start.15
  100.5 2.8 %collective-permute-done.16.beyond_ref = bf16[2,128,256]{2,1,0:T(8,128)(2,1)} collective-permute-done((bf16[2,128,256]{2,1,0:T(8,128)(2,1)}, bf16[2,128,256]{2,1,0:T(8,128)(2,1)}, u32[]{:S(2)}, u32[]{:S(2)}) %collective-permute-start.16) | collective-permute-done | bytes 131104 | tf_op jit(solution)/shard_map/ppermute | solution.py:226
  103.2 5.1 %shard_map.95 = bf16[2,128,256]{2,1,0:T(8,128)(2,1)} custom-call(s32[4]{0:T(128)S(1)} %add_add_fusion.ints_ref, f32[4]{0:T(128)S(1)} %multiply_bitcast_fusion.sigma_ref, bf16[2,128,256]{2,1,0:T(8,128)(2,1)} %shard_map.94.x_ref, bf16[2,128,256]{2,1,0:T(8,128)(2,1)} %collective-permute-done.15.across_ref, ...), custom_call_target="tpu_custom_call" | custom-call | tf_op jit(solution)/shard_map/pallas_call | solution.py:230
  (39 shorter events, 0.5 us)
Async XLA Ops:
  0.0 8.1 %copy-start = (bf16[4,2,128,256]{3,2,1,0:T(8,128)(2,1)S(1)}, bf16[4,2,128,256]{3,2,1,0:T(8,128)(2,1)}, u32[]{:S(2)}) copy-start(bf16[4,2,128,256]{3,2,1,0:T(8,128)(2,1)} %param.9) | copy-start | bytes 1572868
  1.7 13.2 %copy-start.12 = (bf16[1,77,64]{1,2,0:T(8,128)(2,1)S(1)}, bf16[1,77,64]{1,2,0:T(8,128)(2,1)}, u32[]{:S(2)}) copy-start(bf16[1,77,64]{1,2,0:T(8,128)(2,1)} %param.12) | copy-start | bytes 29572
  2.8 40.4 %copy-start.2 = (bf16[1,4,2,128,256]{4,3,2,1,0:T(8,128)(2,1)S(1)}, bf16[1,4,2,128,256]{4,3,2,1,0:T(8,128)(2,1)}, u32[]{:S(2)}) copy-start(bf16[1,4,2,128,256]{4,3,2,1,0:T(8,128)(2,1)} %param.10) | copy-start | bytes 1572868
  3.4 54.1 %copy-start.1 = (bf16[1,3,3,256,256]{4,3,2,1,0:T(8,128)(2,1)S(1)}, bf16[1,3,3,256,256]{4,3,2,1,0:T(8,128)(2,1)}, u32[]{:S(2)}) copy-start(bf16[1,3,3,256,256]{4,3,2,1,0:T(8,128)(2,1)} %param.16) | copy-start | bytes 3538948
  3.4 54.1 %copy-start.3 = (bf16[1,256,512]{2,1,0:T(8,128)(2,1)S(1)}, bf16[1,256,512]{2,1,0:T(8,128)(2,1)}, u32[]{:S(2)}) copy-start(bf16[1,256,512]{2,1,0:T(8,128)(2,1)} %param.15) | copy-start | bytes 786436
  3.4 34.3 %collective-permute-start.4 = (bf16[1424,256]{1,0:T(8,128)(2,1)S(1)}, bf16[1424,256]{1,0:T(8,128)(2,1)}, u32[]{:S(2)}, u32[]{:S(2)}) collective-permute-start(bf16[1424,256]{1,0:T(8,128)(2,1)S(1)} %concatenate.9.pay_ref), channel_id=1, source_target_pairs={{0,192},{64,0},{128,64},{192,128},{1,193},{65,1},{129,65},{193,129... | collective-permute-start | bytes 2187272 | tf_op jit(solution)/shard_map/ppermute | solution.py:199
  6.5 31.2 %collective-permute-start.3 = (bf16[1424,256]{1,0:T(8,128)(2,1)S(1)}, bf16[1424,256]{1,0:T(8,128)(2,1)}, u32[]{:S(2)}, u32[]{:S(2)}) collective-permute-start(bf16[1424,256]{1,0:T(8,128)(2,1)S(1)} %concatenate.9.pay_ref), channel_id=1, source_target_pairs={{0,128},{64,192},{128,0},{192,64},{1,129},{65,193},{129,1},{193,65... | collective-permute-start | bytes 2187272 | tf_op jit(solution)/shard_map/ppermute | solution.py:199
  7.2 34.4 %collective-permute-start.2 = (bf16[1424,256]{1,0:T(8,128)(2,1)S(1)}, bf16[1424,256]{1,0:T(8,128)(2,1)}, u32[]{:S(2)}, u32[]{:S(2)}) collective-permute-start(bf16[1424,256]{1,0:T(8,128)(2,1)S(1)} %concatenate.9.pay_ref), channel_id=1, source_target_pairs={{0,64},{64,128},{128,192},{192,0},{1,65},{65,129},{129,193},{193,1... | collective-permute-start | bytes 2187272 | tf_op jit(solution)/shard_map/ppermute | solution.py:199
  8.1 38.5 %copy-start.4 = (bf16[2,128,256]{2,1,0:T(8,128)(2,1)}, bf16[2,128,256]{2,1,0:T(8,128)(2,1)S(1)}, u32[]{:S(2)}) copy-start(bf16[2,128,256]{2,1,0:T(8,128)(2,1)S(1)} %dynamic-slice_bitcast_fusion.4.x_ref) | copy-start | bytes 393220
  8.2 35.8 %collective-permute-start.1 = (bf16[2,128,256]{2,1,0:T(8,128)(2,1)S(1)}, bf16[2,128,256]{2,1,0:T(8,128)(2,1)S(1)}, u32[]{:S(2)}, u32[]{:S(2)}) collective-permute-start(bf16[2,128,256]{2,1,0:T(8,128)(2,1)S(1)} %dynamic-slice_bitcast_fusion.4.x_ref), channel_id=1, source_target_pairs={{1,2},{3,4},{5,6},{7,8},{9,10},{11,12},{13,14},{15,16},{17,18},{19... | collective-permute-start | bytes 393224 | tf_op jit(solution)/shard_map/ppermute | solution.py:226
  14.8 31.9 %collective-permute-start = (bf16[2,128,256]{2,1,0:T(8,128)(2,1)S(1)}, bf16[2,128,256]{2,1,0:T(8,128)(2,1)}, u32[]{:S(2)}, u32[]{:S(2)}) collective-permute-start(bf16[2,128,256]{2,1,0:T(8,128)(2,1)S(1)} %dynamic-slice_bitcast_fusion.4.x_ref), channel_id=1, source_target_pairs={{0,1},{1,0},{2,3},{3,2},{4,5},{5,4},{6,7},{7,6},{8,9},{9,8},{10,11... | collective-permute-start | bytes 393224 | tf_op jit(solution)/shard_map/ppermute | solution.py:225
  17.2 35.2 %all-to-all-start = ((f32[64,1,256]{2,1,0:T(1,128)}), f32[64,1,256]{2,1,0:T(1,128)S(1)}, u32[]{:S(2)}, u32[]{:S(2)}) async-start(f32[64,1,256]{2,1,0:T(1,128)} %shard_map.91), calls=%async_computation | async-start | bytes 131072 | tf_op jit(solution)/shard_map/all_to_all | solution.py:209
  37.7 19.7 %collective-permute-start.7 = (bf16[1424,256]{1,0:T(8,128)(2,1)}, bf16[1424,256]{1,0:T(8,128)(2,1)}, u32[]{:S(2)}, u32[]{:S(2)}) collective-permute-start(bf16[1424,256]{1,0:T(8,128)(2,1)} %collective-permute-done.4.got3_ref), channel_id=1, source_target_pairs={{0,1},{1,0},{2,3},{3,2},{4,5},{5,4},{6,7},{7,6},{8,9},{9,8},{10,11... | collective-permute-start | bytes 2187272 | tf_op jit(solution)/shard_map/ppermute | solution.py:221
  37.7 19.7 %collective-permute-start.6 = (bf16[1424,256]{1,0:T(8,128)(2,1)}, bf16[1424,256]{1,0:T(8,128)(2,1)}, u32[]{:S(2)}, u32[]{:S(2)}) collective-permute-start(bf16[1424,256]{1,0:T(8,128)(2,1)} %collective-permute-done.3.got2_ref), channel_id=1, source_target_pairs={{0,1},{1,0},{2,3},{3,2},{4,5},{5,4},{6,7},{7,6},{8,9},{9,8},{10,11... | collective-permute-start | bytes 2187272 | tf_op jit(solution)/shard_map/ppermute | solution.py:221
  41.5 15.9 %collective-permute-start.5 = (bf16[1424,256]{1,0:T(8,128)(2,1)}, bf16[1424,256]{1,0:T(8,128)(2,1)}, u32[]{:S(2)}, u32[]{:S(2)}) collective-permute-start(bf16[1424,256]{1,0:T(8,128)(2,1)} %collective-permute-done.2.got1_ref), channel_id=1, source_target_pairs={{0,1},{1,0},{2,3},{3,2},{4,5},{5,4},{6,7},{7,6},{8,9},{9,8},{10,11... | collective-permute-start | bytes 2187272 | tf_op jit(solution)/shard_map/ppermute | solution.py:221
  44.0 0.7 copy-start.6
  44.6 5.9 %collective-permute-start.10 = (bf16[2,128,256]{2,1,0:T(8,128)(2,1)S(1)}, bf16[2,128,256]{2,1,0:T(8,128)(2,1)S(1)}, u32[]{:S(2)}, u32[]{:S(2)}) collective-permute-start(bf16[2,128,256]{2,1,0:T(8,128)(2,1)S(1)} %get-tuple-element.5), channel_id=1, source_target_pairs={{0,192},{64,0},{128,64},{192,128},{1,193},{65,1},{129,65},{193,129... | collective-permute-start | bytes 393224 | tf_op jit(solution)/shard_map/ppermute | solution.py:199
  46.7 7.1 %collective-permute-start.8 = (bf16[2,128,256]{2,1,0:T(8,128)(2,1)}, bf16[2,128,256]{2,1,0:T(8,128)(2,1)S(1)}, u32[]{:S(2)}, u32[]{:S(2)}) collective-permute-start(bf16[2,128,256]{2,1,0:T(8,128)(2,1)} %get-tuple-element.6), channel_id=1, source_target_pairs={{0,64},{64,128},{128,192},{192,0},{1,65},{65,129},{129,193},{193,1... | collective-permute-start | bytes 393224 | tf_op jit(solution)/shard_map/ppermute | solution.py:199
  50.5 6.9 %collective-permute-start.9 = (bf16[2,128,256]{2,1,0:T(8,128)(2,1)}, bf16[2,128,256]{2,1,0:T(8,128)(2,1)}, u32[]{:S(2)}, u32[]{:S(2)}) collective-permute-start(bf16[2,128,256]{2,1,0:T(8,128)(2,1)} %get-tuple-element.7), channel_id=1, source_target_pairs={{0,128},{64,192},{128,0},{192,64},{1,129},{65,193},{129,1},{193,65... | collective-permute-start | bytes 393224 | tf_op jit(solution)/shard_map/ppermute | solution.py:199
  57.5 0.9 copy-start.5
  58.4 0.9 copy-start.7
  59.3 0.7 copy-start.10
  60.0 0.6 copy-start.11
  64.8 9.4 %collective-permute-start.12 = (bf16[2,128,256]{2,1,0:T(8,128)(2,1)}, bf16[2,128,256]{2,1,0:T(8,128)(2,1)}, u32[]{:S(2)}, u32[]{:S(2)}) collective-permute-start(bf16[2,128,256]{2,1,0:T(8,128)(2,1)} %shard_map.92.x_ref), channel_id=1, source_target_pairs={{1,2},{3,4},{5,6},{7,8},{9,10},{11,12},{13,14},{15,16},{17,18},{19... | collective-permute-start | bytes 393224 | tf_op jit(solution)/shard_map/ppermute | solution.py:226
  71.2 3.0 %collective-permute-start.11 = (bf16[2,128,256]{2,1,0:T(8,128)(2,1)}, bf16[2,128,256]{2,1,0:T(8,128)(2,1)}, u32[]{:S(2)}, u32[]{:S(2)}) collective-permute-start(bf16[2,128,256]{2,1,0:T(8,128)(2,1)} %shard_map.92.x_ref), channel_id=1, source_target_pairs={{0,1},{1,0},{2,3},{3,2},{4,5},{5,4},{6,7},{7,6},{8,9},{9,8},{10,11... | collective-permute-start | bytes 393224 | tf_op jit(solution)/shard_map/ppermute | solution.py:225
  74.2 0.7 copy-start.9
  80.0 8.7 %collective-permute-start.14 = (bf16[2,128,256]{2,1,0:T(8,128)(2,1)}, bf16[2,128,256]{2,1,0:T(8,128)(2,1)}, u32[]{:S(2)}, u32[]{:S(2)}) collective-permute-start(bf16[2,128,256]{2,1,0:T(8,128)(2,1)} %shard_map.93.x_ref), channel_id=1, source_target_pairs={{1,2},{3,4},{5,6},{7,8},{9,10},{11,12},{13,14},{15,16},{17,18},{19... | collective-permute-start | bytes 393224 | tf_op jit(solution)/shard_map/ppermute | solution.py:226
  85.7 3.0 %collective-permute-start.13 = (bf16[2,128,256]{2,1,0:T(8,128)(2,1)}, bf16[2,128,256]{2,1,0:T(8,128)(2,1)}, u32[]{:S(2)}, u32[]{:S(2)}) collective-permute-start(bf16[2,128,256]{2,1,0:T(8,128)(2,1)} %shard_map.93.x_ref), channel_id=1, source_target_pairs={{0,1},{1,0},{2,3},{3,2},{4,5},{5,4},{6,7},{7,6},{8,9},{9,8},{10,11... | collective-permute-start | bytes 393224 | tf_op jit(solution)/shard_map/ppermute | solution.py:225
  88.7 0.7 copy-start.8
  94.5 8.7 %collective-permute-start.16 = (bf16[2,128,256]{2,1,0:T(8,128)(2,1)}, bf16[2,128,256]{2,1,0:T(8,128)(2,1)}, u32[]{:S(2)}, u32[]{:S(2)}) collective-permute-start(bf16[2,128,256]{2,1,0:T(8,128)(2,1)} %shard_map.94.x_ref), channel_id=1, source_target_pairs={{1,2},{3,4},{5,6},{7,8},{9,10},{11,12},{13,14},{15,16},{17,18},{19... | collective-permute-start | bytes 393224 | tf_op jit(solution)/shard_map/ppermute | solution.py:226
  100.3 3.0 %collective-permute-start.15 = (bf16[2,128,256]{2,1,0:T(8,128)(2,1)}, bf16[2,128,256]{2,1,0:T(8,128)(2,1)}, u32[]{:S(2)}, u32[]{:S(2)}) collective-permute-start(bf16[2,128,256]{2,1,0:T(8,128)(2,1)} %shard_map.94.x_ref), channel_id=1, source_target_pairs={{0,1},{1,0},{2,3},{3,2},{4,5},{5,4},{6,7},{7,6},{8,9},{9,8},{10,11... | collective-permute-start | bytes 393224 | tf_op jit(solution)/shard_map/ppermute | solution.py:225

commit v2 on v0

v2 whole, which is shorter than its diff:
```python
import functools
import math

import jax
import jax.numpy as jnp
from jax import lax
from jax.experimental import pallas as pl
from jax.experimental.pallas import tpu as pltpu
from jax.sharding import PartitionSpec as P

STEPS = 2
GAIN_ROWS = 16
MIB = 1024 * 1024


def place_of_device():
    row = lax.axis_index("row")
    return lax.axis_index("segment"), row, lax.rem(row, 2)


def prepare_kernel(
    latents, noise, conv, film, gain, x_out, pay0, pay1, more0, more1, noise2, sems
):
    segment, _, core = place_of_device()
    half = conv.shape[0] // 2
    channels = conv.shape[1]
    cols = latents.shape[2]
    cut = pay0.shape[0]
    start = core * half
    before, after = (noise.at[lax.rem(segment + k, 4)] for k in (3, 1))
    pairs = [(latents.at[segment], x_out), (noise.at[lax.rem(segment + 2, 4)], noise2)]
    for target in (pay0, more0):
        pairs.append((conv.at[pl.ds(pl.multiple_of(start, 16), cut)], target.at[pl.ds(0, cut)]))
    for target in (pay1, more1):
        source = conv.at[pl.ds(pl.multiple_of(start + cut, 16), half - cut)]
        pairs.append((source, target.at[pl.ds(0, half - cut)]))
    for i in range(2):
        pairs.append((before.at[i], more0.at[pl.ds(cut + i * cols, cols)]))
        pairs.append((after.at[i], more1.at[pl.ds(pay1.shape[0] + i * cols, cols)]))
    copies = [pltpu.make_async_copy(a, b, sems.at[i]) for i, (a, b) in enumerate(pairs)]
    film_at = pl.ds(half - cut, channels)
    sides = [
        [
            pltpu.make_async_copy(
                film.at[:, i * channels : (i + 1) * channels], target.at[film_at], sems.at[10 + j]
            )
            for j, target in enumerate((pay1, more1))
        ]
        for i in range(2)
    ]
    for copy in copies:
        copy.start()
    for i in range(2):

        @pl.when(core == i)
        def _(i=i):
            for copy in sides[i]:
                copy.start()

    exact = gain[...]
    top = exact.astype(jnp.bfloat16).astype(jnp.float32)
    middle = (exact - top).astype(jnp.bfloat16).astype(jnp.float32)
    low = exact - top - middle
    line = lax.broadcasted_iota(jnp.int32, (GAIN_ROWS, channels), 0)
    rows = jnp.where(line == 0, top, jnp.where(line == 1, middle, jnp.where(line == 2, low, 0.0)))
    for target in (pay1, more1):
        target[pl.ds(half - cut + channels, GAIN_ROWS), :] = rows.astype(jnp.bfloat16)
    for copy in copies:
        copy.wait()
    for i in range(2):

        @pl.when(core == i)
        def _(i=i):
            for copy in sides[i]:
                copy.wait()


def condition_kernel(times, text, text_weight, time_weight, x_core, parts_out, tpart_out):
    segment, _, _ = place_of_device()
    tokens = text.shape[1]
    channels = time_weight.shape[0]
    total = jnp.sum(text[0].astype(jnp.float32), axis=0, keepdims=True)
    mean = (total / tokens).astype(jnp.bfloat16)
    part = jnp.dot(mean, text_weight[...], preferred_element_type=jnp.float32)
    parts_out[...] = jnp.broadcast_to(part[None], parts_out.shape)
    count = tpart_out.shape[0]
    half = channels // 2
    line = lax.broadcasted_iota(jnp.int32, (count, half), 0)
    moments = jnp.zeros((count, half), jnp.float32)
    for i in range(count):
        now = times[segment, i // STEPS, i % STEPS].astype(jnp.float32)
        moments = jnp.where(line == i, now, moments)
    place = lax.broadcasted_iota(jnp.int32, (count, half), 1).astype(jnp.float32)
    angles = moments * jnp.exp(-math.log(10000.0) * place / half)
    embed = jnp.concatenate([jnp.cos(angles), jnp.sin(angles)], axis=-1).astype(jnp.bfloat16)
    value = jnp.dot(embed, time_weight[...], preferred_element_type=jnp.float32)
    tpart_out[...] = value * (0.5 + 0.5 * jnp.tanh(0.5 * value))


def after_kernel(first, second, parts, first_out, second_out):
    pass


def choose_kernel(noise, more1, noise2, more0, first, n_out, sems):
    segment, _, _ = place_of_device()
    sections = 4
    cols = n_out.shape[1]
    for act in ("start", "wait"):
        for section in range(sections - 1):
            behind = lax.rem(segment - section + sections, sections)
            for j in range(sections):

                @pl.when(behind == j)
                def _(j=j, section=section):
                    for i in range(2):
                        source = noise_row(j, i, cols, noise.at[segment], more1, noise2, more0)
                        target = n_out.at[2 * section + i]
                        copy = pltpu.make_async_copy(source, target, sems.at[section, i])
                        getattr(copy, act)()


def noise_row(j, i, cols, own, more1, noise2, more0):
    if j in (0, 2):
        return (own if j == 0 else noise2).at[i]
    source = more1 if j == 1 else more0
    return source.at[pl.ds(source.shape[0] - (2 - i) * cols, cols)]


def cascade_kernel(sections, height, names, *refs):
    r = dict(zip(names, refs))
    segment, row, core = place_of_device()
    lhs, mid, xs = r["lhs"], r["mid"], r["xs"]
    taps, channels = r["conv"].shape
    cols = xs.shape[1]
    half = taps // 2
    own = 2
    total_sections = r["tpart"].shape[0] // STEPS
    leading = sections[0] == 0

    strips = {}
    if leading:
        near, far, back = (r["near"], r["far"], r["back"])
        strips["xs"] = [
            (r["latents"].at[segment], 8, 8),
            (r["x_core"], 10, 6),
            (near.at[0:2], 4, 12),
            (near.at[2:4], 6, 10),
            (far.at[0:2], 0, 16),
            (far.at[2:4], 2, 14),
            (back.at[0:2], 14, 2),
            (back.at[2:4], 12, 4),
            (back.at[4:6], 16, 0),
        ]
    else:
        (n, n_core, n_near, n_far, n_back) = (
            r[key] for key in ("n", "n_core", "n_near", "n_far", "n_back")
        )
        strips["noise0"] = [
            (n.at[0:2], 6, 6),
            (n_core.at[0:2], 8, 4),
            (n_near.at[0:2], 2, 10),
            (n_near.at[4:6], 4, 8),
            (n_far, 0, 12),
            (n_back.at[0:2], 12, 0),
            (n_back.at[2:4], 10, 2),
        ]
        strips["noise1"] = [
            (n.at[2:4], 4, 4),
            (n_core.at[2:4], 6, 2),
            (n_near.at[2:4], 0, 8),
            (n_near.at[6:8], 2, 6),
            (n_back.at[4:6], 8, 0),
        ]
        strips["noise2"] = [(n.at[4:6], 2, 2), (n_core.at[4:6], 4, 0), (n_near.at[8:10], 0, 4)]
    moves = {}
    for key, placed in strips.items():
        moves[key] = []
        for i, (value, first, second) in enumerate(placed):
            target = r[key].at[pl.ds(first + core * (second - first), 2)]
            moves[key].append(pltpu.make_async_copy(value, target, r["strip_sems"].at[len(moves), i]))

    def weights_of(section):
        slot = section - sections[0]
        return [r[key].at[slot] for key in ("conv_buf", "film_buf", "gain_buf")]

    def copies(section, j, which):
        weights, films, gains = weights_of(section)
        sems = r["sems"].at[section]
        if j == 0:
            small = [
                (r["film"].at[:, :channels], films.at[0]),
                (r["film"].at[:, channels:], films.at[1]),
            ]
            large = [(r["conv"], weights)]
        else:
            cut = r["got1_0"].shape[0]
            small, large = ([], [])
            for key, side in (("got", core), ("swap", 1 - core)):
                part0, part1 = (r["%s%d_%d" % (key, j, i)] for i in range(2))
                if not small:
                    small.append((part1.at[pl.ds(half - cut + channels, GAIN_ROWS)], gains))
                at0 = pl.multiple_of(side * half, 16)
                at1 = pl.multiple_of(side * half + cut, 16)
                large.append((part0.at[pl.ds(0, cut)], weights.at[pl.ds(at0, cut)]))
                large.append((part1.at[pl.ds(0, half - cut)], weights.at[pl.ds(at1, half - cut)]))
                small.append((part1.at[pl.ds(half - cut, channels)], films.at[side]))
        pairs = {"small": small, "large": large, "all": small + large}[which]
        base = len(small) if which == "large" else 0
        return [pltpu.make_async_copy(a, b, sems.at[base + i]) for i, (a, b) in enumerate(pairs)]

    behind = [lax.rem(segment - section + 4, 4) for section in range(total_sections)]

    def each(section, act, which="all"):
        for j in range(4):

            @pl.when(behind[section] == j)
            def _(j=j):
                for copy in copies(section, j, which):
                    act(copy)

    def each_noise(act):
        for j in range(4):

            @pl.when(behind[total_sections - 1] == j)
            def _(j=j):
                for i in range(2):
                    source = noise_row(
                        j, i, cols, r["noise"].at[segment], r["got1_1"], r["noise_far"], r["got3_0"]
                    )
                    act(pltpu.make_async_copy(source, r["noise3"].at[i], r["strip_sems"].at[4, i]))

    def start(copy):
        copy.start()

    def wait(copy):
        copy.wait()

    strip_keys = list(moves)
    for copy in moves[strip_keys[0]]:
        copy.start()
    each(sections[0], start)

    def sigma(section):
        moment = r["times"][segment, section, STEPS - 1].astype(jnp.float32)
        return jnp.full((1, channels), moment, jnp.float32) / 1000.0

    pooled = jnp.sum(r["parts"][...], axis=0)
    place = lax.broadcasted_iota(jnp.int32, (cols, channels), 0)
    for copy in moves["xs" if leading else "noise0"]:
        copy.wait()
    if not leading:
        sigma0 = sigma(0)
        for i in range(xs.shape[0]):
            noisy = r["before"][i] + sigma0 * r["noise0"][i].astype(jnp.float32)
            xs[i] = noisy.astype(jnp.bfloat16)

    source = xs
    for section in sections:
        conv_now, film_now, gain_now = weights_of(section)
        each(section, wait, "small")
        gains = gain_now[...].astype(jnp.float32)
        gain = gains[0:1] + gains[1:2] + gains[2:3]
        gain = jnp.where(behind[section] == 0, r["gain"][...], gain)
        noise_scale = sigma(section)
        for step in range(STEPS):
            left_over = (total_sections - section) * STEPS - step
            count = own + 2 * left_over
            for i in range(count):
                values = source[i].astype(jnp.float32)
                inv = lax.rsqrt(jnp.mean(values * values, axis=-1, keepdims=True) + 1e-06)
                normed = values * inv * gain
                if i < left_over or i >= left_over + own:
                    image_row = row * own - left_over + i
                    inside = (image_row >= 0) & (image_row < height)
                    normed = jnp.where(inside, normed, 0.0)
                at = pl.ds(i * cols, cols)
                left = jnp.where(place == 0, 0.0, pltpu.roll(normed, 1, 0))
                right = jnp.where(place == cols - 1, 0.0, pltpu.roll(normed, cols - 1, 0))
                lhs[at, 0:channels] = left.astype(jnp.bfloat16)
                lhs[at, channels : 2 * channels] = normed.astype(jnp.bfloat16)
                lhs[at, 2 * channels :] = right.astype(jnp.bfloat16)
            if step == 0:
                cond = pooled + r["tpart"][STEPS * section : STEPS * (section + 1)]
                cond = cond.astype(jnp.bfloat16)
                scales = 1.0 + jnp.dot(cond, film_now[0], preferred_element_type=jnp.float32)
                shifts = jnp.dot(cond, film_now[1], preferred_element_type=jnp.float32)
                each(section, wait, "large")
                if section == sections[0]:
                    for later in sections[1:]:
                        each(later, start)
                    for key in strip_keys[1:]:
                        for copy in moves[key]:
                            copy.start()
                    if not leading:
                        each_noise(start)
            last = step == STEPS - 1
            noised = last and section > 0
            if noised and section < total_sections - 1:
                for copy in moves["noise%d" % section]:
                    copy.wait()
            elif noised:
                each_noise(wait)
            if not last:
                target = mid
            elif section == sections[-1]:
                target = r["out"]
            else:
                target = xs
            for i in range(count - 2):
                window = jnp.concatenate(
                    [lhs[pl.ds((i + dy) * cols, cols), :] for dy in range(3)], axis=1
                )
                total = jnp.dot(window, conv_now[...], preferred_element_type=jnp.float32)
                moved = total * scales[step : step + 1] + shifts[step : step + 1]
                branch = moved * (0.5 + 0.5 * jnp.tanh(0.5 * moved))
                after = source[i + 1].astype(jnp.float32) + branch
                if noised:
                    fresh = r["noise%d" % section][i].astype(jnp.float32)
                    after = after + noise_scale * fresh
                target[i] = after.astype(target.dtype)
            source = target


def cascade(group, operands, out_dtype, taps, channels, cols, own, sections, height):
    rows = own + 2 * STEPS * (sections - group[0])
    out_rows = own + 2 * STEPS * (sections - 1 - group[-1])
    outputs = {"out": jax.ShapeDtypeStruct((out_rows, cols, channels), out_dtype)}
    scratch = {
        "xs": pltpu.VMEM((rows, cols, channels), jnp.bfloat16),
        "mid": pltpu.VMEM((rows, cols, channels), jnp.bfloat16),
        "lhs": pltpu.VMEM((rows * cols, 3 * channels), jnp.bfloat16),
        "sems": pltpu.SemaphoreType.DMA((sections, 7)),
        "strip_sems": pltpu.SemaphoreType.DMA((5, 9)),
    }
    slots = len(group)
    scratch["conv_buf"] = pltpu.VMEM((slots, taps, channels), jnp.bfloat16)
    scratch["film_buf"] = pltpu.VMEM((slots, 2, channels, channels), jnp.bfloat16)
    scratch["gain_buf"] = pltpu.VMEM((slots, GAIN_ROWS, channels), jnp.bfloat16)
    if group[0] > 0:
        for section in range(sections):
            noise_rows = own + 2 * STEPS * (sections - 1 - section)
            scratch["noise%d" % section] = pltpu.VMEM((noise_rows, cols, channels), jnp.bfloat16)
    names = tuple(operands) + tuple(outputs) + tuple(scratch)
    steps = [own + 2 * STEPS * (sections - s) - 2 * (k + 1) for s in group for k in range(STEPS)]
    flops = 2 * sum(steps) * cols * taps * channels
    return pl.pallas_call(
        functools.partial(cascade_kernel, group, height, names),
        out_shape=list(outputs.values()),
        in_specs=[spec for _, spec in operands.values()],
        out_specs=[pl.BlockSpec(memory_space=pltpu.VMEM)] * len(outputs),
        scratch_shapes=list(scratch.values()),
        cost_estimate=pl.CostEstimate(
            flops=2 * flops, bytes_accessed=2 * sections * taps * channels, transcendentals=0
        ),
        compiler_params=pltpu.CompilerParams(vmem_limit_bytes=24 * MIB),
    )(*[value for value, _ in operands.values()])


def body(
    latents, noise, timesteps, text, text_weight, time_weight, film_weight, conv_weight, norm_gain
):
    sections = lax.axis_size("segment")
    count = lax.axis_size("row")
    own, cols, channels = latents.shape[1:]
    height = own * count
    taps = 9 * channels
    half = taps // 2

    vmem = pl.BlockSpec(memory_space=pltpu.VMEM)
    smem = pl.BlockSpec(memory_space=pltpu.SMEM)
    hbm = pl.BlockSpec(memory_space=pltpu.HBM)

    swap_cores = [(i, i ^ 1) for i in range(count)]
    chips = {d: [(i, (i + (2 * d, -2 * d)[i % 2]) % count) for i in range(count)] for d in (1, 2)}

    def turned(value, k):
        return lax.ppermute(value, "segment", [(i, (i + k) % sections) for i in range(sections)])

    conv = conv_weight.reshape(taps, channels)
    film = film_weight[0]
    strip = jax.ShapeDtypeStruct((own, cols, channels), jnp.bfloat16)
    cut = (half + channels) // 2 // 16 * 16
    pay_shapes = [
        jax.ShapeDtypeStruct((rows, channels), jnp.bfloat16)
        for rows in (cut, half - cut + channels + GAIN_ROWS)
    ]
    more_shapes = [
        jax.ShapeDtypeStruct((value.shape[0] + own * cols, channels), jnp.bfloat16)
        for value in pay_shapes
    ]
    x, pay0, pay1, more0, more1, noise_far = pl.pallas_call(
        prepare_kernel,
        out_shape=[strip, *pay_shapes, *more_shapes, strip],
        in_specs=[hbm] * 4 + [vmem],
        out_specs=[vmem] * 6,
        scratch_shapes=[pltpu.SemaphoreType.DMA((12,))],
        compiler_params=pltpu.CompilerParams(vmem_limit_bytes=57 * MIB),
    )(latents, noise[0], conv, film, norm_gain)
    got = {1: [turned(pay0, 1), None], 3: [None, turned(pay1, 3)]}
    got[1][1] = turned(more1, 1)
    got[3][0] = turned(more0, 3)
    noise_far = turned(noise_far, 2)
    x_core = lax.ppermute(x, "row", swap_cores)
    both = jnp.concatenate([x, x_core])
    near = lax.ppermute(both, "row", chips[1])
    far = lax.ppermute(both, "row", chips[2])
    back = lax.ppermute(jnp.concatenate([near, far[own:]]), "row", swap_cores)

    parts, tpart = pl.pallas_call(
        condition_kernel,
        out_shape=[
            jax.ShapeDtypeStruct((count, 1, channels), jnp.float32),
            jax.ShapeDtypeStruct((sections * STEPS, channels), jnp.float32),
        ],
        in_specs=[smem, vmem, vmem, vmem, hbm],
        out_specs=[vmem, vmem],
        compiler_params=pltpu.CompilerParams(vmem_limit_bytes=4 * MIB),
    )(timesteps, text, text_weight, time_weight, x_core)
    parts = lax.all_to_all(parts, "row", split_axis=0, concat_axis=0, tiled=True)

    firsts = (got[1][0], got[3][1])
    got[1][0], got[3][1] = pl.pallas_call(
        after_kernel,
        out_shape=[jax.ShapeDtypeStruct(v.shape, v.dtype) for v in firsts],
        in_specs=[hbm] * 3,
        out_specs=[hbm] * 2,
        input_output_aliases={0: 0, 1: 1},
        compiler_params=pltpu.CompilerParams(vmem_limit_bytes=MIB),
    )(*firsts, parts)
    got[2] = [turned(got[1][0], 1), turned(got[3][1], 3)]

    n = pl.pallas_call(
        choose_kernel,
        out_shape=jax.ShapeDtypeStruct((3 * own, cols, channels), jnp.bfloat16),
        in_specs=[hbm] * 5,
        out_specs=vmem,
        scratch_shapes=[pltpu.SemaphoreType.DMA((3, 2))],
        compiler_params=pltpu.CompilerParams(vmem_limit_bytes=4 * MIB),
    )(noise[0], got[1][1], noise_far, got[3][0], got[1][0])
    n_core = lax.ppermute(n, "row", swap_cores)
    n_near = lax.ppermute(jnp.concatenate([n[: 2 * own], n_core]), "row", chips[1])
    n_far = lax.ppermute(n_core[:own], "row", chips[2])
    n_back = lax.ppermute(
        jnp.concatenate([n_near[:own], n_near[2 * own : 4 * own]]), "row", swap_cores
    )
    swap = {k: [lax.ppermute(value, "row", swap_cores) for value in got[k]] for k in (1, 3, 2)}

    shared = {
        "times": (timesteps, smem),
        "parts": (parts, vmem),
        "tpart": (tpart, vmem),
        "gain": (norm_gain, vmem),
        "conv": (conv, hbm),
        "film": (film, hbm),
    }
    for k in (1, 2, 3):
        for i in range(2):
            shared["got%d_%d" % (k, i)] = (got[k][i], hbm)
            shared["swap%d_%d" % (k, i)] = (swap[k][i], hbm)
    values = {"latents": latents, "x_core": x_core, "near": near, "far": far, "back": back}
    first = dict(shared, **{key: (value, hbm) for key, value in values.items()})
    shape = (taps, channels, cols, own, sections, height)
    (before,) = cascade((0,), first, jnp.float32, *shape)
    values = {"n": n, "n_core": n_core, "n_near": n_near, "n_far": n_far, "n_back": n_back}
    values.update({"noise": noise[0], "noise_far": noise_far})
    second = dict(shared, **{key: (value, hbm) for key, value in values.items()})
    second["before"] = (before, vmem)
    (x,) = cascade(tuple(range(1, sections)), second, jnp.bfloat16, *shape)
    return x[None]


def solution(mesh):
    in_specs = (
        P(None, "row", None, None),
        P("segment", None, "row", None, None),
        P(),
        P("segment", None, "row"),
        P("row", None),
        P(),
        P("segment", None, None),
        P("segment", None, None, None, None),
        P("segment", None),
    )
    out_specs = P("segment", "row", None, None)
    return jax.shard_map(body, mesh=mesh, in_specs=in_specs, out_specs=out_specs, check_vma=False)
```

time: 393 us -> 94.2 us (0.24)
  blocking collectives: 136 us -> 21.7 us
  starting transfers between devices: 122 us -> 19.8 us
  waiting for transfers between devices: 58.7 us -> 17.3 us
  Pallas kernels: 0 us -> 34.4 us
  other arithmetic: 25.8 us -> 0.13 us
  matrix products: 25.5 us -> 0 us
  between operations: 13.5 us -> 0.45 us
  local copies, waits for them, and re-layouts: 6.84 us -> 0.35 us
    psum x1 -> x0, blocking collectives: 128 us -> none  [body(): summed = lax.psum(partial_pool, 'row')]
    ppermute x35 -> x21, starting transfers between devices: 122 us -> 19.8 us  [the longest x7 6.89 us: turned(): lax.ppermute(value, 'segment', [(i, (i + k) % sections) for i in range(se...]
    pallas_call x0 -> x6, Pallas kernels: none -> 34.4 us  [the longest x2 29.2 us: cascade(): pl.pallas_call(functools.partial(cascade_kernel, group, height, names), o...]
    reduce_scatter x1 -> x0, waiting for transfers between devices: 32.1 us -> none  [body(): lax.psum_scatter(collected, 'segment', scatter_dimension=0, tiled=True)]
    dot_general x129 -> x0, matrix products: 25.5 us -> none  [the longest x126 23.4 us: convolve(): term = jnp.dot(piece, kernel[dy, dx], preferred_element_type=jnp.float32)]
    all_to_all x0 -> x1, blocking collectives: none -> 21.7 us  [body(): lax.all_to_all(parts, 'row', split_axis=0, concat_axis=0, tiled=True)]
    dynamic_update_slice x7 -> x0, other arithmetic: 11.7 us -> none  [tick(): lax.dynamic_update_index_in_dim(collected, jnp.where(keeping, result, pre...]
    reduce_sum x15 -> x0, other arithmetic: 9.36 us -> none  [the longest x14 8.53 us: normalize(): jnp.mean(values * values, axis=-1, keepdims=True) + 1e-06]
  transfers between devices with their start and end apart: 36 -> 21, of which waited for: 22 -> 6; matrix products, arithmetic and copies ran while one was open for 1% -> 0% of each run, Pallas kernels for 0% -> 11%
where the time goes in v2:
time: 94.2 us; the launch traced here: 94 us
  Pallas kernels  34.4 us (37%)
  blocking collectives  21.7 us (23%)
  starting transfers between devices  19.8 us (21%)
  waiting for transfers between devices  17.3 us (18%)
    pallas_call x2, Pallas kernels, cascade(): pl.pallas_call(functools.partial(cascade_kernel, group, height, names), o...  29.2 us
    all_to_all x1, blocking collectives, body(): lax.all_to_all(parts, 'row', split_axis=0, concat_axis=0, tiled=True)  21.7 us
    ppermute x1, waiting for transfers between devices, body(): near = lax.ppermute(both, 'row', chips[1])  10.2 us
    ppermute x7, starting transfers between devices, turned(): lax.ppermute(value, 'segment', [(i, (i + k) % sections) for i in range(se...  6.89 us
    pallas_call x1, Pallas kernels, body(): pl.pallas_call(prepare_kernel, out_shape=[strip, *pay_shapes, *more_shape...  3.64 us
    ppermute x1, waiting for transfers between devices, body(): far = lax.ppermute(both, 'row', chips[2])  3.59 us
    ppermute x6, starting transfers between devices, body(): lax.ppermute(value, 'row', swap_cores)  3.48 us
    ppermute x1, starting transfers between devices, body(): x_core = lax.ppermute(x, 'row', swap_cores)  3.41 us
  transfers between devices with their start and end apart: 21, of which 6 were waited for; matrix products, arithmetic and copies ran while one was open for 0% of the time, Pallas kernels for 11%

profile of v2, /device:TPU:1, one launch (start us, length us, event | category | flops | bytes accessed | tf_op | source)
XLA Modules:
  0.0 94.0 jit_solution(15766702709631490930)
XLA Ops:
  0.0 3.6 %shard_map.91 = (bf16[2,128,256]{2,1,0:T(8,128)(2,1)}, bf16[704,256]{1,0:T(8,128)(2,1)}, bf16[720,256]{1,0:T(8,128)(2,1)}, bf16[960,256]{1,0:T(8,128)(2,1)}, bf1...) custom-call(bf16[4,2,128,256]{3,2,1,0:T(8,128)(2,1)} %refs_18_.1, bf16[4,2,128,256]{3,2,1,0:T(8,128)(2,1)} %bitcast.4, ...), custom_call_target="tpu_custom_call" | custom-call | tf_op jit(solution)/shard_map/pallas_call | solution.py:391
  3.7 2.2 %collective-permute-start.4 = (bf16[976,256]{1,0:T(8,128)(2,1)}, bf16[976,256]{1,0:T(8,128)(2,1)S(1)}, u32[]{:S(2)}, u32[]{:S(2)}) collective-permute-start(bf16[976,256]{1,0:T(8,128)(2,1)} %get-tuple-element.21), channel_id=1, source_target_pairs={{0,64},{64,128},{128,192},{192,0},{1,65},{65,129},{129,193},{193,1... | collective-permute-start | bytes 1499144 | tf_op jit(solution)/shard_map/ppermute | solution.py:377
  5.9 1.5 %collective-permute-start.10 = (bf16[960,256]{1,0:T(8,128)(2,1)}, bf16[960,256]{1,0:T(8,128)(2,1)S(1)}, u32[]{:S(2)}, u32[]{:S(2)}) collective-permute-start(bf16[960,256]{1,0:T(8,128)(2,1)} %get-tuple-element.23), channel_id=1, source_target_pairs={{0,192},{64,0},{128,64},{192,128},{1,193},{65,1},{129,65},{193,129... | collective-permute-start | bytes 1474568 | tf_op jit(solution)/shard_map/ppermute | solution.py:377
  7.4 1.4 %collective-permute-start.2 = (bf16[720,256]{1,0:T(8,128)(2,1)}, bf16[720,256]{1,0:T(8,128)(2,1)S(1)}, u32[]{:S(2)}, u32[]{:S(2)}) collective-permute-start(bf16[720,256]{1,0:T(8,128)(2,1)} %get-tuple-element.19), channel_id=1, source_target_pairs={{0,192},{64,0},{128,64},{192,128},{1,193},{65,1},{129,65},{193,129... | collective-permute-start | bytes 1105928 | tf_op jit(solution)/shard_map/ppermute | solution.py:377
  8.8 0.1 collective-permute-start.1
  8.9 3.4 %collective-permute-start = (bf16[2,128,256]{2,1,0:T(8,128)(2,1)}, bf16[2,128,256]{2,1,0:T(8,128)(2,1)S(1)}, u32[]{:S(2)}, u32[]{:S(2)}) collective-permute-start(bf16[2,128,256]{2,1,0:T(8,128)(2,1)} %get-tuple-element.15), channel_id=1, source_target_pairs={{0,1},{1,0},{2,3},{3,2},{4,5},{5,4},{6,7},{7,6},{8,9},{9,8},{10,11... | collective-permute-start | bytes 393224 | tf_op jit(solution)/shard_map/ppermute | solution.py:403
  12.3 1.2 %collective-permute-done.x_core.refs_19_ = bf16[2,128,256]{2,1,0:T(8,128)(2,1)S(1)} collective-permute-done((bf16[2,128,256]{2,1,0:T(8,128)(2,1)}, bf16[2,128,256]{2,1,0:T(8,128)(2,1)S(1)}, u32[]{:S(2)}, u32[]{:S(2)}) %collective-permute-start) | collective-permute-done | bytes 131104 | tf_op jit(solution)/shard_map/ppermute | solution.py:403
  13.5 0.0 collective-permute-start.13
  13.5 0.1 copy.15.times.refs_0_
  13.6 0.1 copy.13.text
  13.7 0.0 copy-start.7
  13.7 0.8 shard_map.92
  14.6 21.7 %all_to_all.5.parts.refs_1_ = f32[64,1,256]{2,1,0:T(1,128)S(1)} all-to-all(f32[64,1,256]{2,1,0:T(1,128)S(1)} %get-tuple-element.16), channel_id=1, replica_groups=mesh['segment'=4,'row'=64] {'row'}, dimensions={0} | all-to-all | bytes 131072 | tf_op jit(solution)/shard_map/all_to_all | solution.py:419
  36.2 0.0 collective-permute-done.1.first
  36.2 0.0 collective-permute-done.2.second
  36.3 0.0 collective-permute-done.13.noise2.refs_24_
  36.3 0.0 collective-permute-done.10.more0.refs_14_
  36.3 0.0 collective-permute-done.4.more1.refs_8_
  36.3 0.7 shard_map.94.refs_18_
  37.0 0.5 collective-permute-start.14
  37.5 3.2 %collective-permute-start.19 = (bf16[4,128,256]{2,1,0:T(8,128)(2,1)S(1)}, bf16[4,128,256]{2,1,0:T(8,128)(2,1)S(1)}, u32[]{:S(2)}, u32[]{:S(2)}) collective-permute-start(bf16[4,128,256]{2,1,0:T(8,128)(2,1)S(1)} %constant_dynamic-update-slice_fusion), channel_id=1, source_target_pairs={{0,4},{1,61},{2,6},{3,63},{4,8},{5,1},{6,10},{7,3},{8,12},{9,5},{1... | collective-permute-start | bytes 786440 | tf_op jit(solution)/shard_map/ppermute | solution.py:406
  40.7 0.0 copy-start.1
  40.7 0.0 copy-start.2
  40.7 0.0 copy-start.3
  40.7 0.0 copy-start.6
  40.8 0.1 pad_maximum_fusion
  40.8 0.8 collective-permute-start.15
  41.6 0.7 collective-permute-start.18
  42.4 0.9 collective-permute-start.6
  43.2 3.6 %collective-permute-done.19.refs_21_ = bf16[4,128,256]{2,1,0:T(8,128)(2,1)S(1)} collective-permute-done((bf16[4,128,256]{2,1,0:T(8,128)(2,1)S(1)}, bf16[4,128,256]{2,1,0:T(8,128)(2,1)S(1)}, u32[]{:S(2)}, u32[]{:S(2)}) %collective-permute-start.19) | collective-permute-done | bytes 262176 | tf_op jit(solution)/shard_map/ppermute | solution.py:406
  46.8 0.8 collective-permute-start.8
  47.7 10.2 %collective-permute-done.18.refs_20_ = bf16[4,128,256]{2,1,0:T(8,128)(2,1)S(1)} collective-permute-done((bf16[4,128,256]{2,1,0:T(8,128)(2,1)S(1)}, bf16[4,128,256]{2,1,0:T(8,128)(2,1)S(1)}, u32[]{:S(2)}, u32[]{:S(2)}) %collective-permute-start.18) | collective-permute-done | bytes 262176 | tf_op jit(solution)/shard_map/ppermute | solution.py:405
  57.8 2.4 %collective-permute-start.12 = (bf16[720,256]{1,0:T(8,128)(2,1)S(1)}, bf16[720,256]{1,0:T(8,128)(2,1)S(1)}, u32[]{:S(2)}, u32[]{:S(2)}) collective-permute-start(bf16[720,256]{1,0:T(8,128)(2,1)S(1)} %get-tuple-element.22.refs_16_), channel_id=1, source_target_pairs={{0,1},{1,0},{2,3},{3,2},{4,5},{5,4},{6,7},{7,6},{8,9},{9,8},{10,11... | collective-permute-start | bytes 1105928 | tf_op jit(solution)/shard_map/ppermute | solution.py:446
  60.2 0.1 collective-permute-start.11
  60.3 0.0 collective-permute-done.3.refs_7_
  60.4 0.5 collective-permute-start.5
  60.9 0.0 collective-permute-done.8.refs_12_
  60.9 0.4 collective-permute-start.20
  61.3 0.3 collective-permute-done.12.refs_17_
  61.5 0.4 collective-permute-start.9
  61.9 0.0 collective-permute-done.15.refs_20_
  61.9 0.1 collective-permute-start.7
  62.2 1.4 %collective-permute-done.20.refs_22_ = bf16[6,128,256]{2,1,0:T(8,128)(2,1)S(1)} collective-permute-done((bf16[6,128,256]{2,1,0:T(8,128)(2,1)S(1)}, bf16[6,128,256]{2,1,0:T(8,128)(2,1)S(1)}, u32[]{:S(2)}, u32[]{:S(2)}) %collective-permute-start.20) | collective-permute-done | bytes 393248 | tf_op jit(solution)/shard_map/ppermute | solution.py:407
  63.5 0.4 collective-permute-start.17
  63.9 0.7 collective-permute-done.7.refs_11_
  64.6 9.3 %shard_map.95.refs_25_ = f32[14,128,256]{2,1,0:T(8,128)S(1)} custom-call(s32[4,4,2]{2,1,0:T(4,128)S(1)} %copy.15.times.refs_0_, f32[64,1,256]{2,1,0:T(1,128)S(1)} %all_to_all.5.parts.refs_1_, f32[8,256]{1,0:T(8,128)S(1)} %get-tuple-element.17.refs_2_, f32[1,256]{1,0:T(1,128)S(1)} %copy-done.6, bf16[2304,256]{1,0:T(8,128)(2,1)S(1)} %bitcast.8, ...), custom_call_target="tpu_custom_call" | custom-call | flops 9059696640 | bytes 4718592 | tf_op jit(solution)/shard_map/pallas_call | solution.py:346
  73.8 0.0 collective-permute-done.16.refs_21_
  73.9 20.0 %shard_map.96 = bf16[2,128,256]{2,1,0:T(8,128)(2,1)} custom-call(s32[4,4,2]{2,1,0:T(4,128)S(1)} %copy.15.times.refs_0_, f32[64,1,256]{2,1,0:T(1,128)S(1)} %all_to_all.5.parts.refs_1_, f32[8,256]{1,0:T(8,128)S(1)} %get-tuple-element.17.refs_2_, f32[1,256]{1,0:T(1,128)S(1)} %copy-done.6, bf16[2304,256]{1,0:T(8,128)(2,1)S(1)} %bitcast.9, ...), custom_call_target="tpu_custom_call" | custom-call | flops 12683575296 | bytes 4718592 | tf_op jit(solution)/shard_map/pallas_call | solution.py:346
  (33 shorter events, 0.2 us)
Async XLA Ops:
  0.0 13.5 %copy-start.9 = (s32[4,4,2]{1,2,0:T(2,128)S(1)}, s32[4,4,2]{1,2,0:T(2,128)}, u32[]{:S(2)}) copy-start(s32[4,4,2]{1,2,0:T(2,128)} %param.11) | copy-start | bytes 388
  0.0 13.6 %copy-start.8 = (bf16[1,77,64]{1,2,0:T(8,128)(2,1)S(1)}, bf16[1,77,64]{1,2,0:T(8,128)(2,1)}, u32[]{:S(2)}) copy-start(bf16[1,77,64]{1,2,0:T(8,128)(2,1)} %param.12) | copy-start | bytes 29572
  0.0 13.7 %copy-start.5 = (bf16[64,256]{1,0:T(8,128)(2,1)S(1)}, bf16[64,256]{1,0:T(8,128)(2,1)}, u32[]{:S(2)}) copy-start(bf16[64,256]{1,0:T(8,128)(2,1)} %text_weight.1) | copy-start | bytes 98308
  0.0 13.7 %copy-start.4 = (bf16[256,256]{1,0:T(8,128)(2,1)S(1)}, bf16[256,256]{1,0:T(8,128)(2,1)}, u32[]{:S(2)}) copy-start(bf16[256,256]{1,0:T(8,128)(2,1)} %time_weight.1) | copy-start | bytes 393220
  0.0 36.3 %copy-start = (bf16[1,4,2,128,256]{4,3,2,1,0:T(8,128)(2,1)S(1)}, bf16[1,4,2,128,256]{4,3,2,1,0:T(8,128)(2,1)}, u32[]{:S(2)}) copy-start(bf16[1,4,2,128,256]{4,3,2,1,0:T(8,128)(2,1)} %param.10) | copy-start | bytes 1572868
  3.7 32.6 %collective-permute-start.4 = (bf16[976,256]{1,0:T(8,128)(2,1)}, bf16[976,256]{1,0:T(8,128)(2,1)S(1)}, u32[]{:S(2)}, u32[]{:S(2)}) collective-permute-start(bf16[976,256]{1,0:T(8,128)(2,1)} %get-tuple-element.21), channel_id=1, source_target_pairs={{0,64},{64,128},{128,192},{192,0},{1,65},{65,129},{129,193},{193,1... | collective-permute-start | bytes 1499144 | tf_op jit(solution)/shard_map/ppermute | solution.py:377
  5.9 30.4 %collective-permute-start.10 = (bf16[960,256]{1,0:T(8,128)(2,1)}, bf16[960,256]{1,0:T(8,128)(2,1)S(1)}, u32[]{:S(2)}, u32[]{:S(2)}) collective-permute-start(bf16[960,256]{1,0:T(8,128)(2,1)} %get-tuple-element.23), channel_id=1, source_target_pairs={{0,192},{64,0},{128,64},{192,128},{1,193},{65,1},{129,65},{193,129... | collective-permute-start | bytes 1474568 | tf_op jit(solution)/shard_map/ppermute | solution.py:377
  7.4 28.8 %collective-permute-start.2 = (bf16[720,256]{1,0:T(8,128)(2,1)}, bf16[720,256]{1,0:T(8,128)(2,1)S(1)}, u32[]{:S(2)}, u32[]{:S(2)}) collective-permute-start(bf16[720,256]{1,0:T(8,128)(2,1)} %get-tuple-element.19), channel_id=1, source_target_pairs={{0,192},{64,0},{128,64},{192,128},{1,193},{65,1},{129,65},{193,129... | collective-permute-start | bytes 1105928 | tf_op jit(solution)/shard_map/ppermute | solution.py:377
  8.8 27.5 %collective-permute-start.1 = (bf16[704,256]{1,0:T(8,128)(2,1)}, bf16[704,256]{1,0:T(8,128)(2,1)S(1)}, u32[]{:S(2)}, u32[]{:S(2)}) collective-permute-start(bf16[704,256]{1,0:T(8,128)(2,1)} %get-tuple-element.18), channel_id=1, source_target_pairs={{0,64},{64,128},{128,192},{192,0},{1,65},{65,129},{129,193},{193,1... | collective-permute-start | bytes 1081352 | tf_op jit(solution)/shard_map/ppermute | solution.py:377
  8.9 4.6 %collective-permute-start = (bf16[2,128,256]{2,1,0:T(8,128)(2,1)}, bf16[2,128,256]{2,1,0:T(8,128)(2,1)S(1)}, u32[]{:S(2)}, u32[]{:S(2)}) collective-permute-start(bf16[2,128,256]{2,1,0:T(8,128)(2,1)} %get-tuple-element.15), channel_id=1, source_target_pairs={{0,1},{1,0},{2,3},{3,2},{4,5},{5,4},{6,7},{7,6},{8,9},{9,8},{10,11... | collective-permute-start | bytes 393224 | tf_op jit(solution)/shard_map/ppermute | solution.py:403
  13.5 22.8 %collective-permute-start.13 = (bf16[2,128,256]{2,1,0:T(8,128)(2,1)}, bf16[2,128,256]{2,1,0:T(8,128)(2,1)S(1)}, u32[]{:S(2)}, u32[]{:S(2)}) collective-permute-start(bf16[2,128,256]{2,1,0:T(8,128)(2,1)} %get-tuple-element.24), channel_id=1, source_target_pairs={{0,128},{64,192},{128,0},{192,64},{1,129},{65,193},{129,1},{193,65... | collective-permute-start | bytes 393224 | tf_op jit(solution)/shard_map/ppermute | solution.py:377
  13.7 23.7 %copy-start.7 = (bf16[2,128,256]{2,1,0:T(8,128)(2,1)S(1)}, bf16[2,128,256]{2,1,0:T(8,128)(2,1)}, u32[]{:S(2)}) copy-start(bf16[2,128,256]{2,1,0:T(8,128)(2,1)} %get-tuple-element.15) | copy-start | bytes 393220
  37.0 3.8 %collective-permute-start.14 = (bf16[6,128,256]{2,1,0:T(8,128)(2,1)S(1)}, bf16[6,128,256]{2,1,0:T(8,128)(2,1)S(1)}, u32[]{:S(2)}, u32[]{:S(2)}) collective-permute-start(bf16[6,128,256]{2,1,0:T(8,128)(2,1)S(1)} %shard_map.94.refs_18_), channel_id=1, source_target_pairs={{0,1},{1,0},{2,3},{3,2},{4,5},{5,4},{6,7},{7,6},{8,9},{9,8},{10,11... | collective-permute-start | bytes 1179656 | tf_op jit(solution)/shard_map/ppermute | solution.py:440
  37.5 9.3 %collective-permute-start.19 = (bf16[4,128,256]{2,1,0:T(8,128)(2,1)S(1)}, bf16[4,128,256]{2,1,0:T(8,128)(2,1)S(1)}, u32[]{:S(2)}, u32[]{:S(2)}) collective-permute-start(bf16[4,128,256]{2,1,0:T(8,128)(2,1)S(1)} %constant_dynamic-update-slice_fusion), channel_id=1, source_target_pairs={{0,4},{1,61},{2,6},{3,63},{4,8},{5,1},{6,10},{7,3},{8,12},{9,5},{1... | collective-permute-start | bytes 786440 | tf_op jit(solution)/shard_map/ppermute | solution.py:406
  40.7 23.9 %copy-start.1 = (bf16[1,3,3,256,256]{4,3,2,1,0:T(8,128)(2,1)S(1)}, bf16[1,3,3,256,256]{4,3,2,1,0:T(8,128)(2,1)}, u32[]{:S(2)}) copy-start(bf16[1,3,3,256,256]{4,3,2,1,0:T(8,128)(2,1)} %param.16) | copy-start | bytes 3538948
  40.7 23.9 %copy-start.2 = (bf16[4,2,128,256]{3,2,1,0:T(8,128)(2,1)S(1)}, bf16[4,2,128,256]{3,2,1,0:T(8,128)(2,1)}, u32[]{:S(2)}) copy-start(bf16[4,2,128,256]{3,2,1,0:T(8,128)(2,1)} %refs_18_.1) | copy-start | bytes 1572868
  40.7 23.8 %copy-start.3 = (bf16[1,256,512]{2,1,0:T(8,128)(2,1)S(1)}, bf16[1,256,512]{2,1,0:T(8,128)(2,1)}, u32[]{:S(2)}) copy-start(bf16[1,256,512]{2,1,0:T(8,128)(2,1)} %param.15) | copy-start | bytes 786436
  40.7 23.8 %copy-start.6 = (f32[1,256]{1,0:T(1,128)S(1)}, f32[1,256]{1,0:T(1,128)}, u32[]{:S(2)}) copy-start(f32[1,256]{1,0:T(1,128)} %refs_3_.3) | copy-start | bytes 3076
  40.8 21.1 %collective-permute-start.15 = (bf16[10,128,256]{2,1,0:T(8,128)(2,1)S(1)}, bf16[10,128,256]{2,1,0:T(8,128)(2,1)S(1)}, u32[]{:S(2)}, u32[]{:S(2)}) collective-permute-start(bf16[10,128,256]{2,1,0:T(8,128)(2,1)S(1)} %pad_maximum_fusion), channel_id=1, source_target_pairs={{0,2},{1,63},{2,4},{3,1},{4,6},{5,3},{6,8},{7,5},{8,10},{9,7},{10,... | collective-permute-start | bytes 1966088 | tf_op jit(solution)/shard_map/ppermute | solution.py:441
  41.6 16.2 %collective-permute-start.18 = (bf16[4,128,256]{2,1,0:T(8,128)(2,1)S(1)}, bf16[4,128,256]{2,1,0:T(8,128)(2,1)S(1)}, u32[]{:S(2)}, u32[]{:S(2)}) collective-permute-start(bf16[4,128,256]{2,1,0:T(8,128)(2,1)S(1)} %constant_dynamic-update-slice_fusion), channel_id=1, source_target_pairs={{0,2},{1,63},{2,4},{3,1},{4,6},{5,3},{6,8},{7,5},{8,10},{9,7},{10,... | collective-permute-start | bytes 786440 | tf_op jit(solution)/shard_map/ppermute | solution.py:405
  42.4 17.9 %collective-permute-start.6 = (bf16[704,256]{1,0:T(8,128)(2,1)S(1)}, bf16[704,256]{1,0:T(8,128)(2,1)S(1)}, u32[]{:S(2)}, u32[]{:S(2)}) collective-permute-start(bf16[704,256]{1,0:T(8,128)(2,1)S(1)} %get-tuple-element.20.first.refs_6_), channel_id=1, source_target_pairs={{0,64},{64,128},{128,192},{192,0},{1,65},{65,129},{129,193},{193,1... | collective-permute-start | bytes 1081352 | tf_op jit(solution)/shard_map/ppermute | solution.py:377
  43.2 17.1 %collective-permute-start.3 = (bf16[704,256]{1,0:T(8,128)(2,1)S(1)}, bf16[704,256]{1,0:T(8,128)(2,1)S(1)}, u32[]{:S(2)}, u32[]{:S(2)}) collective-permute-start(bf16[704,256]{1,0:T(8,128)(2,1)S(1)} %get-tuple-element.20.first.refs_6_), channel_id=1, source_target_pairs={{0,1},{1,0},{2,3},{3,2},{4,5},{5,4},{6,7},{7,6},{8,9},{9,8},{10,11... | collective-permute-start | bytes 1081352 | tf_op jit(solution)/shard_map/ppermute | solution.py:446
  46.8 14.1 %collective-permute-start.8 = (bf16[720,256]{1,0:T(8,128)(2,1)S(1)}, bf16[720,256]{1,0:T(8,128)(2,1)S(1)}, u32[]{:S(2)}, u32[]{:S(2)}) collective-permute-start(bf16[720,256]{1,0:T(8,128)(2,1)S(1)} %get-tuple-element.22.refs_16_), channel_id=1, source_target_pairs={{0,192},{64,0},{128,64},{192,128},{1,193},{65,1},{129,65},{193,129... | collective-permute-start | bytes 1105928 | tf_op jit(solution)/shard_map/ppermute | solution.py:377
  57.8 3.7 %collective-permute-start.12 = (bf16[720,256]{1,0:T(8,128)(2,1)S(1)}, bf16[720,256]{1,0:T(8,128)(2,1)S(1)}, u32[]{:S(2)}, u32[]{:S(2)}) collective-permute-start(bf16[720,256]{1,0:T(8,128)(2,1)S(1)} %get-tuple-element.22.refs_16_), channel_id=1, source_target_pairs={{0,1},{1,0},{2,3},{3,2},{4,5},{5,4},{6,7},{7,6},{8,9},{9,8},{10,11... | collective-permute-start | bytes 1105928 | tf_op jit(solution)/shard_map/ppermute | solution.py:446
  60.2 3.3 %collective-permute-start.11 = (bf16[960,256]{1,0:T(8,128)(2,1)S(1)}, bf16[960,256]{1,0:T(8,128)(2,1)S(1)}, u32[]{:S(2)}, u32[]{:S(2)}) collective-permute-start(bf16[960,256]{1,0:T(8,128)(2,1)S(1)} %collective-permute-done.10.more0.refs_14_), channel_id=1, source_target_pairs={{0,1},{1,0},{2,3},{3,2},{4,5},{5,4},{6,7},{7,6},{8,9},{9,8},{10,11... | collective-permute-start | bytes 1474568 | tf_op jit(solution)/shard_map/ppermute | solution.py:446
  60.4 3.5 %collective-permute-start.5 = (bf16[976,256]{1,0:T(8,128)(2,1)S(1)}, bf16[976,256]{1,0:T(8,128)(2,1)S(1)}, u32[]{:S(2)}, u32[]{:S(2)}) collective-permute-start(bf16[976,256]{1,0:T(8,128)(2,1)S(1)} %collective-permute-done.4.more1.refs_8_), channel_id=1, source_target_pairs={{0,1},{1,0},{2,3},{3,2},{4,5},{5,4},{6,7},{7,6},{8,9},{9,8},{10,11... | collective-permute-start | bytes 1499144 | tf_op jit(solution)/shard_map/ppermute | solution.py:446
  60.9 2.6 %collective-permute-start.20 = (bf16[6,128,256]{2,1,0:T(8,128)(2,1)S(1)}, bf16[6,128,256]{2,1,0:T(8,128)(2,1)S(1)}, u32[]{:S(2)}, u32[]{:S(2)}) collective-permute-start(bf16[6,128,256]{2,1,0:T(8,128)(2,1)S(1)} %pad_maximum_fusion.2), channel_id=1, source_target_pairs={{0,1},{1,0},{2,3},{3,2},{4,5},{5,4},{6,7},{7,6},{8,9},{9,8},{10,11... | collective-permute-start | bytes 1179656 | tf_op jit(solution)/shard_map/ppermute | solution.py:407
  61.5 3.0 %collective-permute-start.9 = (bf16[720,256]{1,0:T(8,128)(2,1)S(1)}, bf16[720,256]{1,0:T(8,128)(2,1)S(1)}, u32[]{:S(2)}, u32[]{:S(2)}) collective-permute-start(bf16[720,256]{1,0:T(8,128)(2,1)S(1)} %collective-permute-done.8.refs_12_), channel_id=1, source_target_pairs={{0,1},{1,0},{2,3},{3,2},{4,5},{5,4},{6,7},{7,6},{8,9},{9,8},{10,11... | collective-permute-start | bytes 1105928 | tf_op jit(solution)/shard_map/ppermute | solution.py:446
  61.9 2.6 %collective-permute-start.7 = (bf16[704,256]{1,0:T(8,128)(2,1)S(1)}, bf16[704,256]{1,0:T(8,128)(2,1)S(1)}, u32[]{:S(2)}, u32[]{:S(2)}) collective-permute-start(bf16[704,256]{1,0:T(8,128)(2,1)S(1)} %collective-permute-done.6.refs_10_), channel_id=1, source_target_pairs={{0,1},{1,0},{2,3},{3,2},{4,5},{5,4},{6,7},{7,6},{8,9},{9,8},{10,11... | collective-permute-start | bytes 1081352 | tf_op jit(solution)/shard_map/ppermute | solution.py:446
  63.5 10.3 %collective-permute-start.16 = (bf16[2,128,256]{2,1,0:T(8,128)(2,1)S(1)}, bf16[2,128,256]{2,1,0:T(8,128)(2,1)S(1)}, u32[]{:S(2)}, u32[]{:S(2)}) collective-permute-start(bf16[2,128,256]{2,1,0:T(8,128)(2,1)S(1)} %slice.21), channel_id=1, source_target_pairs={{0,4},{1,61},{2,6},{3,63},{4,8},{5,1},{6,10},{7,3},{8,12},{9,5},{1... | collective-permute-start | bytes 393224 | tf_op jit(solution)/shard_map/ppermute | solution.py:442
  63.5 10.3 %collective-permute-start.17 = (bf16[6,128,256]{2,1,0:T(8,128)(2,1)S(1)}, bf16[6,128,256]{2,1,0:T(8,128)(2,1)S(1)}, u32[]{:S(2)}, u32[]{:S(2)}) collective-permute-start(bf16[6,128,256]{2,1,0:T(8,128)(2,1)S(1)} %pad_maximum_fusion.1), channel_id=1, source_target_pairs={{0,1},{1,0},{2,3},{3,2},{4,5},{5,4},{6,7},{7,6},{8,9},{9,8},{10,11... | collective-permute-start | bytes 1179656 | tf_op jit(solution)/shard_map/ppermute | solution.py:443

commit v3 on v2

v3 whole, which is shorter than its diff:
```python
import functools
import math

import jax
import jax.numpy as jnp
from jax import lax
from jax.experimental import pallas as pl
from jax.experimental.pallas import tpu as pltpu
from jax.sharding import PartitionSpec as P

STEPS = 2
GAIN_ROWS = 16
MIB = 1024 * 1024


def place_of_device():
    row = lax.axis_index("row")
    return lax.axis_index("segment"), row, lax.rem(row, 2)


def prepare_kernel(latents, noise, conv, film, gain, x_out, pay1, pay2, pay3, sems):
    segment, _, core = place_of_device()
    half = conv.shape[0] // 2
    channels = conv.shape[1]
    cols = latents.shape[2]
    pays = (pay1, pay2, pay3)
    here = pl.ds(pl.multiple_of(core * half, half), half)
    pairs = [(latents.at[segment], x_out)]
    for k, target in enumerate(pays):
        pairs.append((conv.at[here], target.at[pl.ds(0, half)]))
        for i in range(2):
            source = noise.at[lax.rem(segment + k + 1, 4), i]
            at = half + channels + GAIN_ROWS + i * cols
            pairs.append((source, target.at[pl.ds(at, cols)]))
    copies = [pltpu.make_async_copy(a, b, sems.at[i]) for i, (a, b) in enumerate(pairs)]
    film_at = pl.ds(half, channels)
    sides = [
        [
            pltpu.make_async_copy(
                film.at[:, i * channels : (i + 1) * channels], target.at[film_at], sems.at[10 + j]
            )
            for j, target in enumerate(pays)
        ]
        for i in range(2)
    ]
    for copy in copies:
        copy.start()
    for i in range(2):

        @pl.when(core == i)
        def _(i=i):
            for copy in sides[i]:
                copy.start()

    exact = gain[...]
    top = exact.astype(jnp.bfloat16).astype(jnp.float32)
    middle = (exact - top).astype(jnp.bfloat16).astype(jnp.float32)
    low = exact - top - middle
    line = lax.broadcasted_iota(jnp.int32, (GAIN_ROWS, channels), 0)
    rows = jnp.where(line == 0, top, jnp.where(line == 1, middle, jnp.where(line == 2, low, 0.0)))
    for target in pays:
        target[pl.ds(half + channels, GAIN_ROWS), :] = rows.astype(jnp.bfloat16)
    for copy in copies:
        copy.wait()
    for i in range(2):

        @pl.when(core == i)
        def _(i=i):
            for copy in sides[i]:
                copy.wait()


def condition_kernel(times, text, text_weight, time_weight, back, parts_out, tpart_out):
    segment, _, _ = place_of_device()
    tokens = text.shape[1]
    channels = time_weight.shape[0]
    total = jnp.sum(text[0].astype(jnp.float32), axis=0, keepdims=True)
    mean = (total / tokens).astype(jnp.bfloat16)
    part = jnp.dot(mean, text_weight[...], preferred_element_type=jnp.float32)
    parts_out[...] = jnp.broadcast_to(part[None], parts_out.shape)
    count = tpart_out.shape[0]
    half = channels // 2
    line = lax.broadcasted_iota(jnp.int32, (count, half), 0)
    moments = jnp.zeros((count, half), jnp.float32)
    for i in range(count):
        now = times[segment, i // STEPS, i % STEPS].astype(jnp.float32)
        moments = jnp.where(line == i, now, moments)
    place = lax.broadcasted_iota(jnp.int32, (count, half), 1).astype(jnp.float32)
    angles = moments * jnp.exp(-math.log(10000.0) * place / half)
    embed = jnp.concatenate([jnp.cos(angles), jnp.sin(angles)], axis=-1).astype(jnp.bfloat16)
    value = jnp.dot(embed, time_weight[...], preferred_element_type=jnp.float32)
    tpart_out[...] = value * (0.5 + 0.5 * jnp.tanh(0.5 * value))


def choose_kernel(noise, got1, got2, got3, parts, n_out, sems):
    segment, _, _ = place_of_device()
    sections = 4
    cols = n_out.shape[1]
    for act in ("start", "wait"):
        for section in range(sections - 1):
            behind = lax.rem(segment - section + sections, sections)
            for j in range(sections):

                @pl.when(behind == j)
                def _(j=j, section=section):
                    for i in range(2):
                        source = noise_row(j, i, cols, noise.at[segment], got1, got2, got3)
                        target = n_out.at[2 * section + i]
                        copy = pltpu.make_async_copy(source, target, sems.at[section, i])
                        getattr(copy, act)()


def noise_row(j, i, cols, own, *got):
    if j == 0:
        return own.at[i]
    source = got[j - 1]
    return source.at[pl.ds(source.shape[0] - (2 - i) * cols, cols)]


def return_kernel(near, far, before, out):
    out[0:2] = near[0:2]
    out[2:6] = near[4:8]


def cascade_kernel(sections, height, names, *refs):
    r = dict(zip(names, refs))
    segment, row, core = place_of_device()
    conv_buf, film_buf, gain_buf, sems = (r["conv_buf"], r["film_buf"], r["gain_buf"], r["sems"])
    lhs, mid, xs = r["lhs"], r["mid"], r["xs"]
    taps, channels = conv_buf.shape[1:]
    cols = xs.shape[1]
    half = taps // 2
    own = 2
    total_sections = r["tpart"].shape[0] // STEPS
    behind = [lax.rem(segment - section + 4, 4) for section in sections]


    def copies(slot, j):
        weights, films, gains = conv_buf.at[slot], film_buf.at[slot], gain_buf.at[slot]
        if j == 0:
            pairs = [
                (r["conv"], weights),
                (r["film"].at[:, :channels], films.at[0]),
                (r["film"].at[:, channels:], films.at[1]),
            ]
        else:
            pairs = []
            for key, side in (("got", core), ("swap", 1 - core)):
                source = r["%s%d" % (key, j)]
                at = pl.multiple_of(side * half, half)
                pairs.append((source.at[pl.ds(0, half)], weights.at[pl.ds(at, half)]))
                pairs.append((source.at[pl.ds(half, channels)], films.at[side]))
            pairs.append((r["got%d" % j].at[pl.ds(half + channels, GAIN_ROWS)], gains))
        if sections[slot] == total_sections - 1:
            for i in range(2):
                got = (r["got%d" % k] for k in (1, 2, 3))
                source = noise_row(j, i, cols, r["noise"].at[segment], *got)
                pairs.append((source, r["noise3"].at[i]))
        return [pltpu.make_async_copy(a, b, sems.at[slot, i]) for i, (a, b) in enumerate(pairs)]

    def each(slot, act):
        for j in range(4):

            @pl.when(behind[slot] == j)
            def _(j=j):
                for copy in copies(slot, j):
                    act(copy)

    strips = {}
    if sections[0] == 0:
        near, far, back = (r["near"], r["far"], r["back"])
        strips["xs"] = [
            (r["latents"].at[segment], 8, 8),
            (r["x_core"], 10, 6),
            (near.at[0:2], 4, 12),
            (near.at[2:4], 6, 10),
            (far.at[0:2], 0, 16),
            (far.at[2:4], 2, 14),
            (back.at[0:2], 14, 2),
            (back.at[2:4], 12, 4),
            (back.at[4:6], 16, 0),
        ]
    else:
        (n, n_core, n_near, n_far, n_back) = (
            r[key] for key in ("n", "n_core", "n_near", "n_far", "n_back")
        )
        strips["noise0"] = [
            (n.at[0:2], 6, 6),
            (n_core.at[0:2], 8, 4),
            (n_near.at[0:2], 2, 10),
            (n_near.at[4:6], 4, 8),
            (n_far, 0, 12),
            (n_back.at[0:2], 12, 0),
            (n_back.at[2:4], 10, 2),
        ]
        strips["noise1"] = [
            (n.at[2:4], 4, 4),
            (n_core.at[2:4], 6, 2),
            (n_near.at[2:4], 0, 8),
            (n_near.at[6:8], 2, 6),
            (n_back.at[4:6], 8, 0),
        ]
        strips["noise2"] = [(n.at[4:6], 2, 2), (n_core.at[4:6], 4, 0), (n_near.at[8:10], 0, 4)]
    moves = {}
    for key, placed in strips.items():
        moves[key] = []
        for i, (value, first, second) in enumerate(placed):
            target = r[key].at[pl.ds(first + core * (second - first), 2)]
            moves[key].append(pltpu.make_async_copy(value, target, r["strip_sems"].at[len(moves), i]))

    first = next(iter(strips))
    for copy in moves[first]:
        copy.start()
    for slot in range(len(sections)):
        each(slot, lambda copy: copy.start())
    for key in moves:
        if key != first:
            for copy in moves[key]:
                copy.start()
    for copy in moves[first]:
        copy.wait()

    def sigma(section):
        moment = r["times"][segment, section, STEPS - 1].astype(jnp.float32)
        return jnp.full((1, channels), moment, jnp.float32) / 1000.0

    source = xs
    if sections[0] > 0:
        sigma0 = sigma(0)
        for i in range(xs.shape[0]):
            noisy = r["before"][i] + sigma0 * r["noise0"][i].astype(jnp.float32)
            xs[i] = noisy.astype(jnp.bfloat16)

    pooled = jnp.sum(r["parts"][...], axis=0)
    place = lax.broadcasted_iota(jnp.int32, (cols, channels), 0)
    for slot, section in enumerate(sections):
        each(slot, lambda copy: copy.wait())
        gains = gain_buf[slot].astype(jnp.float32)
        gain = gains[0:1] + gains[1:2] + gains[2:3]
        gain = jnp.where(behind[slot] == 0, r["gain"][...], gain)
        cond = (pooled + r["tpart"][STEPS * section : STEPS * (section + 1)]).astype(jnp.bfloat16)
        scales = 1.0 + jnp.dot(cond, film_buf[slot, 0], preferred_element_type=jnp.float32)
        shifts = jnp.dot(cond, film_buf[slot, 1], preferred_element_type=jnp.float32)
        for step in range(STEPS):
            left_over = (total_sections - section) * STEPS - step
            count = own + 2 * left_over
            for i in range(count):
                values = source[i].astype(jnp.float32)
                inv = lax.rsqrt(jnp.mean(values * values, axis=-1, keepdims=True) + 1e-06)
                normed = values * inv * gain
                if i < left_over or i >= left_over + own:
                    image_row = row * own - left_over + i
                    inside = (image_row >= 0) & (image_row < height)
                    normed = jnp.where(inside, normed, 0.0)
                at = pl.ds(i * cols, cols)
                left = jnp.where(place == 0, 0.0, pltpu.roll(normed, 1, 0))
                right = jnp.where(place == cols - 1, 0.0, pltpu.roll(normed, cols - 1, 0))
                lhs[at, 0:channels] = left.astype(jnp.bfloat16)
                lhs[at, channels : 2 * channels] = normed.astype(jnp.bfloat16)
                lhs[at, 2 * channels :] = right.astype(jnp.bfloat16)
            last = step == STEPS - 1
            noised = last and section > 0
            if noised and section < total_sections - 1:
                for copy in moves["noise%d" % section]:
                    copy.wait()
            if not last:
                target = mid
            elif slot == len(sections) - 1:
                target = r["out"]
            else:
                target = xs
            for i in range(count - 2):
                window = jnp.concatenate(
                    [lhs[pl.ds((i + dy) * cols, cols), :] for dy in range(3)], axis=1
                )
                total = jnp.dot(window, conv_buf[slot], preferred_element_type=jnp.float32)
                moved = total * scales[step : step + 1] + shifts[step : step + 1]
                branch = moved * (0.5 + 0.5 * jnp.tanh(0.5 * moved))
                after = source[i + 1].astype(jnp.float32) + branch
                if noised:
                    fresh = r["noise%d" % section][i].astype(jnp.float32)
                    after = after + sigma(section) * fresh
                target[i] = after.astype(target.dtype)
            source = target


def cascade(group, operands, dtype, taps, channels, cols, own, sections, height):
    slots = len(group)
    rows = own + 2 * STEPS * (sections - group[0])
    out_rows = own + 2 * STEPS * (sections - 1 - group[-1])
    scratch = {
        "conv_buf": pltpu.VMEM((slots, taps, channels), jnp.bfloat16),
        "film_buf": pltpu.VMEM((slots, 2, channels, channels), jnp.bfloat16),
        "gain_buf": pltpu.VMEM((slots, GAIN_ROWS, channels), jnp.bfloat16),
        "xs": pltpu.VMEM((rows, cols, channels), jnp.bfloat16),
        "mid": pltpu.VMEM((rows, cols, channels), jnp.bfloat16),
        "lhs": pltpu.VMEM((rows * cols, 3 * channels), jnp.bfloat16),
        "sems": pltpu.SemaphoreType.DMA((slots, 9)),
        "strip_sems": pltpu.SemaphoreType.DMA((4, 9)),
    }
    if group[0] > 0:
        for section in range(sections):
            noise_rows = own + 2 * STEPS * (sections - 1 - section)
            scratch["noise%d" % section] = pltpu.VMEM((noise_rows, cols, channels), jnp.bfloat16)
    names = tuple(operands) + ("out",) + tuple(scratch)
    steps = [own + 2 * STEPS * (sections - s) - 2 * (k + 1) for s in group for k in range(STEPS)]
    flops = 2 * sum(steps) * cols * taps * channels
    return pl.pallas_call(
        functools.partial(cascade_kernel, group, height, names),
        out_shape=jax.ShapeDtypeStruct((out_rows, cols, channels), dtype),
        in_specs=[spec for _, spec in operands.values()],
        out_specs=pl.BlockSpec(memory_space=pltpu.VMEM),
        scratch_shapes=list(scratch.values()),
        cost_estimate=pl.CostEstimate(
            flops=flops, bytes_accessed=2 * slots * taps * channels, transcendentals=0
        ),
        compiler_params=pltpu.CompilerParams(vmem_limit_bytes=24 * MIB),
    )(*[value for value, _ in operands.values()])


def body(
    latents, noise, timesteps, text, text_weight, time_weight, film_weight, conv_weight, norm_gain
):
    sections = lax.axis_size("segment")
    count = lax.axis_size("row")
    own, cols, channels = latents.shape[1:]
    height = own * count
    taps = 9 * channels
    half = taps // 2

    vmem = pl.BlockSpec(memory_space=pltpu.VMEM)
    smem = pl.BlockSpec(memory_space=pltpu.SMEM)
    hbm = pl.BlockSpec(memory_space=pltpu.HBM)

    swap_cores = [(i, i ^ 1) for i in range(count)]
    chips = {d: [(i, (i + (2 * d, -2 * d)[i % 2]) % count) for i in range(count)] for d in (1, 2)}

    def turned(value, k):
        return lax.ppermute(value, "segment", [(i, (i + k) % sections) for i in range(sections)])

    conv = conv_weight.reshape(taps, channels)
    film = film_weight[0]
    strip = jax.ShapeDtypeStruct((own, cols, channels), jnp.bfloat16)
    pay_rows = half + channels + GAIN_ROWS + own * cols
    pay_shape = jax.ShapeDtypeStruct((pay_rows, channels), jnp.bfloat16)
    x, *pays = pl.pallas_call(
        prepare_kernel,
        out_shape=[strip, pay_shape, pay_shape, pay_shape],
        in_specs=[hbm] * 4 + [vmem],
        out_specs=[vmem] * 4,
        scratch_shapes=[pltpu.SemaphoreType.DMA((13,))],
        compiler_params=pltpu.CompilerParams(vmem_limit_bytes=57 * MIB),
    )(latents, noise[0], conv, film, norm_gain)
    got = {k: turned(pays[k - 1], k) for k in (1, 3, 2)}

    x_core = lax.ppermute(x, "row", swap_cores)
    both = jnp.concatenate([x, x_core])
    near = lax.ppermute(both, "row", chips[1])
    far = lax.ppermute(both, "row", chips[2])
    back = lax.ppermute(jnp.concatenate([near, far[own:]]), "row", swap_cores)

    parts, tpart = pl.pallas_call(
        condition_kernel,
        out_shape=[
            jax.ShapeDtypeStruct((count, 1, channels), jnp.float32),
            jax.ShapeDtypeStruct((sections * STEPS, channels), jnp.float32),
        ],
        in_specs=[smem, vmem, vmem, vmem, hbm],
        out_specs=[vmem, vmem],
        compiler_params=pltpu.CompilerParams(vmem_limit_bytes=4 * MIB),
    )(timesteps, text, text_weight, time_weight, back)
    parts = lax.all_to_all(parts, "row", split_axis=0, concat_axis=0, tiled=True)

    n = pl.pallas_call(
        choose_kernel,
        out_shape=jax.ShapeDtypeStruct((3 * own, cols, channels), jnp.bfloat16),
        in_specs=[hbm] * 5,
        out_specs=vmem,
        scratch_shapes=[pltpu.SemaphoreType.DMA((3, 2))],
        compiler_params=pltpu.CompilerParams(vmem_limit_bytes=4 * MIB),
    )(noise[0], got[1], got[2], got[3], parts)
    n_core = lax.ppermute(n, "row", swap_cores)
    n_near = lax.ppermute(jnp.concatenate([n[: 2 * own], n_core]), "row", chips[1])
    n_far = lax.ppermute(n_core[:own], "row", chips[2])
    swap = {k: lax.ppermute(got[k], "row", swap_cores) for k in (1, 3, 2)}

    shared = {
        "times": (timesteps, smem),
        "parts": (parts, vmem),
        "tpart": (tpart, vmem),
        "gain": (norm_gain, vmem),
        "conv": (conv, hbm),
        "film": (film, hbm),
    }
    for k in (1, 2, 3):
        shared["got%d" % k] = (got[k], hbm)
        shared["swap%d" % k] = (swap[k], hbm)
    values = {"latents": latents, "x_core": x_core, "near": near, "far": far, "back": back}
    first = dict(shared, **{key: (value, hbm) for key, value in values.items()})
    before = cascade((0,), first, jnp.float32, taps, channels, cols, own, sections, height)
    n_some = pl.pallas_call(
        return_kernel,
        out_shape=jax.ShapeDtypeStruct((3 * own, cols, channels), jnp.bfloat16),
        in_specs=[vmem, hbm, hbm],
        out_specs=vmem,
        compiler_params=pltpu.CompilerParams(vmem_limit_bytes=4 * MIB),
    )(n_near, n_far, before)
    n_back = lax.ppermute(n_some, "row", swap_cores)
    values = {"n": n, "n_core": n_core, "n_near": n_near, "n_far": n_far, "n_back": n_back}
    values.update({"noise": noise[0]})
    second = dict(shared, **{key: (value, hbm) for key, value in values.items()})
    second["before"] = (before, vmem)
    later = tuple(range(1, sections))
    x = cascade(later, second, jnp.bfloat16, taps, channels, cols, own, sections, height)
    return x[None]


def solution(mesh):
    in_specs = (
        P(None, "row", None, None),
        P("segment", None, "row", None, None),
        P(),
        P("segment", None, "row"),
        P("row", None),
        P(),
        P("segment", None, None),
        P("segment", None, None, None, None),
        P("segment", None),
    )
    out_specs = P("segment", "row", None, None)
    return jax.shard_map(body, mesh=mesh, in_specs=in_specs, out_specs=out_specs, check_vma=False)
```

time: 94.2 us -> 90.7 us (0.963)
  blocking collectives: 21.7 us -> 0 us
  starting transfers between devices: 19.8 us -> 37.5 us
  local copies, waits for them, and re-layouts: 0.35 us -> 4.91 us
  Pallas kernels: 34.4 us -> 30 us
    all_to_all x1 -> x0, blocking collectives: 21.7 us -> none  [body(): lax.all_to_all(parts, 'row', split_axis=0, concat_axis=0, tiled=True)]
    ppermute x1, waiting for transfers between devices: 10.2 us -> 2.1 us  [body(): near = lax.ppermute(both, 'row', chips[1])]
    all_to_all x0 -> x1, starting transfers between devices: none -> 7.68 us  [body(): lax.all_to_all(parts, 'row', split_axis=0, concat_axis=0, tiled=True)]
    ppermute x1, starting transfers between devices: 3.21 us -> 8.29 us  [body(): far = lax.ppermute(both, 'row', chips[2])]
    pallas_call x2, Pallas kernels: 29.2 us -> 24.3 us  [cascade(): pl.pallas_call(functools.partial(cascade_kernel, group, height, names), o...]
    all_to_all x0 -> x1, waiting for transfers between devices: none -> 4.75 us  [body(): lax.all_to_all(parts, 'row', split_axis=0, concat_axis=0, tiled=True)]
    unnamed x23 -> x35, local copies, waits for them, and re-layouts: 0.28 us -> 4.86 us
    ppermute x7 -> x3, starting transfers between devices: 6.89 us -> 3.25 us  [turned(): lax.ppermute(value, 'segment', [(i, (i + k) % sections) for i in range(se...]
  transfers between devices with their start and end apart: 21 -> 15, of which waited for: 6 -> 7; matrix products, arithmetic and copies ran while one was open for 0% -> 2% of each run, Pallas kernels for 11% -> 11%
where the time goes in v3:
time: 90.7 us; the launch traced here: 90.3 us
  starting transfers between devices  37.5 us (41%)
  Pallas kernels  30 us (33%)
  waiting for transfers between devices  16.7 us (18%)
  local copies, waits for them, and re-layouts  4.91 us (5%)
    pallas_call x2, Pallas kernels, cascade(): pl.pallas_call(functools.partial(cascade_kernel, group, height, names), o...  24.3 us
    ppermute x1, starting transfers between devices, body(): far = lax.ppermute(both, 'row', chips[2])  8.29 us
    all_to_all x1, starting transfers between devices, body(): lax.all_to_all(parts, 'row', split_axis=0, concat_axis=0, tiled=True)  7.68 us
    ppermute x1, waiting for transfers between devices, body(): far = lax.ppermute(both, 'row', chips[2])  5.4 us
    ppermute x3, starting transfers between devices, body(): swap = {k: lax.ppermute(got[k], 'row', swap_cores) for k in (1, 3, 2)}  4.91 us
    unnamed x35, local copies, waits for them, and re-layouts  4.86 us
    all_to_all x1, waiting for transfers between devices, body(): lax.all_to_all(parts, 'row', split_axis=0, concat_axis=0, tiled=True)  4.75 us
    pallas_call x1, Pallas kernels, body(): pl.pallas_call(prepare_kernel, out_shape=[strip, pay_shape, pay_shape, pa...  4.21 us
  transfers between devices with their start and end apart: 15, of which 7 were waited for; matrix products, arithmetic and copies ran while one was open for 2% of the time, Pallas kernels for 11%

profile of v3, /device:TPU:1, one launch (start us, length us, event | category | flops | bytes accessed | tf_op | source)
XLA Modules:
  0.0 90.3 jit_solution(7350128039469792575)
XLA Ops:
  0.0 4.2 %shard_map.91 = (bf16[2,128,256]{2,1,0:T(8,128)(2,1)}, bf16[1680,256]{1,0:T(8,128)(2,1)}, bf16[1680,256]{1,0:T(8,128)(2,1)}, bf16[1680,256]{1,0:T(8,128)(2,1)}) custom-call(bf16[4,2,128,256]{3,2,1,0:T(8,128)(2,1)} %refs_12_.1, bf16[4,2,128,256]{3,2,1,0:T(8,128)(2,1)} %bitcast.4, bf16[2304,256]{1,0:T(8,128)(2,1)} %bitcast.7, bf16[256,512]{1,0:T(8,128)(2,1)} %bitcast.10, ...), custom_call_target="tpu_custom_call" | custom-call | tf_op jit(solution)/shard_map/pallas_call | solution.py:346
  4.2 3.5 %collective-permute-start = (bf16[2,128,256]{2,1,0:T(8,128)(2,1)}, bf16[2,128,256]{2,1,0:T(8,128)(2,1)S(1)}, u32[]{:S(2)}, u32[]{:S(2)}) collective-permute-start(bf16[2,128,256]{2,1,0:T(8,128)(2,1)} %get-tuple-element.11), channel_id=1, source_target_pairs={{0,1},{1,0},{2,3},{3,2},{4,5},{5,4},{6,7},{7,6},{8,9},{9,8},{10,11... | collective-permute-start | bytes 393224 | tf_op jit(solution)/shard_map/ppermute | solution.py:356
  7.7 0.0 collective-permute-start.4
  7.7 2.2 %collective-permute-start.6 = (bf16[1680,256]{1,0:T(8,128)(2,1)}, bf16[1680,256]{1,0:T(8,128)(2,1)S(1)}, u32[]{:S(2)}, u32[]{:S(2)}) collective-permute-start(bf16[1680,256]{1,0:T(8,128)(2,1)} %get-tuple-element.15), channel_id=1, source_target_pairs={{0,128},{64,192},{128,0},{192,64},{1,129},{65,193},{129,1},{193,65... | collective-permute-start | bytes 2580488 | tf_op jit(solution)/shard_map/ppermute | solution.py:339
  9.9 1.0 %collective-permute-start.8 = (bf16[1680,256]{1,0:T(8,128)(2,1)}, bf16[1680,256]{1,0:T(8,128)(2,1)S(1)}, u32[]{:S(2)}, u32[]{:S(2)}) collective-permute-start(bf16[1680,256]{1,0:T(8,128)(2,1)} %get-tuple-element.16), channel_id=1, source_target_pairs={{0,192},{64,0},{128,64},{192,128},{1,193},{65,1},{129,65},{193,129... | collective-permute-start | bytes 2580488 | tf_op jit(solution)/shard_map/ppermute | solution.py:339
  10.9 0.9 %constant_dynamic-update-slice_fusion.1 = bf16[4,128,256]{2,1,0:T(8,128)(2,1)S(1)} fusion(bf16[2,128,256]{2,1,0:T(8,128)(2,1)} %get-tuple-element.11), kind=kLoop, calls=%fused_computation.3 | loop fusion | bytes 262144
  11.9 0.0 copy-start.6
  11.9 8.3 %collective-permute-start.2 = (bf16[4,128,256]{2,1,0:T(8,128)(2,1)S(1)}, bf16[4,128,256]{2,1,0:T(8,128)(2,1)S(1)}, u32[]{:S(2)}, u32[]{:S(2)}) collective-permute-start(bf16[4,128,256]{2,1,0:T(8,128)(2,1)S(1)} %constant_dynamic-update-slice_fusion), channel_id=1, source_target_pairs={{0,4},{1,61},{2,6},{3,63},{4,8},{5,1},{6,10},{7,3},{8,12},{9,5},{1... | collective-permute-start | bytes 786440 | tf_op jit(solution)/shard_map/ppermute | solution.py:359
  20.2 0.7 collective-permute-start.1
  20.9 5.4 %collective-permute-done.2.refs_15_ = bf16[4,128,256]{2,1,0:T(8,128)(2,1)S(1)} collective-permute-done((bf16[4,128,256]{2,1,0:T(8,128)(2,1)S(1)}, bf16[4,128,256]{2,1,0:T(8,128)(2,1)S(1)}, u32[]{:S(2)}, u32[]{:S(2)}) %collective-permute-start.2) | collective-permute-done | bytes 262176 | tf_op jit(solution)/shard_map/ppermute | solution.py:359
  26.3 0.7 copy-done.9
  27.0 2.1 %collective-permute-done.1.refs_14_ = bf16[4,128,256]{2,1,0:T(8,128)(2,1)S(1)} collective-permute-done((bf16[4,128,256]{2,1,0:T(8,128)(2,1)S(1)}, bf16[4,128,256]{2,1,0:T(8,128)(2,1)S(1)}, u32[]{:S(2)}, u32[]{:S(2)}) %collective-permute-start.1) | collective-permute-done | bytes 262176 | tf_op jit(solution)/shard_map/ppermute | solution.py:358
  29.1 0.8 pad_maximum_fusion.1
  29.9 0.7 copy-done.4
  30.6 1.8 %collective-permute-start.3 = (bf16[6,128,256]{2,1,0:T(8,128)(2,1)}, bf16[6,128,256]{2,1,0:T(8,128)(2,1)S(1)}, u32[]{:S(2)}, u32[]{:S(2)}) collective-permute-start(bf16[6,128,256]{2,1,0:T(8,128)(2,1)} %pad_maximum_fusion.1), channel_id=1, source_target_pairs={{0,1},{1,0},{2,3},{3,2},{4,5},{5,4},{6,7},{7,6},{8,9},{9,8},{10,11... | collective-permute-start | bytes 1179656 | tf_op jit(solution)/shard_map/ppermute | solution.py:360
  32.4 0.1 copy.13.times.refs_0_
  32.5 0.1 copy.11.text
  32.6 1.3 %collective-permute-done.3.back.refs_16_ = bf16[6,128,256]{2,1,0:T(8,128)(2,1)S(1)} collective-permute-done((bf16[6,128,256]{2,1,0:T(8,128)(2,1)}, bf16[6,128,256]{2,1,0:T(8,128)(2,1)S(1)}, u32[]{:S(2)}, u32[]{:S(2)}) %collective-permute-start.3) | collective-permute-done | bytes 393248 | tf_op jit(solution)/shard_map/ppermute | solution.py:360
  33.9 0.9 copy-done.8
  34.8 0.8 copy-done.12
  35.6 0.8 shard_map.92
  36.5 0.6 copy-done.11
  37.1 7.7 %all-to-all-start = ((f32[64,1,256]{2,1,0:T(1,128)}), f32[64,1,256]{2,1,0:T(1,128)}, u32[]{:S(2)}, u32[]{:S(2)}) async-start(f32[64,1,256]{2,1,0:T(1,128)} %copy-done.11), calls=%async_computation | async-start | bytes 131072 | tf_op jit(solution)/shard_map/all_to_all | solution.py:372
  44.8 0.0 collective-permute-done.4.got1.refs_6_
  44.8 4.3 %collective-permute-start.5 = (bf16[1680,256]{1,0:T(8,128)(2,1)S(1)}, bf16[1680,256]{1,0:T(8,128)(2,1)}, u32[]{:S(2)}, u32[]{:S(2)}) collective-permute-start(bf16[1680,256]{1,0:T(8,128)(2,1)S(1)} %collective-permute-done.4.got1.refs_6_), channel_id=1, source_target_pairs={{0,1},{1,0},{2,3},{3,2},{4,5},{5,4},{6,7},{7,6},{8,9},{9,8},{10,11... | collective-permute-start | bytes 2580488 | tf_op jit(solution)/shard_map/ppermute | solution.py:385
  49.1 0.0 collective-permute-start.7
  49.1 0.0 collective-permute-done.8.got3.refs_10_
  49.1 0.6 collective-permute-start.9
  49.7 4.7 %all-to-all-done.parts.refs_1_ = f32[64,1,256]{2,1,0:T(1,128)} async-done(((f32[64,1,256]{2,1,0:T(1,128)}), f32[64,1,256]{2,1,0:T(1,128)}, u32[]{:S(2)}, u32[]{:S(2)}) %all-to-all-start) | async-done | bytes 65568 | tf_op jit(solution)/shard_map/all_to_all | solution.py:372
  54.5 0.6 shard_map.93.refs_12_
  55.1 0.0 copy-start.1
  55.1 0.0 copy-start.2
  55.1 0.0 copy-start.3
  55.1 0.0 copy-start.7
  55.2 0.0 copy-start.13
  55.2 0.5 collective-permute-start.10
  55.7 1.3 %collective-permute-done.10.refs_13_ = bf16[6,128,256]{2,1,0:T(8,128)(2,1)S(1)} collective-permute-done((bf16[6,128,256]{2,1,0:T(8,128)(2,1)S(1)}, bf16[6,128,256]{2,1,0:T(8,128)(2,1)S(1)}, u32[]{:S(2)}, u32[]{:S(2)}) %collective-permute-start.10) | collective-permute-done | bytes 393248 | tf_op jit(solution)/shard_map/ppermute | solution.py:382
  57.0 0.1 pad_maximum_fusion
  57.1 3.3 %collective-permute-start.11 = (bf16[10,128,256]{2,1,0:T(8,128)(2,1)S(1)}, bf16[10,128,256]{2,1,0:T(8,128)(2,1)S(1)}, u32[]{:S(2)}, u32[]{:S(2)}) collective-permute-start(bf16[10,128,256]{2,1,0:T(8,128)(2,1)S(1)} %pad_maximum_fusion), channel_id=1, source_target_pairs={{0,2},{1,63},{2,4},{3,1},{4,6},{5,3},{6,8},{7,5},{8,10},{9,7},{10,... | collective-permute-start | bytes 1966088 | tf_op jit(solution)/shard_map/ppermute | solution.py:383
  60.3 1.2 %collective-permute-start.12 = (bf16[2,128,256]{2,1,0:T(8,128)(2,1)S(1)}, bf16[2,128,256]{2,1,0:T(8,128)(2,1)S(1)}, u32[]{:S(2)}, u32[]{:S(2)}) collective-permute-start(bf16[2,128,256]{2,1,0:T(8,128)(2,1)S(1)} %slice.14), channel_id=1, source_target_pairs={{0,4},{1,61},{2,6},{3,63},{4,8},{5,1},{6,10},{7,3},{8,12},{9,5},{1... | collective-permute-start | bytes 393224 | tf_op jit(solution)/shard_map/ppermute | solution.py:384
  61.6 0.0 collective-permute-done.7.refs_9_
  61.6 0.0 collective-permute-done.9.refs_11_
  61.7 8.6 %shard_map.94.before.refs_18_ = f32[14,128,256]{2,1,0:T(8,128)S(1)} custom-call(s32[4,4,2]{2,1,0:T(4,128)S(1)} %copy.13.times.refs_0_, f32[64,1,256]{2,1,0:T(1,128)} %all-to-all-done.parts.refs_1_, f32[8,256]{1,0:T(8,128)S(1)} %get-tuple-element.13.refs_2_, f32[1,256]{1,0:T(1,128)S(1)} %copy-done.13, bf16[2304,256]{1,0:T(8,128)(2,1)S(1)} %bitcast.8, ...), custom_call_target="tpu_custom_call" | custom-call | flops 4529848320 | bytes 1179648 | tf_op jit(solution)/shard_map/pallas_call | solution.py:308
  70.2 0.4 collective-permute-done.12.far.refs_15_
  70.7 0.0 collective-permute-done.11.near.refs_14_
  70.7 2.4 %collective-permute-start.13 = (bf16[6,128,256]{2,1,0:T(8,128)(2,1)S(1)}, bf16[6,128,256]{2,1,0:T(8,128)(2,1)S(1)}, u32[]{:S(2)}, u32[]{:S(2)}) collective-permute-start(bf16[6,128,256]{2,1,0:T(8,128)(2,1)S(1)} %shard_map.95), channel_id=1, source_target_pairs={{0,1},{1,0},{2,3},{3,2},{4,5},{5,4},{6,7},{7,6},{8,9},{9,8},{10,11... | collective-permute-start | bytes 1179656 | tf_op jit(solution)/shard_map/ppermute | solution.py:408
  73.1 1.3 %collective-permute-done.13.refs_16_ = bf16[6,128,256]{2,1,0:T(8,128)(2,1)S(1)} collective-permute-done((bf16[6,128,256]{2,1,0:T(8,128)(2,1)S(1)}, bf16[6,128,256]{2,1,0:T(8,128)(2,1)S(1)}, u32[]{:S(2)}, u32[]{:S(2)}) %collective-permute-start.13) | collective-permute-done | bytes 393248 | tf_op jit(solution)/shard_map/ppermute | solution.py:408
  74.4 15.7 %shard_map.96 = bf16[2,128,256]{2,1,0:T(8,128)(2,1)} custom-call(s32[4,4,2]{2,1,0:T(4,128)S(1)} %copy.13.times.refs_0_, f32[64,1,256]{2,1,0:T(1,128)} %all-to-all-done.parts.refs_1_, f32[8,256]{1,0:T(8,128)S(1)} %get-tuple-element.13.refs_2_, f32[1,256]{1,0:T(1,128)S(1)} %copy-done.13, bf16[2304,256]{1,0:T(8,128)(2,1)S(1)} %bitcast.9, ...), custom_call_target="tpu_custom_call" | custom-call | flops 6341787648 | bytes 3538944 | tf_op jit(solution)/shard_map/pallas_call | solution.py:308
  (29 shorter events, 0.1 us)
Async XLA Ops:
  0.0 32.4 %copy-start.15 = (s32[4,4,2]{1,2,0:T(2,128)S(1)}, s32[4,4,2]{1,2,0:T(2,128)}, u32[]{:S(2)}) copy-start(s32[4,4,2]{1,2,0:T(2,128)} %param.11) | copy-start | bytes 388
  0.0 32.5 %copy-start.14 = (bf16[1,77,64]{1,2,0:T(8,128)(2,1)S(1)}, bf16[1,77,64]{1,2,0:T(8,128)(2,1)}, u32[]{:S(2)}) copy-start(bf16[1,77,64]{1,2,0:T(8,128)(2,1)} %param.12) | copy-start | bytes 29572
  0.0 54.5 %copy-start = (bf16[1,4,2,128,256]{4,3,2,1,0:T(8,128)(2,1)S(1)}, bf16[1,4,2,128,256]{4,3,2,1,0:T(8,128)(2,1)}, u32[]{:S(2)}) copy-start(bf16[1,4,2,128,256]{4,3,2,1,0:T(8,128)(2,1)} %param.10) | copy-start | bytes 1572868
  4.2 7.6 %collective-permute-start = (bf16[2,128,256]{2,1,0:T(8,128)(2,1)}, bf16[2,128,256]{2,1,0:T(8,128)(2,1)S(1)}, u32[]{:S(2)}, u32[]{:S(2)}) collective-permute-start(bf16[2,128,256]{2,1,0:T(8,128)(2,1)} %get-tuple-element.11), channel_id=1, source_target_pairs={{0,1},{1,0},{2,3},{3,2},{4,5},{5,4},{6,7},{7,6},{8,9},{9,8},{10,11... | collective-permute-start | bytes 393224 | tf_op jit(solution)/shard_map/ppermute | solution.py:356
  7.7 37.1 %collective-permute-start.4 = (bf16[1680,256]{1,0:T(8,128)(2,1)}, bf16[1680,256]{1,0:T(8,128)(2,1)S(1)}, u32[]{:S(2)}, u32[]{:S(2)}) collective-permute-start(bf16[1680,256]{1,0:T(8,128)(2,1)} %get-tuple-element.14), channel_id=1, source_target_pairs={{0,64},{64,128},{128,192},{192,0},{1,65},{65,129},{129,193},{193,1... | collective-permute-start | bytes 2580488 | tf_op jit(solution)/shard_map/ppermute | solution.py:339
  7.7 41.4 %collective-permute-start.6 = (bf16[1680,256]{1,0:T(8,128)(2,1)}, bf16[1680,256]{1,0:T(8,128)(2,1)S(1)}, u32[]{:S(2)}, u32[]{:S(2)}) collective-permute-start(bf16[1680,256]{1,0:T(8,128)(2,1)} %get-tuple-element.15), channel_id=1, source_target_pairs={{0,128},{64,192},{128,0},{192,64},{1,129},{65,193},{129,1},{193,65... | collective-permute-start | bytes 2580488 | tf_op jit(solution)/shard_map/ppermute | solution.py:339
  9.9 39.2 %collective-permute-start.8 = (bf16[1680,256]{1,0:T(8,128)(2,1)}, bf16[1680,256]{1,0:T(8,128)(2,1)S(1)}, u32[]{:S(2)}, u32[]{:S(2)}) collective-permute-start(bf16[1680,256]{1,0:T(8,128)(2,1)} %get-tuple-element.16), channel_id=1, source_target_pairs={{0,192},{64,0},{128,64},{192,128},{1,193},{65,1},{129,65},{193,129... | collective-permute-start | bytes 2580488 | tf_op jit(solution)/shard_map/ppermute | solution.py:339
  11.9 14.5 %copy-start.6 = (bf16[2,128,256]{2,1,0:T(8,128)(2,1)}, bf16[2,128,256]{2,1,0:T(8,128)(2,1)S(1)}, u32[]{:S(2)}) copy-start(bf16[2,128,256]{2,1,0:T(8,128)(2,1)S(1)} %collective-permute-done.refs_13_) | copy-start | bytes 393220
  11.9 14.4 %collective-permute-start.2 = (bf16[4,128,256]{2,1,0:T(8,128)(2,1)S(1)}, bf16[4,128,256]{2,1,0:T(8,128)(2,1)S(1)}, u32[]{:S(2)}, u32[]{:S(2)}) collective-permute-start(bf16[4,128,256]{2,1,0:T(8,128)(2,1)S(1)} %constant_dynamic-update-slice_fusion), channel_id=1, source_target_pairs={{0,4},{1,61},{2,6},{3,63},{4,8},{5,1},{6,10},{7,3},{8,12},{9,5},{1... | collective-permute-start | bytes 786440 | tf_op jit(solution)/shard_map/ppermute | solution.py:359
  20.2 8.9 %collective-permute-start.1 = (bf16[4,128,256]{2,1,0:T(8,128)(2,1)S(1)}, bf16[4,128,256]{2,1,0:T(8,128)(2,1)S(1)}, u32[]{:S(2)}, u32[]{:S(2)}) collective-permute-start(bf16[4,128,256]{2,1,0:T(8,128)(2,1)S(1)} %constant_dynamic-update-slice_fusion), channel_id=1, source_target_pairs={{0,2},{1,63},{2,4},{3,1},{4,6},{5,3},{6,8},{7,5},{8,10},{9,7},{10,... | collective-permute-start | bytes 786440 | tf_op jit(solution)/shard_map/ppermute | solution.py:358
  26.3 0.7 copy-start.9
  29.9 0.7 copy-start.4
  30.6 3.3 %collective-permute-start.3 = (bf16[6,128,256]{2,1,0:T(8,128)(2,1)}, bf16[6,128,256]{2,1,0:T(8,128)(2,1)S(1)}, u32[]{:S(2)}, u32[]{:S(2)}) collective-permute-start(bf16[6,128,256]{2,1,0:T(8,128)(2,1)} %pad_maximum_fusion.1), channel_id=1, source_target_pairs={{0,1},{1,0},{2,3},{3,2},{4,5},{5,4},{6,7},{7,6},{8,9},{9,8},{10,11... | collective-permute-start | bytes 1179656 | tf_op jit(solution)/shard_map/ppermute | solution.py:360
  33.9 0.9 %copy-start.8 = (bf16[256,256]{1,0:T(8,128)(2,1)S(1)}, bf16[256,256]{1,0:T(8,128)(2,1)}, u32[]{:S(2)}) copy-start(bf16[256,256]{1,0:T(8,128)(2,1)} %time_weight.1) | copy-start | bytes 393220
  34.8 0.8 copy-start.12
  36.5 0.6 copy-start.11
  37.1 17.4 %all-to-all-start = ((f32[64,1,256]{2,1,0:T(1,128)}), f32[64,1,256]{2,1,0:T(1,128)}, u32[]{:S(2)}, u32[]{:S(2)}) async-start(f32[64,1,256]{2,1,0:T(1,128)} %copy-done.11), calls=%async_computation | async-start | bytes 131072 | tf_op jit(solution)/shard_map/all_to_all | solution.py:372
  44.8 16.8 %collective-permute-start.5 = (bf16[1680,256]{1,0:T(8,128)(2,1)S(1)}, bf16[1680,256]{1,0:T(8,128)(2,1)}, u32[]{:S(2)}, u32[]{:S(2)}) collective-permute-start(bf16[1680,256]{1,0:T(8,128)(2,1)S(1)} %collective-permute-done.4.got1.refs_6_), channel_id=1, source_target_pairs={{0,1},{1,0},{2,3},{3,2},{4,5},{5,4},{6,7},{7,6},{8,9},{9,8},{10,11... | collective-permute-start | bytes 2580488 | tf_op jit(solution)/shard_map/ppermute | solution.py:385
  49.1 12.5 %collective-permute-start.7 = (bf16[1680,256]{1,0:T(8,128)(2,1)S(1)}, bf16[1680,256]{1,0:T(8,128)(2,1)}, u32[]{:S(2)}, u32[]{:S(2)}) collective-permute-start(bf16[1680,256]{1,0:T(8,128)(2,1)S(1)} %collective-permute-done.6.got2.refs_8_), channel_id=1, source_target_pairs={{0,1},{1,0},{2,3},{3,2},{4,5},{5,4},{6,7},{7,6},{8,9},{9,8},{10,11... | collective-permute-start | bytes 2580488 | tf_op jit(solution)/shard_map/ppermute | solution.py:385
  49.1 12.5 %collective-permute-start.9 = (bf16[1680,256]{1,0:T(8,128)(2,1)S(1)}, bf16[1680,256]{1,0:T(8,128)(2,1)}, u32[]{:S(2)}, u32[]{:S(2)}) collective-permute-start(bf16[1680,256]{1,0:T(8,128)(2,1)S(1)} %collective-permute-done.8.got3.refs_10_), channel_id=1, source_target_pairs={{0,1},{1,0},{2,3},{3,2},{4,5},{5,4},{6,7},{7,6},{8,9},{9,8},{10,11... | collective-permute-start | bytes 2580488 | tf_op jit(solution)/shard_map/ppermute | solution.py:385
  54.5 7.1 %copy-start.5 = (bf16[4,128,256]{2,1,0:T(8,128)(2,1)S(1)}, bf16[4,128,256]{2,1,0:T(8,128)(2,1)}, u32[]{:S(2)}) copy-start(bf16[4,128,256]{2,1,0:T(8,128)(2,1)} %copy-done.4) | copy-start | bytes 786436
  54.5 7.1 %copy-start.10 = (bf16[4,128,256]{2,1,0:T(8,128)(2,1)S(1)}, bf16[4,128,256]{2,1,0:T(8,128)(2,1)}, u32[]{:S(2)}) copy-start(bf16[4,128,256]{2,1,0:T(8,128)(2,1)} %copy-done.9) | copy-start | bytes 786436
  55.1 6.5 %copy-start.1 = (bf16[1,3,3,256,256]{4,3,2,1,0:T(8,128)(2,1)S(1)}, bf16[1,3,3,256,256]{4,3,2,1,0:T(8,128)(2,1)}, u32[]{:S(2)}) copy-start(bf16[1,3,3,256,256]{4,3,2,1,0:T(8,128)(2,1)} %param.16) | copy-start | bytes 3538948
  55.1 6.5 %copy-start.2 = (bf16[4,2,128,256]{3,2,1,0:T(8,128)(2,1)S(1)}, bf16[4,2,128,256]{3,2,1,0:T(8,128)(2,1)}, u32[]{:S(2)}) copy-start(bf16[4,2,128,256]{3,2,1,0:T(8,128)(2,1)} %refs_12_.1) | copy-start | bytes 1572868
  55.1 6.5 %copy-start.3 = (bf16[1,256,512]{2,1,0:T(8,128)(2,1)S(1)}, bf16[1,256,512]{2,1,0:T(8,128)(2,1)}, u32[]{:S(2)}) copy-start(bf16[1,256,512]{2,1,0:T(8,128)(2,1)} %param.15) | copy-start | bytes 786436
  55.1 6.5 %copy-start.7 = (bf16[2,128,256]{2,1,0:T(8,128)(2,1)S(1)}, bf16[2,128,256]{2,1,0:T(8,128)(2,1)}, u32[]{:S(2)}) copy-start(bf16[2,128,256]{2,1,0:T(8,128)(2,1)} %copy-done.6) | copy-start | bytes 393220
  55.2 6.5 %copy-start.13 = (f32[1,256]{1,0:T(1,128)S(1)}, f32[1,256]{1,0:T(1,128)}, u32[]{:S(2)}) copy-start(f32[1,256]{1,0:T(1,128)} %refs_3_.3) | copy-start | bytes 3076
  55.2 1.8 %collective-permute-start.10 = (bf16[6,128,256]{2,1,0:T(8,128)(2,1)S(1)}, bf16[6,128,256]{2,1,0:T(8,128)(2,1)S(1)}, u32[]{:S(2)}, u32[]{:S(2)}) collective-permute-start(bf16[6,128,256]{2,1,0:T(8,128)(2,1)S(1)} %shard_map.93.refs_12_), channel_id=1, source_target_pairs={{0,1},{1,0},{2,3},{3,2},{4,5},{5,4},{6,7},{7,6},{8,9},{9,8},{10,11... | collective-permute-start | bytes 1179656 | tf_op jit(solution)/shard_map/ppermute | solution.py:382
  57.1 13.6 %collective-permute-start.11 = (bf16[10,128,256]{2,1,0:T(8,128)(2,1)S(1)}, bf16[10,128,256]{2,1,0:T(8,128)(2,1)S(1)}, u32[]{:S(2)}, u32[]{:S(2)}) collective-permute-start(bf16[10,128,256]{2,1,0:T(8,128)(2,1)S(1)} %pad_maximum_fusion), channel_id=1, source_target_pairs={{0,2},{1,63},{2,4},{3,1},{4,6},{5,3},{6,8},{7,5},{8,10},{9,7},{10,... | collective-permute-start | bytes 1966088 | tf_op jit(solution)/shard_map/ppermute | solution.py:383
  60.3 10.3 %collective-permute-start.12 = (bf16[2,128,256]{2,1,0:T(8,128)(2,1)S(1)}, bf16[2,128,256]{2,1,0:T(8,128)(2,1)S(1)}, u32[]{:S(2)}, u32[]{:S(2)}) collective-permute-start(bf16[2,128,256]{2,1,0:T(8,128)(2,1)S(1)} %slice.14), channel_id=1, source_target_pairs={{0,4},{1,61},{2,6},{3,63},{4,8},{5,1},{6,10},{7,3},{8,12},{9,5},{1... | collective-permute-start | bytes 393224 | tf_op jit(solution)/shard_map/ppermute | solution.py:384
  70.7 3.7 %collective-permute-start.13 = (bf16[6,128,256]{2,1,0:T(8,128)(2,1)S(1)}, bf16[6,128,256]{2,1,0:T(8,128)(2,1)S(1)}, u32[]{:S(2)}, u32[]{:S(2)}) collective-permute-start(bf16[6,128,256]{2,1,0:T(8,128)(2,1)S(1)} %shard_map.95), channel_id=1, source_target_pairs={{0,1},{1,0},{2,3},{3,2},{4,5},{5,4},{6,7},{7,6},{8,9},{9,8},{10,11... | collective-permute-start | bytes 1179656 | tf_op jit(solution)/shard_map/ppermute | solution.py:408

commit v4 on v3

--- a/solution.py
+++ b/solution.py
@@ -70,7 +70,7 @@
                 copy.wait()
 
 
-def condition_kernel(times, text, text_weight, time_weight, back, parts_out, tpart_out):
+def condition_kernel(times, text, text_weight, time_weight, near, far, parts_out, tpart_out):
     segment, _, _ = place_of_device()
     tokens = text.shape[1]
     channels = time_weight.shape[0]
@@ -365,10 +365,10 @@
             jax.ShapeDtypeStruct((count, 1, channels), jnp.float32),
             jax.ShapeDtypeStruct((sections * STEPS, channels), jnp.float32),
         ],
-        in_specs=[smem, vmem, vmem, vmem, hbm],
+        in_specs=[smem, vmem, vmem, vmem, hbm, hbm],
         out_specs=[vmem, vmem],
         compiler_params=pltpu.CompilerParams(vmem_limit_bytes=4 * MIB),
-    )(timesteps, text, text_weight, time_weight, back)
+    )(timesteps, text, text_weight, time_weight, near, far)
     parts = lax.all_to_all(parts, "row", split_axis=0, concat_axis=0, tiled=True)
 
     n = pl.pallas_call(

time: 90.7 us -> 89.7 us (0.989)
  starting transfers between devices: 37.5 us -> 36.2 us
  waiting for transfers between devices: 16.7 us -> 17.8 us
    ppermute x1, starting transfers between devices: 8.29 us -> 1.17 us  [body(): far = lax.ppermute(both, 'row', chips[2])]
    ppermute x1, starting transfers between devices: 0.73 us -> 7.77 us  [body(): near = lax.ppermute(both, 'row', chips[1])]
    ppermute x3, waiting for transfers between devices: 0.01 us -> 3.28 us  [turned(): lax.ppermute(value, 'segment', [(i, (i + k) % sections) for i in range(se...]
    ppermute x3, starting transfers between devices: 4.91 us -> 2.24 us  [body(): swap = {k: lax.ppermute(got[k], 'row', swap_cores) for k in (1, 3, 2)}]
    ppermute x3, starting transfers between devices: 3.25 us -> 5.9 us  [turned(): lax.ppermute(value, 'segment', [(i, (i + k) % sections) for i in range(se...]
    ppermute x1, starting transfers between devices: 3.46 us -> 1.62 us  [body(): x_core = lax.ppermute(x, 'row', swap_cores)]
    ppermute x1, starting transfers between devices: 3.25 us -> 4.88 us  [body(): lax.ppermute(jnp.concatenate([n[:2 * own], n_core]), 'row', chips[1])]
    ppermute x1, starting transfers between devices: 1.79 us -> 0.22 us  [body(): back = lax.ppermute(jnp.concatenate([near, far[own:]]), 'row', swap_cores)]
  transfers between devices with their start and end apart: 15 -> 15, of which waited for: 7 -> 6; matrix products, arithmetic and copies ran while one was open for 2% -> 4% of each run, Pallas kernels for 11% -> 11%
where the time goes in v4:
time: 89.7 us; the launch traced here: 89.4 us
  starting transfers between devices  36.2 us (40%)
  Pallas kernels  29.3 us (33%)
  waiting for transfers between devices  17.8 us (20%)
  local copies, waits for them, and re-layouts  5.57 us (6%)
    pallas_call x2, Pallas kernels, cascade(): pl.pallas_call(functools.partial(cascade_kernel, group, height, names), o...  23.6 us
    all_to_all x1, starting transfers between devices, body(): lax.all_to_all(parts, 'row', split_axis=0, concat_axis=0, tiled=True)  8.32 us
    ppermute x1, starting transfers between devices, body(): near = lax.ppermute(both, 'row', chips[1])  7.77 us
    ppermute x3, starting transfers between devices, turned(): lax.ppermute(value, 'segment', [(i, (i + k) % sections) for i in range(se...  5.9 us
    ppermute x1, waiting for transfers between devices, body(): far = lax.ppermute(both, 'row', chips[2])  5.06 us
    ppermute x1, starting transfers between devices, body(): lax.ppermute(jnp.concatenate([n[:2 * own], n_core]), 'row', chips[1])  4.88 us
    all_to_all x1, waiting for transfers between devices, body(): lax.all_to_all(parts, 'row', split_axis=0, concat_axis=0, tiled=True)  4.24 us
    pallas_call x1, Pallas kernels, body(): pl.pallas_call(prepare_kernel, out_shape=[strip, pay_shape, pay_shape, pa...  4.24 us
  transfers between devices with their start and end apart: 15, of which 6 were waited for; matrix products, arithmetic and copies ran while one was open for 4% of the time, Pallas kernels for 11%

profile of v4, /device:TPU:1, one launch (start us, length us, event | category | flops | bytes accessed | tf_op | source)
XLA Modules:
  0.0 89.4 jit_solution(16000694361873429353)
XLA Ops:
  0.0 4.2 %shard_map.91 = (bf16[2,128,256]{2,1,0:T(8,128)(2,1)}, bf16[1680,256]{1,0:T(8,128)(2,1)}, bf16[1680,256]{1,0:T(8,128)(2,1)}, bf16[1680,256]{1,0:T(8,128)(2,1)}) custom-call(bf16[4,2,128,256]{3,2,1,0:T(8,128)(2,1)} %refs_12_.1, bf16[4,2,128,256]{3,2,1,0:T(8,128)(2,1)} %bitcast.4, bf16[2304,256]{1,0:T(8,128)(2,1)} %bitcast.7, bf16[256,512]{1,0:T(8,128)(2,1)} %bitcast.10, ...), custom_call_target="tpu_custom_call" | custom-call | tf_op jit(solution)/shard_map/pallas_call | solution.py:346
  4.3 2.2 %collective-permute-start.3 = (bf16[1680,256]{1,0:T(8,128)(2,1)}, bf16[1680,256]{1,0:T(8,128)(2,1)S(1)}, u32[]{:S(2)}, u32[]{:S(2)}) collective-permute-start(bf16[1680,256]{1,0:T(8,128)(2,1)} %get-tuple-element.14), channel_id=1, source_target_pairs={{0,64},{64,128},{128,192},{192,0},{1,65},{65,129},{129,193},{193,1... | collective-permute-start | bytes 2580488 | tf_op jit(solution)/shard_map/ppermute | solution.py:339
  6.5 2.6 %collective-permute-start.5 = (bf16[1680,256]{1,0:T(8,128)(2,1)}, bf16[1680,256]{1,0:T(8,128)(2,1)S(1)}, u32[]{:S(2)}, u32[]{:S(2)}) collective-permute-start(bf16[1680,256]{1,0:T(8,128)(2,1)} %get-tuple-element.15), channel_id=1, source_target_pairs={{0,128},{64,192},{128,0},{192,64},{1,129},{65,193},{129,1},{193,65... | collective-permute-start | bytes 2580488 | tf_op jit(solution)/shard_map/ppermute | solution.py:339
  9.1 1.1 %collective-permute-start.7 = (bf16[1680,256]{1,0:T(8,128)(2,1)}, bf16[1680,256]{1,0:T(8,128)(2,1)S(1)}, u32[]{:S(2)}, u32[]{:S(2)}) collective-permute-start(bf16[1680,256]{1,0:T(8,128)(2,1)} %get-tuple-element.16), channel_id=1, source_target_pairs={{0,192},{64,0},{128,64},{192,128},{1,193},{65,1},{129,65},{193,129... | collective-permute-start | bytes 2580488 | tf_op jit(solution)/shard_map/ppermute | solution.py:339
  10.2 1.6 %collective-permute-start = (bf16[2,128,256]{2,1,0:T(8,128)(2,1)}, bf16[2,128,256]{2,1,0:T(8,128)(2,1)S(1)}, u32[]{:S(2)}, u32[]{:S(2)}) collective-permute-start(bf16[2,128,256]{2,1,0:T(8,128)(2,1)} %get-tuple-element.11), channel_id=1, source_target_pairs={{0,1},{1,0},{2,3},{3,2},{4,5},{5,4},{6,7},{7,6},{8,9},{9,8},{10,11... | collective-permute-start | bytes 393224 | tf_op jit(solution)/shard_map/ppermute | solution.py:356
  11.8 1.6 %constant_dynamic-update-slice_fusion.1 = bf16[4,128,256]{2,1,0:T(8,128)(2,1)} fusion(bf16[2,128,256]{2,1,0:T(8,128)(2,1)} %get-tuple-element.11), kind=kLoop, calls=%fused_computation.3 | loop fusion | bytes 262144
  13.3 0.0 collective-permute-done.refs_13_
  13.4 0.7 constant_dynamic-update-slice_fusion
  14.0 0.7 copy-done.4
  14.7 7.8 %collective-permute-start.1 = (bf16[4,128,256]{2,1,0:T(8,128)(2,1)}, bf16[4,128,256]{2,1,0:T(8,128)(2,1)S(1)}, u32[]{:S(2)}, u32[]{:S(2)}) collective-permute-start(bf16[4,128,256]{2,1,0:T(8,128)(2,1)} %constant_dynamic-update-slice_fusion), channel_id=1, source_target_pairs={{0,2},{1,63},{2,4},{3,1},{4,6},{5,3},{6,8},{7,5},{8,10},{9,7},{10,... | collective-permute-start | bytes 786440 | tf_op jit(solution)/shard_map/ppermute | solution.py:358
  22.4 1.2 %collective-permute-start.2 = (bf16[4,128,256]{2,1,0:T(8,128)(2,1)}, bf16[4,128,256]{2,1,0:T(8,128)(2,1)}, u32[]{:S(2)}, u32[]{:S(2)}) collective-permute-start(bf16[4,128,256]{2,1,0:T(8,128)(2,1)} %constant_dynamic-update-slice_fusion), channel_id=1, source_target_pairs={{0,4},{1,61},{2,6},{3,63},{4,8},{5,1},{6,10},{7,3},{8,12},{9,5},{1... | collective-permute-start | bytes 786440 | tf_op jit(solution)/shard_map/ppermute | solution.py:359
  23.6 0.1 copy.13.times.refs_0_
  23.7 0.1 copy.11.text
  23.8 2.8 %collective-permute-done.1.near.refs_14_ = bf16[4,128,256]{2,1,0:T(8,128)(2,1)S(1)} collective-permute-done((bf16[4,128,256]{2,1,0:T(8,128)(2,1)}, bf16[4,128,256]{2,1,0:T(8,128)(2,1)S(1)}, u32[]{:S(2)}, u32[]{:S(2)}) %collective-permute-start.1) | collective-permute-done | bytes 262176 | tf_op jit(solution)/shard_map/ppermute | solution.py:358
  26.7 5.1 %collective-permute-done.2.far.refs_15_ = bf16[4,128,256]{2,1,0:T(8,128)(2,1)} collective-permute-done((bf16[4,128,256]{2,1,0:T(8,128)(2,1)}, bf16[4,128,256]{2,1,0:T(8,128)(2,1)}, u32[]{:S(2)}, u32[]{:S(2)}) %collective-permute-start.2) | collective-permute-done | bytes 262176 | tf_op jit(solution)/shard_map/ppermute | solution.py:359
  31.7 0.8 copy-done.8
  32.5 0.8 shard_map.92
  33.3 0.6 copy-done.7
  34.0 8.3 %all-to-all-start = ((f32[64,1,256]{2,1,0:T(1,128)}), f32[64,1,256]{2,1,0:T(1,128)S(1)}, u32[]{:S(2)}, u32[]{:S(2)}) async-start(f32[64,1,256]{2,1,0:T(1,128)} %copy-done.7), calls=%async_computation | async-start | bytes 131072 | tf_op jit(solution)/shard_map/all_to_all | solution.py:372
  42.3 0.0 collective-permute-done.3.got1.refs_6_
  42.3 0.5 collective-permute-start.4
  42.8 3.3 %collective-permute-done.5.got2.refs_8_ = bf16[1680,256]{1,0:T(8,128)(2,1)S(1)} collective-permute-done((bf16[1680,256]{1,0:T(8,128)(2,1)}, bf16[1680,256]{1,0:T(8,128)(2,1)S(1)}, u32[]{:S(2)}, u32[]{:S(2)}) %collective-permute-start.5) | collective-permute-done | bytes 860192 | tf_op jit(solution)/shard_map/ppermute | solution.py:339
  46.1 1.7 %collective-permute-start.6 = (bf16[1680,256]{1,0:T(8,128)(2,1)S(1)}, bf16[1680,256]{1,0:T(8,128)(2,1)}, u32[]{:S(2)}, u32[]{:S(2)}) collective-permute-start(bf16[1680,256]{1,0:T(8,128)(2,1)S(1)} %collective-permute-done.5.got2.refs_8_), channel_id=1, source_target_pairs={{0,1},{1,0},{2,3},{3,2},{4,5},{5,4},{6,7},{7,6},{8,9},{9,8},{10,11... | collective-permute-start | bytes 2580488 | tf_op jit(solution)/shard_map/ppermute | solution.py:385
  47.8 0.0 collective-permute-done.7.got3.refs_10_
  47.8 0.0 collective-permute-start.8
  47.8 4.2 %all-to-all-done.parts.refs_1_ = f32[64,1,256]{2,1,0:T(1,128)S(1)} async-done(((f32[64,1,256]{2,1,0:T(1,128)}), f32[64,1,256]{2,1,0:T(1,128)S(1)}, u32[]{:S(2)}, u32[]{:S(2)}) %all-to-all-start) | async-done | bytes 65568 | tf_op jit(solution)/shard_map/all_to_all | solution.py:372
  52.1 0.6 shard_map.93.refs_12_
  52.7 0.0 copy-start.1
  52.7 0.0 copy-start.2
  52.7 0.0 copy-start.3
  52.7 0.0 copy-start.5
  52.7 0.0 copy-start.9
  52.8 0.5 collective-permute-start.9
  53.2 1.0 %slice.14 = bf16[2,128,256]{2,1,0:T(8,128)(2,1)S(1)} slice(bf16[4,128,256]{2,1,0:T(8,128)(2,1)} %collective-permute-done.2.far.refs_15_), slice={[2:4], [0:128], [0:256]} | slice | bytes 262144 | tf_op jit(solution)/shard_map/slice | solution.py:360
  54.3 0.2 collective-permute-start.12
  54.5 0.0 collective-permute-done.9.refs_13_
  54.6 0.1 pad_maximum_fusion
  54.6 4.9 %collective-permute-start.10 = (bf16[10,128,256]{2,1,0:T(8,128)(2,1)S(1)}, bf16[10,128,256]{2,1,0:T(8,128)(2,1)S(1)}, u32[]{:S(2)}, u32[]{:S(2)}) collective-permute-start(bf16[10,128,256]{2,1,0:T(8,128)(2,1)S(1)} %pad_maximum_fusion), channel_id=1, source_target_pairs={{0,2},{1,63},{2,4},{3,1},{4,6},{5,3},{6,8},{7,5},{8,10},{9,7},{10,... | collective-permute-start | bytes 1966088 | tf_op jit(solution)/shard_map/ppermute | solution.py:383
  59.5 0.0 collective-permute-done.12.refs_16_
  59.6 1.2 %collective-permute-start.11 = (bf16[2,128,256]{2,1,0:T(8,128)(2,1)S(1)}, bf16[2,128,256]{2,1,0:T(8,128)(2,1)S(1)}, u32[]{:S(2)}, u32[]{:S(2)}) collective-permute-start(bf16[2,128,256]{2,1,0:T(8,128)(2,1)S(1)} %slice.13), channel_id=1, source_target_pairs={{0,4},{1,61},{2,6},{3,63},{4,8},{5,1},{6,10},{7,3},{8,12},{9,5},{1... | collective-permute-start | bytes 393224 | tf_op jit(solution)/shard_map/ppermute | solution.py:384
  60.8 0.0 collective-permute-done.4.refs_7_
  60.8 0.0 collective-permute-done.6.refs_9_
  60.8 0.0 collective-permute-done.8.refs_11_
  60.9 8.0 %shard_map.94.before.refs_18_ = f32[14,128,256]{2,1,0:T(8,128)S(1)} custom-call(s32[4,4,2]{2,1,0:T(4,128)S(1)} %copy.13.times.refs_0_, f32[64,1,256]{2,1,0:T(1,128)S(1)} %all-to-all-done.parts.refs_1_, f32[8,256]{1,0:T(8,128)S(1)} %get-tuple-element.13.refs_2_, f32[1,256]{1,0:T(1,128)S(1)} %copy-done.9, bf16[2304,256]{1,0:T(8,128)(2,1)S(1)} %bitcast.8, ...), custom_call_target="tpu_custom_call" | custom-call | flops 4529848320 | bytes 1179648 | tf_op jit(solution)/shard_map/pallas_call | solution.py:308
  68.9 1.0 %collective-permute-done.11.far.refs_15_ = bf16[2,128,256]{2,1,0:T(8,128)(2,1)S(1)} collective-permute-done((bf16[2,128,256]{2,1,0:T(8,128)(2,1)S(1)}, bf16[2,128,256]{2,1,0:T(8,128)(2,1)S(1)}, u32[]{:S(2)}, u32[]{:S(2)}) %collective-permute-start.11) | collective-permute-done | bytes 131104 | tf_op jit(solution)/shard_map/ppermute | solution.py:384
  69.9 2.4 %collective-permute-start.13 = (bf16[6,128,256]{2,1,0:T(8,128)(2,1)S(1)}, bf16[6,128,256]{2,1,0:T(8,128)(2,1)S(1)}, u32[]{:S(2)}, u32[]{:S(2)}) collective-permute-start(bf16[6,128,256]{2,1,0:T(8,128)(2,1)S(1)} %shard_map.95), channel_id=1, source_target_pairs={{0,1},{1,0},{2,3},{3,2},{4,5},{5,4},{6,7},{7,6},{8,9},{9,8},{10,11... | collective-permute-start | bytes 1179656 | tf_op jit(solution)/shard_map/ppermute | solution.py:408
  72.3 1.3 %collective-permute-done.13.refs_16_ = bf16[6,128,256]{2,1,0:T(8,128)(2,1)S(1)} collective-permute-done((bf16[6,128,256]{2,1,0:T(8,128)(2,1)S(1)}, bf16[6,128,256]{2,1,0:T(8,128)(2,1)S(1)}, u32[]{:S(2)}, u32[]{:S(2)}) %collective-permute-start.13) | collective-permute-done | bytes 393248 | tf_op jit(solution)/shard_map/ppermute | solution.py:408
  73.6 15.6 %shard_map.96 = bf16[2,128,256]{2,1,0:T(8,128)(2,1)} custom-call(s32[4,4,2]{2,1,0:T(4,128)S(1)} %copy.13.times.refs_0_, f32[64,1,256]{2,1,0:T(1,128)S(1)} %all-to-all-done.parts.refs_1_, f32[8,256]{1,0:T(8,128)S(1)} %get-tuple-element.13.refs_2_, f32[1,256]{1,0:T(1,128)S(1)} %copy-done.9, bf16[2304,256]{1,0:T(8,128)(2,1)S(1)} %bitcast.9, ...), custom_call_target="tpu_custom_call" | custom-call | flops 6341787648 | bytes 3538944 | tf_op jit(solution)/shard_map/pallas_call | solution.py:308
  (21 shorter events, 0.1 us)
Async XLA Ops:
  0.0 23.6 %copy-start.11 = (s32[4,4,2]{1,2,0:T(2,128)S(1)}, s32[4,4,2]{1,2,0:T(2,128)}, u32[]{:S(2)}) copy-start(s32[4,4,2]{1,2,0:T(2,128)} %param.11) | copy-start | bytes 388
  0.0 23.7 %copy-start.10 = (bf16[1,77,64]{1,2,0:T(8,128)(2,1)S(1)}, bf16[1,77,64]{1,2,0:T(8,128)(2,1)}, u32[]{:S(2)}) copy-start(bf16[1,77,64]{1,2,0:T(8,128)(2,1)} %param.12) | copy-start | bytes 29572
  0.0 31.7 %copy-start.6 = (bf16[256,256]{1,0:T(8,128)(2,1)S(1)}, bf16[256,256]{1,0:T(8,128)(2,1)}, u32[]{:S(2)}) copy-start(bf16[256,256]{1,0:T(8,128)(2,1)} %time_weight.1) | copy-start | bytes 393220
  0.0 52.1 %copy-start = (bf16[1,4,2,128,256]{4,3,2,1,0:T(8,128)(2,1)S(1)}, bf16[1,4,2,128,256]{4,3,2,1,0:T(8,128)(2,1)}, u32[]{:S(2)}) copy-start(bf16[1,4,2,128,256]{4,3,2,1,0:T(8,128)(2,1)} %param.10) | copy-start | bytes 1572868
  4.3 38.0 %collective-permute-start.3 = (bf16[1680,256]{1,0:T(8,128)(2,1)}, bf16[1680,256]{1,0:T(8,128)(2,1)S(1)}, u32[]{:S(2)}, u32[]{:S(2)}) collective-permute-start(bf16[1680,256]{1,0:T(8,128)(2,1)} %get-tuple-element.14), channel_id=1, source_target_pairs={{0,64},{64,128},{128,192},{192,0},{1,65},{65,129},{129,193},{193,1... | collective-permute-start | bytes 2580488 | tf_op jit(solution)/shard_map/ppermute | solution.py:339
  6.5 39.7 %collective-permute-start.5 = (bf16[1680,256]{1,0:T(8,128)(2,1)}, bf16[1680,256]{1,0:T(8,128)(2,1)S(1)}, u32[]{:S(2)}, u32[]{:S(2)}) collective-permute-start(bf16[1680,256]{1,0:T(8,128)(2,1)} %get-tuple-element.15), channel_id=1, source_target_pairs={{0,128},{64,192},{128,0},{192,64},{1,129},{65,193},{129,1},{193,65... | collective-permute-start | bytes 2580488 | tf_op jit(solution)/shard_map/ppermute | solution.py:339
  9.1 38.7 %collective-permute-start.7 = (bf16[1680,256]{1,0:T(8,128)(2,1)}, bf16[1680,256]{1,0:T(8,128)(2,1)S(1)}, u32[]{:S(2)}, u32[]{:S(2)}) collective-permute-start(bf16[1680,256]{1,0:T(8,128)(2,1)} %get-tuple-element.16), channel_id=1, source_target_pairs={{0,192},{64,0},{128,64},{192,128},{1,193},{65,1},{129,65},{193,129... | collective-permute-start | bytes 2580488 | tf_op jit(solution)/shard_map/ppermute | solution.py:339
  10.2 3.2 %collective-permute-start = (bf16[2,128,256]{2,1,0:T(8,128)(2,1)}, bf16[2,128,256]{2,1,0:T(8,128)(2,1)S(1)}, u32[]{:S(2)}, u32[]{:S(2)}) collective-permute-start(bf16[2,128,256]{2,1,0:T(8,128)(2,1)} %get-tuple-element.11), channel_id=1, source_target_pairs={{0,1},{1,0},{2,3},{3,2},{4,5},{5,4},{6,7},{7,6},{8,9},{9,8},{10,11... | collective-permute-start | bytes 393224 | tf_op jit(solution)/shard_map/ppermute | solution.py:356
  14.0 0.7 copy-start.4
  14.7 12.0 %collective-permute-start.1 = (bf16[4,128,256]{2,1,0:T(8,128)(2,1)}, bf16[4,128,256]{2,1,0:T(8,128)(2,1)S(1)}, u32[]{:S(2)}, u32[]{:S(2)}) collective-permute-start(bf16[4,128,256]{2,1,0:T(8,128)(2,1)} %constant_dynamic-update-slice_fusion), channel_id=1, source_target_pairs={{0,2},{1,63},{2,4},{3,1},{4,6},{5,3},{6,8},{7,5},{8,10},{9,7},{10,... | collective-permute-start | bytes 786440 | tf_op jit(solution)/shard_map/ppermute | solution.py:358
  22.4 9.3 %collective-permute-start.2 = (bf16[4,128,256]{2,1,0:T(8,128)(2,1)}, bf16[4,128,256]{2,1,0:T(8,128)(2,1)}, u32[]{:S(2)}, u32[]{:S(2)}) collective-permute-start(bf16[4,128,256]{2,1,0:T(8,128)(2,1)} %constant_dynamic-update-slice_fusion), channel_id=1, source_target_pairs={{0,4},{1,61},{2,6},{3,63},{4,8},{5,1},{6,10},{7,3},{8,12},{9,5},{1... | collective-permute-start | bytes 786440 | tf_op jit(solution)/shard_map/ppermute | solution.py:359
  31.7 0.8 copy-start.8
  33.3 0.6 copy-start.7
  34.0 18.1 %all-to-all-start = ((f32[64,1,256]{2,1,0:T(1,128)}), f32[64,1,256]{2,1,0:T(1,128)S(1)}, u32[]{:S(2)}, u32[]{:S(2)}) async-start(f32[64,1,256]{2,1,0:T(1,128)} %copy-done.7), calls=%async_computation | async-start | bytes 131072 | tf_op jit(solution)/shard_map/all_to_all | solution.py:372
  42.3 18.5 %collective-permute-start.4 = (bf16[1680,256]{1,0:T(8,128)(2,1)S(1)}, bf16[1680,256]{1,0:T(8,128)(2,1)}, u32[]{:S(2)}, u32[]{:S(2)}) collective-permute-start(bf16[1680,256]{1,0:T(8,128)(2,1)S(1)} %collective-permute-done.3.got1.refs_6_), channel_id=1, source_target_pairs={{0,1},{1,0},{2,3},{3,2},{4,5},{5,4},{6,7},{7,6},{8,9},{9,8},{10,11... | collective-permute-start | bytes 2580488 | tf_op jit(solution)/shard_map/ppermute | solution.py:385
  46.1 14.7 %collective-permute-start.6 = (bf16[1680,256]{1,0:T(8,128)(2,1)S(1)}, bf16[1680,256]{1,0:T(8,128)(2,1)}, u32[]{:S(2)}, u32[]{:S(2)}) collective-permute-start(bf16[1680,256]{1,0:T(8,128)(2,1)S(1)} %collective-permute-done.5.got2.refs_8_), channel_id=1, source_target_pairs={{0,1},{1,0},{2,3},{3,2},{4,5},{5,4},{6,7},{7,6},{8,9},{9,8},{10,11... | collective-permute-start | bytes 2580488 | tf_op jit(solution)/shard_map/ppermute | solution.py:385
  47.8 13.0 %collective-permute-start.8 = (bf16[1680,256]{1,0:T(8,128)(2,1)S(1)}, bf16[1680,256]{1,0:T(8,128)(2,1)}, u32[]{:S(2)}, u32[]{:S(2)}) collective-permute-start(bf16[1680,256]{1,0:T(8,128)(2,1)S(1)} %collective-permute-done.7.got3.refs_10_), channel_id=1, source_target_pairs={{0,1},{1,0},{2,3},{3,2},{4,5},{5,4},{6,7},{7,6},{8,9},{9,8},{10,11... | collective-permute-start | bytes 2580488 | tf_op jit(solution)/shard_map/ppermute | solution.py:385
  52.7 8.1 %copy-start.1 = (bf16[1,3,3,256,256]{4,3,2,1,0:T(8,128)(2,1)S(1)}, bf16[1,3,3,256,256]{4,3,2,1,0:T(8,128)(2,1)}, u32[]{:S(2)}) copy-start(bf16[1,3,3,256,256]{4,3,2,1,0:T(8,128)(2,1)} %param.16) | copy-start | bytes 3538948
  52.7 8.1 %copy-start.2 = (bf16[4,2,128,256]{3,2,1,0:T(8,128)(2,1)S(1)}, bf16[4,2,128,256]{3,2,1,0:T(8,128)(2,1)}, u32[]{:S(2)}) copy-start(bf16[4,2,128,256]{3,2,1,0:T(8,128)(2,1)} %refs_12_.1) | copy-start | bytes 1572868
  52.7 8.1 %copy-start.3 = (bf16[1,256,512]{2,1,0:T(8,128)(2,1)S(1)}, bf16[1,256,512]{2,1,0:T(8,128)(2,1)}, u32[]{:S(2)}) copy-start(bf16[1,256,512]{2,1,0:T(8,128)(2,1)} %param.15) | copy-start | bytes 786436
  52.7 8.1 %copy-start.5 = (bf16[2,128,256]{2,1,0:T(8,128)(2,1)S(1)}, bf16[2,128,256]{2,1,0:T(8,128)(2,1)}, u32[]{:S(2)}) copy-start(bf16[2,128,256]{2,1,0:T(8,128)(2,1)} %copy-done.4) | copy-start | bytes 393220
  52.7 8.1 %copy-start.9 = (f32[1,256]{1,0:T(1,128)S(1)}, f32[1,256]{1,0:T(1,128)}, u32[]{:S(2)}) copy-start(f32[1,256]{1,0:T(1,128)} %refs_3_.3) | copy-start | bytes 3076
  52.8 1.8 %collective-permute-start.9 = (bf16[6,128,256]{2,1,0:T(8,128)(2,1)S(1)}, bf16[6,128,256]{2,1,0:T(8,128)(2,1)S(1)}, u32[]{:S(2)}, u32[]{:S(2)}) collective-permute-start(bf16[6,128,256]{2,1,0:T(8,128)(2,1)S(1)} %shard_map.93.refs_12_), channel_id=1, source_target_pairs={{0,1},{1,0},{2,3},{3,2},{4,5},{5,4},{6,7},{7,6},{8,9},{9,8},{10,11... | collective-permute-start | bytes 1179656 | tf_op jit(solution)/shard_map/ppermute | solution.py:382
  54.3 5.2 %collective-permute-start.12 = (bf16[6,128,256]{2,1,0:T(8,128)(2,1)S(1)}, bf16[6,128,256]{2,1,0:T(8,128)(2,1)S(1)}, u32[]{:S(2)}, u32[]{:S(2)}) collective-permute-start(bf16[6,128,256]{2,1,0:T(8,128)(2,1)S(1)} %pad_maximum_fusion.1), channel_id=1, source_target_pairs={{0,1},{1,0},{2,3},{3,2},{4,5},{5,4},{6,7},{7,6},{8,9},{9,8},{10,11... | collective-permute-start | bytes 1179656 | tf_op jit(solution)/shard_map/ppermute | solution.py:360
  54.6 15.2 %collective-permute-start.10 = (bf16[10,128,256]{2,1,0:T(8,128)(2,1)S(1)}, bf16[10,128,256]{2,1,0:T(8,128)(2,1)S(1)}, u32[]{:S(2)}, u32[]{:S(2)}) collective-permute-start(bf16[10,128,256]{2,1,0:T(8,128)(2,1)S(1)} %pad_maximum_fusion), channel_id=1, source_target_pairs={{0,2},{1,63},{2,4},{3,1},{4,6},{5,3},{6,8},{7,5},{8,10},{9,7},{10,... | collective-permute-start | bytes 1966088 | tf_op jit(solution)/shard_map/ppermute | solution.py:383
  59.6 10.3 %collective-permute-start.11 = (bf16[2,128,256]{2,1,0:T(8,128)(2,1)S(1)}, bf16[2,128,256]{2,1,0:T(8,128)(2,1)S(1)}, u32[]{:S(2)}, u32[]{:S(2)}) collective-permute-start(bf16[2,128,256]{2,1,0:T(8,128)(2,1)S(1)} %slice.13), channel_id=1, source_target_pairs={{0,4},{1,61},{2,6},{3,63},{4,8},{5,1},{6,10},{7,3},{8,12},{9,5},{1... | collective-permute-start | bytes 393224 | tf_op jit(solution)/shard_map/ppermute | solution.py:384
  69.9 3.7 %collective-permute-start.13 = (bf16[6,128,256]{2,1,0:T(8,128)(2,1)S(1)}, bf16[6,128,256]{2,1,0:T(8,128)(2,1)S(1)}, u32[]{:S(2)}, u32[]{:S(2)}) collective-permute-start(bf16[6,128,256]{2,1,0:T(8,128)(2,1)S(1)} %shard_map.95), channel_id=1, source_target_pairs={{0,1},{1,0},{2,3},{3,2},{4,5},{5,4},{6,7},{7,6},{8,9},{9,8},{10,11... | collective-permute-start | bytes 1179656 | tf_op jit(solution)/shard_map/ppermute | solution.py:408
